TPU v7x, 32 devices: a whole 2x2x4 slice. The times are simulated.
32 devices in a mesh: dp: 4 (over x, core), head: 8 (over z, y).
Axes of the slice: x: 2, y: 2, z: 4, core: 2. Of those that a mesh axis runs over, the one named last changes fastest.
Arguments:
- block_input: bfloat16 [4, 4096, 1024], P('dp', 'head'), may hold values from -6 to 6
- lengths: int32 [4, 3], P('dp'), may hold values from 680 to 2240, as said below
- scale_ids: int32 [4, 4096], P('dp'), may hold values from 0 to 9, as said below
- class_ids: int32 [4], P('dp'), may hold values from 0 to 1000
- code_ids: int32 [4, 4096], P('dp', 'head'), may hold values from 0 to 4095
- cotangent: bfloat16 [4, 4096, 1024], P('dp', 'head'), may hold values from -6 to 6
- class_table: bfloat16 [1001, 1024], replicated, may hold values from -6 to 6
- ada_weight: bfloat16 [1024, 6144], P(None, 'head'), may hold values from -0.1875 to 0.1875
- ada_bias: bfloat16 [6144], P('head'), may hold values from -3 to 3
- qkv_weight: bfloat16 [1024, 3072], P(None, 'head'), may hold values from -0.1875 to 0.1875
- qv_bias: bfloat16 [2048], P('head'), may hold values from -3 to 3
- qk_scale: float32 [16], P('head'), may hold values from 2 to 3.2
- proj_weight: bfloat16 [1024, 1024], P('head'), may hold values from -1 to 1
- proj_bias: bfloat16 [1024], replicated, may hold values from -4 to 4
- fc1_weight: bfloat16 [1024, 4096], P(None, 'head'), may hold values from -0.1875 to 0.1875
- fc1_bias: bfloat16 [4096], P('head'), may hold values from -3 to 3
- fc2_weight: bfloat16 [4096, 1024], P('head'), may hold values from -0.375 to 0.375
- fc2_bias: bfloat16 [1024], replicated, may hold values from -4 to 4
Outputs:
- block_output: bfloat16 [4, 4096, 1024], P('dp', 'head')
- input_grad: bfloat16 [4, 4096, 1024], P('dp', 'head')
- class_table_grad: float32 [1001, 1024], replicated
- ada_weight_grad: float32 [1024, 6144], P(None, 'head')
- ada_bias_grad: float32 [6144], P('head')
- qkv_weight_grad: float32 [1024, 3072], P(None, 'head')
- qv_bias_grad: float32 [2048], P('head')
- qk_scale_grad: float32 [16], P('head')
- proj_weight_grad: float32 [1024, 1024], P('head')
- proj_bias_grad: float32 [1024], replicated
- fc1_weight_grad: float32 [1024, 4096], P(None, 'head')
- fc1_bias_grad: float32 [4096], P('head')
- fc2_weight_grad: float32 [4096, 1024], P('head')
- fc2_bias_grad: float32 [1024], replicated
- code_hist: int32 [4096], replicated
Inputs may be any that keep to these rules, and one draw needn't show every extreme that they name: `lengths`: each row holds one item of 2240 tokens and two of 680, in an order that varies from row to row; the slots after them are padding. `scale_ids`: within an item, the slot at offset o has scale k where k counts the entries of c that are at most o, with c = 1, 5, 14, 30, 66, 147, 316, 640, 1216, 2240 for an item of 2240 tokens and c = 1, 5, 14, 30, 55, 91, 155, 255, 424, 680 for one of 680; padding slots have scale 0.
All inputs are finite; a program needn't handle non-finite values.
Results may differ from a plain program's by a relative error of at most 0.03.
Values may be sent and summed in bfloat16 or wider, within the bound.
No kernel may reach another device: no remote copies, remote signals or barrier semaphores. Data moves between devices by JAX's collectives and lax.ppermute only.
A program may use at most 256 MiB of HBM per device.

v0:
```python
import jax
import jax.numpy as jnp
from jax import lax
from jax.sharding import PartitionSpec as P

HD = 64
CODES = 4096
QBLOCK = 512


EPS_NORM = 1e-06
HIGH = lax.Precision.HIGHEST


def normalize(values):
    mean_val = jnp.mean(values, -1, keepdims=True)
    centered = values - mean_val
    variance = jnp.mean(centered * centered, -1, keepdims=True)
    recip = lax.rsqrt(variance + EPS_NORM)
    return (centered * recip, recip)


def norm_back(unit, recip, upstream):
    mean_up = jnp.mean(upstream, -1, keepdims=True)
    mean_cross = jnp.mean(upstream * unit, -1, keepdims=True)
    return recip * (upstream - mean_up - unit * mean_cross)


def gelu_tanh(values):
    return jax.nn.gelu(values, approximate=True)


def block_mask(item_ids, scale_ids, item_block, scale_block):
    return (item_block[:, :, None] == item_ids[:, None, :]) & (
        scale_ids[:, None, :] <= scale_block[:, :, None]
    )


def attention_forward(query_low, key_low, value_low, item_ids, scale_ids):
    rows_here, all_slots, heads_here, head_size = query_low.shape
    blocks = all_slots // QBLOCK

    def one_block(block_index):
        begin_at = block_index * QBLOCK
        query_block = lax.dynamic_slice_in_dim(query_low, begin_at, QBLOCK, 1)
        item_block = lax.dynamic_slice_in_dim(item_ids, begin_at, QBLOCK, 1)
        scale_block = lax.dynamic_slice_in_dim(scale_ids, begin_at, QBLOCK, 1)
        allowed = block_mask(item_ids, scale_ids, item_block, scale_block)
        scores = jnp.einsum(
            "rqhd,rkhd->rhqk", query_block, key_low, preferred_element_type=jnp.float32
        )
        scores = jnp.where(allowed[:, None], scores, jnp.float32(-1e30))
        top_score = jnp.max(scores, -1, keepdims=True)
        exp_scores = jnp.exp(scores - top_score)
        denom_sum = jnp.sum(exp_scores, -1, keepdims=True)
        probs = (exp_scores / denom_sum).astype(jnp.bfloat16)
        log_total = top_score[..., 0] + jnp.log(denom_sum[..., 0])
        result = jnp.einsum("rhqk,rkhd->rqhd", probs, value_low, preferred_element_type=jnp.float32)
        return (result.astype(jnp.bfloat16), log_total)

    results, log_totals = lax.map(one_block, jnp.arange(blocks, dtype=jnp.int32))
    attended = jnp.transpose(results, (1, 0, 2, 3, 4)).reshape(
        rows_here, all_slots, heads_here, head_size
    )
    log_sum = jnp.transpose(log_totals, (1, 2, 0, 3)).reshape(rows_here, heads_here, all_slots)
    return (attended, log_sum)


def attention_backward(query_low, key_low, value_low, item_ids, scale_ids, log_sum, grad_attended):
    rows_here, all_slots, heads_here, head_size = query_low.shape
    blocks = all_slots // QBLOCK

    def one_block(carry, block_index):
        grad_keys, grad_values = carry
        begin_at = block_index * QBLOCK
        query_block = lax.dynamic_slice_in_dim(query_low, begin_at, QBLOCK, 1)
        grad_block = lax.dynamic_slice_in_dim(grad_attended, begin_at, QBLOCK, 1)
        item_block = lax.dynamic_slice_in_dim(item_ids, begin_at, QBLOCK, 1)
        scale_block = lax.dynamic_slice_in_dim(scale_ids, begin_at, QBLOCK, 1)
        lse_block = lax.dynamic_slice_in_dim(log_sum, begin_at, QBLOCK, 2)
        allowed = block_mask(item_ids, scale_ids, item_block, scale_block)
        scores = jnp.einsum(
            "rqhd,rkhd->rhqk", query_block, key_low, preferred_element_type=jnp.float32
        )
        scores = jnp.where(allowed[:, None], scores, jnp.float32(-1e30))
        probs = jnp.exp(scores - lse_block[..., None])
        grad_probs = jnp.einsum(
            "rqhd,rkhd->rhqk", grad_block, value_low, preferred_element_type=jnp.float32
        )
        delta = jnp.sum(probs * grad_probs, -1, keepdims=True)
        grad_scores = (probs * (grad_probs - delta)).astype(jnp.bfloat16)
        grad_query = jnp.einsum(
            "rhqk,rkhd->rqhd", grad_scores, key_low, preferred_element_type=jnp.float32
        )
        grad_keys = grad_keys + jnp.einsum(
            "rhqk,rqhd->rkhd", grad_scores, query_block, preferred_element_type=jnp.float32
        )
        grad_values = grad_values + jnp.einsum(
            "rhqk,rqhd->rkhd",
            probs.astype(jnp.bfloat16),
            grad_block,
            preferred_element_type=jnp.float32,
        )
        return ((grad_keys, grad_values), grad_query)

    zero_grad = jnp.zeros((rows_here, all_slots, heads_here, head_size), jnp.float32)
    (grad_keys, grad_values), grad_blocks = lax.scan(
        one_block, (zero_grad, zero_grad), jnp.arange(blocks, dtype=jnp.int32)
    )
    grad_queries = jnp.transpose(grad_blocks, (1, 0, 2, 3, 4)).reshape(
        rows_here, all_slots, heads_here, head_size
    )
    return (grad_queries, grad_keys, grad_values)


def shards(
    block_input,
    lengths,
    scale_ids,
    class_ids,
    code_ids,
    cotangent,
    class_table,
    ada_weight,
    ada_bias,
    qkv_weight,
    qv_bias,
    qk_scale,
    proj_weight,
    proj_bias,
    fc1_weight,
    fc1_bias,
    fc2_weight,
    fc2_bias,
):
    rows_here, local_slots, width = block_input.shape
    head_count = lax.axis_size("head")
    all_slots = local_slots * head_count
    heads_here = qk_scale.shape[0]
    cond = jnp.take(class_table, class_ids, axis=0).astype(jnp.float32)
    act = jax.nn.silu(cond).astype(jnp.bfloat16)
    mod_local = jnp.dot(act, ada_weight, preferred_element_type=jnp.float32) + ada_bias.astype(
        jnp.float32
    )
    modulation = lax.all_gather(mod_local, "head", axis=1, tiled=True)
    pieces = jnp.split(modulation, 6, axis=1)
    shift_one, scale_one, gate_one, shift_two, scale_two, gate_two = [
        piece[:, None, :] for piece in pieces
    ]
    inputs_full = block_input.astype(jnp.float32)
    unit_one, recip_one = normalize(inputs_full)
    normed_one_local = (unit_one * (1.0 + scale_one) + shift_one).astype(jnp.bfloat16)
    normed_one = lax.all_gather(normed_one_local, "head", axis=1, tiled=True)
    bias_pair = qv_bias.astype(jnp.float32).reshape(heads_here, 2, HD)
    bias_full = jnp.stack(
        [bias_pair[:, 0], jnp.zeros_like(bias_pair[:, 0]), bias_pair[:, 1]], 1
    ).reshape(heads_here * 3 * HD)
    projected = (
        jnp.einsum("rsd,de->rse", normed_one, qkv_weight, preferred_element_type=jnp.float32)
        + bias_full
    )
    projected = projected.reshape(rows_here, all_slots, heads_here, 3, HD)
    queries = projected[:, :, :, 0]
    key_raw = projected[:, :, :, 1]
    value_raw = projected[:, :, :, 2]
    query_recip = lax.rsqrt(jnp.sum(queries * queries, -1, keepdims=True) + EPS_NORM)
    key_recip = lax.rsqrt(jnp.sum(key_raw * key_raw, -1, keepdims=True) + EPS_NORM)
    query_unit = queries * query_recip
    key_unit = key_raw * key_recip
    scale_exp = jnp.exp(qk_scale)[None, None, :, None]
    query_low = (query_unit * scale_exp).astype(jnp.bfloat16)
    key_low = key_unit.astype(jnp.bfloat16)
    value_low = value_raw.astype(jnp.bfloat16)
    bounds = jnp.cumsum(lengths, 1)
    places = jnp.arange(all_slots, dtype=jnp.int32)
    item_ids = jnp.sum((places[None, :, None] >= bounds[:, None, :]).astype(jnp.int32), -1)
    attended, log_sum = attention_forward(query_low, key_low, value_low, item_ids, scale_ids)
    attended_flat = attended.reshape(rows_here, all_slots, heads_here * HD)
    attn_terms = jnp.einsum(
        "rsk,kd->rsd", attended_flat, proj_weight, preferred_element_type=jnp.float32
    )
    attn_branch = lax.psum_scatter(
        attn_terms, "head", scatter_dimension=1, tiled=True
    ) + proj_bias.astype(jnp.float32)
    resid = inputs_full + gate_one * attn_branch
    unit_two, recip_two = normalize(resid)
    normed_two_local = (unit_two * (1.0 + scale_two) + shift_two).astype(jnp.bfloat16)
    normed_two = lax.all_gather(normed_two_local, "head", axis=1, tiled=True)
    pre_act = jnp.einsum(
        "rsd,df->rsf", normed_two, fc1_weight, preferred_element_type=jnp.float32
    ) + fc1_bias.astype(jnp.float32)
    hidden = gelu_tanh(pre_act).astype(jnp.bfloat16)
    mlp_terms = jnp.einsum("rsf,fd->rsd", hidden, fc2_weight, preferred_element_type=jnp.float32)
    mlp_branch = lax.psum_scatter(
        mlp_terms.astype(jnp.bfloat16), "head", scatter_dimension=1, tiled=True
    ).astype(jnp.float32) + fc2_bias.astype(jnp.float32)
    block_output = (resid + gate_two * mlp_branch).astype(jnp.bfloat16)
    cot_full = cotangent.astype(jnp.float32)
    grad_mlp_local = (cot_full * gate_two).astype(jnp.bfloat16)
    grad_gate_two = jnp.sum(cot_full * mlp_branch, 1)
    grad_mlp = lax.all_gather(grad_mlp_local, "head", axis=1, tiled=True)
    normed_one_back, normed_two_back = (
        lax.all_gather(normed_one_local, "head", axis=1, tiled=True),
        lax.all_gather(normed_two_local, "head", axis=1, tiled=True),
    )
    fc2_bias_grad = jnp.sum(grad_mlp.astype(jnp.float32), (0, 1))
    fc2_weight_grad = jnp.einsum(
        "rsf,rsd->fd", hidden, grad_mlp, preferred_element_type=jnp.float32
    )
    grad_hidden = jnp.einsum(
        "rsd,fd->rsf", grad_mlp, fc2_weight, preferred_element_type=jnp.float32
    )
    gelu_value, gelu_pull = jax.vjp(gelu_tanh, pre_act)
    grad_pre = gelu_pull(grad_hidden)[0].astype(jnp.bfloat16)
    fc1_weight_grad = jnp.einsum(
        "rsd,rsf->df", normed_two_back, grad_pre, preferred_element_type=jnp.float32
    )
    fc1_bias_grad = jnp.sum(grad_pre.astype(jnp.float32), (0, 1))
    grad_two_terms = jnp.einsum(
        "rsf,df->rsd", grad_pre, fc1_weight, preferred_element_type=jnp.float32
    )
    grad_normed_two = lax.psum_scatter(grad_two_terms, "head", scatter_dimension=1, tiled=True)
    grad_shift_two = jnp.sum(grad_normed_two, 1)
    grad_scale_two = jnp.sum(grad_normed_two * unit_two, 1)
    grad_resid = cot_full + norm_back(unit_two, recip_two, grad_normed_two * (1.0 + scale_two))
    grad_attn_local = (grad_resid * gate_one).astype(jnp.bfloat16)
    grad_gate_one = jnp.sum(grad_resid * attn_branch, 1)
    grad_attn = lax.all_gather(grad_attn_local, "head", axis=1, tiled=True)
    proj_bias_grad = jnp.sum(grad_attn.astype(jnp.float32), (0, 1))
    proj_weight_grad = jnp.einsum(
        "rsk,rsd->kd", attended_flat, grad_attn, preferred_element_type=jnp.float32
    )
    grad_attended = jnp.einsum(
        "rsd,kd->rsk", grad_attn, proj_weight, preferred_element_type=jnp.float32
    ).astype(jnp.bfloat16)
    grad_attended = grad_attended.reshape(rows_here, all_slots, heads_here, HD)
    grad_queries, grad_keys, grad_values = attention_backward(
        query_low, key_low, value_low, item_ids, scale_ids, log_sum, grad_attended
    )
    qk_scale_grad = jnp.exp(qk_scale) * jnp.sum(grad_queries * query_unit, (0, 1, 3))
    scaled_grad = scale_exp * grad_queries
    grad_q = query_recip * (
        scaled_grad - query_unit * jnp.sum(scaled_grad * query_unit, -1, keepdims=True)
    )
    grad_k = key_recip * (grad_keys - key_unit * jnp.sum(grad_keys * key_unit, -1, keepdims=True))
    grad_projected = jnp.stack([grad_q, grad_k, grad_values], 3).astype(jnp.bfloat16)
    grad_projected = grad_projected.reshape(rows_here, all_slots, heads_here * 3 * HD)
    qkv_weight_grad = jnp.einsum(
        "rsd,rse->de", normed_one_back, grad_projected, preferred_element_type=jnp.float32
    )
    bias_sums = jnp.sum(grad_projected.astype(jnp.float32), (0, 1)).reshape(heads_here, 3, HD)
    qv_bias_grad = jnp.stack([bias_sums[:, 0], bias_sums[:, 2]], 1).reshape(heads_here * 2 * HD)
    grad_one_terms = jnp.einsum(
        "rse,de->rsd", grad_projected, qkv_weight, preferred_element_type=jnp.float32
    )
    grad_normed_one = lax.psum_scatter(
        grad_one_terms.astype(jnp.bfloat16), "head", scatter_dimension=1, tiled=True
    ).astype(jnp.float32)
    grad_shift_one = jnp.sum(grad_normed_one, 1)
    grad_scale_one = jnp.sum(grad_normed_one * unit_one, 1)
    input_grad = (
        grad_resid + norm_back(unit_one, recip_one, grad_normed_one * (1.0 + scale_one))
    ).astype(jnp.bfloat16)
    grad_mod_partial = jnp.concatenate(
        [
            grad_shift_one,
            grad_scale_one,
            grad_gate_one,
            grad_shift_two,
            grad_scale_two,
            grad_gate_two,
        ],
        1,
    )
    grad_mod = lax.psum_scatter(grad_mod_partial, "head", scatter_dimension=1, tiled=True)
    ada_weight_grad = jnp.dot(act.astype(jnp.float32).T, grad_mod, precision=HIGH)
    ada_bias_grad = jnp.sum(grad_mod, 0)
    cond_terms = jnp.dot(grad_mod, ada_weight.astype(jnp.float32).T, precision=HIGH)
    all_terms, all_classes = (
        lax.all_gather(cond_terms, ("dp", "head"), axis=0, tiled=True),
        lax.all_gather(class_ids.astype(jnp.float32), ("dp", "head"), axis=0, tiled=True),
    )
    class_range = jnp.arange(class_table.shape[0], dtype=jnp.float32)
    one_hot = (class_range[:, None] == all_classes[None, :]).astype(jnp.float32)
    class_sums = jnp.dot(one_hot, all_terms, precision=HIGH)
    silu_value, silu_pull = jax.vjp(jax.nn.silu, class_table.astype(jnp.float32))
    class_table_grad = silu_pull(class_sums)[0]
    (
        ada_weight_grad,
        ada_bias_grad,
        qkv_weight_grad,
        qv_bias_grad,
        qk_scale_grad,
        proj_weight_grad,
        proj_bias_grad,
        fc1_weight_grad,
        fc1_bias_grad,
        fc2_weight_grad,
        fc2_bias_grad,
    ) = (
        lax.psum(ada_weight_grad.astype(jnp.bfloat16), "dp").astype(jnp.float32),
        lax.psum(ada_bias_grad.astype(jnp.bfloat16), "dp").astype(jnp.float32),
        lax.psum(qkv_weight_grad.astype(jnp.bfloat16), "dp").astype(jnp.float32),
        lax.psum(qv_bias_grad.astype(jnp.bfloat16), "dp").astype(jnp.float32),
        lax.psum(qk_scale_grad.astype(jnp.bfloat16), "dp").astype(jnp.float32),
        lax.psum(proj_weight_grad.astype(jnp.bfloat16), "dp").astype(jnp.float32),
        lax.psum(proj_bias_grad.astype(jnp.bfloat16), "dp").astype(jnp.float32),
        lax.psum(fc1_weight_grad.astype(jnp.bfloat16), "dp").astype(jnp.float32),
        lax.psum(fc1_bias_grad.astype(jnp.bfloat16), "dp").astype(jnp.float32),
        lax.psum(fc2_weight_grad.astype(jnp.bfloat16), "dp").astype(jnp.float32),
        lax.psum(fc2_bias_grad.astype(jnp.bfloat16), "dp").astype(jnp.float32),
    )
    slot_places = lax.axis_index("head") * local_slots + jnp.arange(local_slots, dtype=jnp.int32)
    valid = slot_places[None, :] < bounds[:, 2:3]
    code_range = jnp.arange(CODES, dtype=jnp.int32)
    code_hits = (code_ids[:, :, None] == code_range[None, None, :]) & valid[:, :, None]
    local_counts = jnp.sum(code_hits.astype(jnp.int32), (0, 1))
    code_hist = lax.psum(local_counts, ("dp", "head"))
    return (
        block_output,
        input_grad,
        class_table_grad,
        ada_weight_grad,
        ada_bias_grad,
        qkv_weight_grad,
        qv_bias_grad,
        qk_scale_grad,
        proj_weight_grad,
        proj_bias_grad,
        fc1_weight_grad,
        fc1_bias_grad,
        fc2_weight_grad,
        fc2_bias_grad,
        code_hist,
    )


def solution(mesh):
    placed = (
        P("dp", "head", None),
        P("dp", None),
        P("dp", None),
        P("dp"),
        P("dp", "head"),
        P("dp", "head", None),
        P(),
        P(None, "head"),
        P("head"),
        P(None, "head"),
        P("head"),
        P("head"),
        P("head", None),
        P(),
        P(None, "head"),
        P("head"),
        P("head", None),
        P(),
    )
    return jax.shard_map(
        shards,
        mesh=mesh,
        in_specs=placed,
        out_specs=(
            P("dp", "head", None),
            P("dp", "head", None),
            P(),
            P(None, "head"),
            P("head"),
            P(None, "head"),
            P("head"),
            P("head"),
            P("head", None),
            P(),
            P(None, "head"),
            P("head"),
            P("head", None),
            P(),
            P(),
        ),
        check_vma=False,
    )
```

profile of v0, /device:TPU:1, one launch (start us, length us, event | category | flops | bytes accessed | tf_op | source)
XLA Modules:
  0.0 2312.9 jit_solution(11986604508133760518)
XLA Ops:
  13.0 25.1 %all-gather.2 = f32[8,1,768]{2,1,0:T(1,128)S(1)} all-gather(f32[1,1,768]{2,1,0:T(1,128)S(1)} %reshape.1022), channel_id=2, replica_groups=mesh['dp'=4,'head'=8] {'head'}, dimensions={0}, use_global_device_ids=true | all-gather | bytes 27648 | tf_op jit(solution)/shard_map/all_gather | solution.py:145
  41.5 131.1 %all-gather.8.cloned.1.call-done = bf16[1,4096,1024]{2,1,0:T(8,128)(2,1)} async-done(((bf16[1,512,1024]{2,1,0:T(8,128)(2,1)}), bf16[1,4096,1024]{2,1,0:T(8,128)(2,1)}) %all-gather.8.cloned.1.call-update) | async-done | bytes 8388624 | tf_op jit(solution)/shard_map/all_gather | solution.py:153
  183.6 148.3 %while.28 = (s32[]{:T(128)}, bf16[8,1,512,2,64]{2,4,3,1,0:T(8,128)(2,1)}, f32[8,1,2,512]{3,2,1,0:T(2,128)S(1)}, s32[8]{0:T(128)S(1)}, s32[1,4096]{1,0:T(1,128)S(...) while((s32[]{:T(128)}, ...), condition=%wide.region_9.10_spmd, body=%wide.region_6.9_spmd.sunk | while | flops 1117846528 | bytes 61157584 | solution.py:61
  344.0 280.7 %reduce-scatter.8.cloned.1.call-done = f32[1,512,1024]{2,1,0:T(8,128)} async-done(((f32[1,4096,1024]{2,1,0:T(8,128)}), f32[1,512,1024]{2,1,0:T(8,128)}) %reduce-scatter.8.cloned.1.call-update) | async-done | bytes 2097168 | tf_op jit(solution)/shard_map/reduce_scatter | solution.py:182
  632.3 121.1 %all-gather.10.cloned.1.call-done = bf16[1,4096,1024]{2,1,0:T(8,128)(2,1)} async-done(((bf16[1,512,1024]{2,1,0:T(8,128)(2,1)}), bf16[1,4096,1024]{2,1,0:T(8,128)(2,1)}) %all-gather.10.cloned.1.call-update) | async-done | bytes 8388624 | tf_op jit(solution)/shard_map/all_gather | solution.py:188
  765.3 114.0 %all-gather.12.cloned.1.call-done = bf16[1,4096,1024]{2,1,0:T(8,128)(2,1)} async-done(((bf16[1,512,1024]{2,1,0:T(8,128)(2,1)}), bf16[1,4096,1024]{2,1,0:T(8,128)(2,1)}) %all-gather.12.cloned.1.call-update) | async-done | bytes 8388624 | tf_op jit(solution)/shard_map/all_gather | solution.py:201
  879.4 15.0 fusion.117
  918.0 268.1 %reduce-scatter.12.cloned.1.call-done = f32[1,512,1024]{2,1,0:T(8,128)} async-done(((f32[1,4096,1024]{2,1,0:T(8,128)}), f32[1,512,1024]{2,1,0:T(8,128)}) %reduce-scatter.12.cloned.1.call-update) | async-done | bytes 2097168 | tf_op jit(solution)/shard_map/reduce_scatter | solution.py:222
  1189.7 147.9 %reduce-scatter.10.cloned.1.call-done = bf16[1,512,1024]{2,1,0:T(8,128)(2,1)} async-done(((bf16[1,4096,1024]{2,1,0:T(8,128)(2,1)}), bf16[1,512,1024]{2,1,0:T(8,128)(2,1)}) %reduce-scatter.10.cloned.1.call-update) | async-done | bytes 1048592 | tf_op jit(solution)/shard_map/reduce_scatter | solution.py:194
  1351.0 118.4 %all-gather.14.cloned.1.call-done = bf16[1,4096,1024]{2,1,0:T(8,128)(2,1)} async-done(((bf16[1,512,1024]{2,1,0:T(8,128)(2,1)}), bf16[1,4096,1024]{2,1,0:T(8,128)(2,1)}) %all-gather.14.cloned.1.call-update) | async-done | bytes 8388624 | tf_op jit(solution)/shard_map/all_gather | solution.py:228
  1476.6 475.1 %while.29 = (s32[]{:T(128)}, f32[1,4096,2,64]{1,3,2,0:T(8,128)}, f32[1,4096,2,64]{1,3,2,0:T(8,128)}, f32[8,1,512,2,64]{2,0,4,3,1:T(8,128)}, s32[8]{0:T(128)S(1)}...) while((s32[]{:T(128)}, f32[1,4096,2,64]{1,3,2,0:T(8,128)}, ...), condition=%wide.region_19.20_spmd.clone, body=%wide.region_17.19_spmd.clone.sunk | while | flops 2743073792 | bytes 185409936 | solution.py:107
  1497.6 12.9 multiply_reduce_fusion.11
  1557.0 12.9 multiply_reduce_fusion.11
  1616.3 12.9 multiply_reduce_fusion.11
  1675.6 12.9 multiply_reduce_fusion.11
  1734.9 12.9 multiply_reduce_fusion.11
  1794.2 12.9 multiply_reduce_fusion.11
  1853.5 12.9 multiply_reduce_fusion.11
  1912.9 12.9 multiply_reduce_fusion.11
  1971.1 42.6 %all-reduce = f32[32]{0:T(128)S(1)} all-reduce(f32[32]{0:T(128)S(1)} %convert_dynamic-update-slice_fusion), channel_id=1, replica_groups=mesh['dp'=4,'head'=8] {'dp','head'}, use_global_device_ids=true, to_apply=%add | all-reduce | flops 32 | bytes 256
  2017.2 42.6 %psum.95 = s32[4096]{0:T(1024)} all-reduce(s32[4096]{0:T(1024)S(1)} %convert_reduce_fusion), channel_id=1, replica_groups=mesh['dp'=4,'head'=8] {'dp','head'}, use_global_device_ids=true, to_apply=%region_49.50 | all-reduce | flops 4096 | bytes 32768 | tf_op jit(solution)/shard_map/psum | solution.py:318
  2092.1 28.3 %reduce-scatter.14.cloned.1.call-done = bf16[1,512,1024]{2,1,0:T(8,128)(2,1)} async-done(((bf16[1,4096,1024]{2,1,0:T(8,128)(2,1)}), bf16[1,512,1024]{2,1,0:T(8,128)(2,1)}) %reduce-scatter.14.cloned.1.call-update) | async-done | bytes 1048592 | tf_op jit(solution)/shard_map/reduce_scatter | solution.py:256
  2130.8 66.9 %reduce-scatter.16.cloned.1.call-done = f32[768,1]{1,0:T(8,128)} async-done(((f32[6144,1]{1,0:T(8,128)}), f32[768,1]{1,0:T(8,128)}) %reduce-scatter.16.cloned.1.call-update) | async-done | bytes 3088 | tf_op jit(solution)/shard_map/reshape.111
  2221.0 60.4 %all-gather.1 = f32[32768]{0:T(1024)S(1)} all-gather(f32[1024]{0:T(1024)S(1)} %bitcast.325), channel_id=3, replica_groups=mesh['dp'=4,'head'=8] {'dp','head'}, dimensions={0}, use_global_device_ids=true | all-gather | bytes 135168 | tf_op jit(solution)/shard_map/all_gather | solution.py:280
  (484 shorter events, 718.7 us)
Async XLA Ops:
  7.2 165.4 %all-gather.8.cloned.1.call-start = ((), (), s32[]{:S(2)}) async-start(), calls=%async_computation.5 | async-start | bytes 9437184 | tf_op jit(solution)/shard_map/all_gather | solution.py:153
  40.7 584.0 %reduce-scatter.8.cloned.1.call-start = ((), (), s32[]{:S(2)}) async-start(), calls=%async_computation.6 | async-start | bytes 18874368 | tf_op jit(solution)/shard_map/reduce_scatter | solution.py:182
  40.8 140.4 %copy-start.47 = (f32[2]{0:T(128)}, f32[2]{0:T(128)S(1)}, u32[]{:S(2)}) copy-start(f32[2]{0:T(128)S(1)} %exp.41) | copy-start | bytes 28
  41.0 137.8 %copy-start.57 = (s32[1,3]{1,0:T(1,128)}, s32[1,3]{1,0:T(1,128)S(1)}, u32[]{:S(2)}) copy-start(s32[1,3]{1,0:T(1,128)S(1)} %reduce_window_sum.11) | copy-start | bytes 40
  343.3 281.4 %copy-start.37 = (f32[1,1024]{1,0:T(1,128)S(1)}, f32[1,1024]{1,0:T(1,128)}, u32[]{:S(2)}) copy-start(f32[1,1024]{1,0:T(1,128)} %get-tuple-element.272) | copy-start | bytes 12292
  343.3 410.1 %all-gather.10.cloned.1.call-start = ((), (), s32[]{:S(2)}) async-start(), calls=%async_computation.7 | async-start | bytes 9437184 | tf_op jit(solution)/shard_map/all_gather | solution.py:188
  629.7 249.6 %all-gather.12.cloned.1.call-start = ((), (), s32[]{:S(2)}) async-start(), calls=%async_computation.9 | async-start | bytes 9437184 | tf_op jit(solution)/shard_map/all_gather | solution.py:201
  632.3 553.8 %reduce-scatter.12.cloned.1.call-start = ((), (), s32[]{:S(2)}) async-start(), calls=%async_computation.10 | async-start | bytes 18874368 | tf_op jit(solution)/shard_map/reduce_scatter | solution.py:222
  632.3 272.4 %copy-start.52 = (f32[512]{0:T(512)}, f32[512]{0:T(512)S(1)}, u32[]{:S(2)}) copy-start(f32[512]{0:T(512)S(1)} %convert_element_type.323) | copy-start | bytes 6148
  904.5 433.1 %reduce-scatter.10.cloned.1.call-start = ((), (), s32[]{:S(2)}) async-start(), calls=%async_computation.8 | async-start | bytes 9437184 | tf_op jit(solution)/shard_map/reduce_scatter | solution.py:194
  917.3 552.1 %all-gather.14.cloned.1.call-start = ((), (), s32[]{:S(2)}) async-start(), calls=%async_computation.11 | async-start | bytes 9437184 | tf_op jit(solution)/shard_map/all_gather | solution.py:228
  1345.8 774.7 %reduce-scatter.14.cloned.1.call-start = ((), (), s32[]{:S(2)}) async-start(), calls=%async_computation.12 | async-start | bytes 9437184 | tf_op jit(solution)/shard_map/reduce_scatter | solution.py:256
  1970.9 42.8 %copy-start.58 = (s32[1,3]{1,0:T(1,128)S(1)}, s32[1,3]{1,0:T(1,128)}, u32[]{:S(2)}) copy-start(s32[1,3]{1,0:T(1,128)} %copy-done.57) | copy-start | bytes 40
  1970.9 44.0 %copy-start.61 = (s32[1,512]{1,0:T(1,128)S(1)}, s32[1,512]{1,0:T(1,128)}, u32[]{:S(2)}) copy-start(s32[1,512]{1,0:T(1,128)} %param.26) | copy-start | bytes 6148
  1970.9 226.8 %reduce-scatter.16.cloned.1.call-start = ((), (), s32[]{:S(2)}) async-start(), calls=%async_computation.13 | async-start | bytes 3538944 | tf_op jit(solution)/shard_map/reshape.111
  2086.4 34.1 %copy-start.11 = (bf16[1,512,1024]{2,1,0:T(8,128)(2,1)S(1)}, bf16[1,512,1024]{2,1,0:T(8,128)(2,1)}, u32[]{:S(2)}) copy-start(bf16[1,512,1024]{2,1,0:T(8,128)(2,1)} %param.22) | copy-start | bytes 3145732
  2086.4 34.1 %copy-start.34 = (f32[1,1024]{1,0:T(1,128)S(1)}, f32[1,1024]{1,0:T(1,128)}, u32[]{:S(2)}) copy-start(f32[1,1024]{1,0:T(1,128)} %copy-done.33) | copy-start | bytes 12292
  2086.4 34.1 %copy-start.36 = (f32[512]{0:T(512)S(1)}, f32[512]{0:T(512)}, u32[]{:S(2)}) copy-start(f32[512]{0:T(512)} %copy-done.35) | copy-start | bytes 6148
  2086.4 36.3 %copy-start.46 = (f32[1024]{0:T(1024)S(1)}, f32[1024]{0:T(1024)}, u32[]{:S(2)}) copy-start(f32[1024]{0:T(1024)} %get-tuple-element.251) | copy-start | bytes 12292
  2086.4 36.3 %copy-start.44 = (f32[1024]{0:T(1024)S(1)}, f32[1024]{0:T(1024)}, u32[]{:S(2)}) copy-start(f32[1024]{0:T(1024)} %get-tuple-element.189) | copy-start | bytes 12292
  2086.4 36.3 %copy-start.43 = (f32[1024]{0:T(1024)S(1)}, f32[1024]{0:T(1024)}, u32[]{:S(2)}) copy-start(f32[1024]{0:T(1024)} %get-tuple-element.184) | copy-start | bytes 12292
  2086.4 36.4 %copy-start.45 = (f32[1024]{0:T(1024)S(1)}, f32[1024]{0:T(1024)}, u32[]{:S(2)}) copy-start(f32[1024]{0:T(1024)} %get-tuple-element.266) | copy-start | bytes 12292
  2125.1 73.8 %copy-start.42 = (f32[1,1024]{1,0:T(1,128)S(1)}, f32[1,1024]{1,0:T(1,128)}, u32[]{:S(2)}) copy-start(f32[1,1024]{1,0:T(1,128)} %get-tuple-element.249) | copy-start | bytes 12292
  2125.1 171.0 %all-reduce.5.cloned.1.call-start = ((), (), s32[]{:S(2)}) async-start(), calls=%async_computation.14 | async-start | bytes 9437184 | tf_op jit(solution)/shard_map/psum | solution.py:301
  (89 other events, 678.2 us)
Sparse Core Ops, SparseCore 0:
  40.8 131.7 all-gather.7
  343.4 281.2 reduce-scatter.7
  629.9 123.5 all-gather.9
  756.2 123.1 all-gather.11
  904.6 281.3 reduce-scatter.11
  1189.5 148.0 reduce-scatter.9
  1345.9 123.4 all-gather.13
  1971.0 149.4 reduce-scatter.13
  2125.2 72.4 reduce-scatter.15
  2201.4 94.6 all-reduce.4
where the time goes:
time: 2320 us; the launch traced here: 2310 us
  waiting for transfers between devices  1280 us (55%)
  matrix products  492 us (21%)
  other arithmetic  227 us (10%)
  blocking collectives  178 us (8%)
  local copies, waits for them, and re-layouts  102 us (4%)
    reduce_scatter x1, waiting for transfers between devices, shards(): lax.psum_scatter(attn_terms, 'head', scatter_dimension=1, tiled=True)  281 us
    reduce_scatter x1, waiting for transfers between devices, shards(): lax.psum_scatter(grad_two_terms, 'head', scatter_dimension=1, tiled=True)  268 us
    reduce_scatter x1, waiting for transfers between devices, shards(): lax.psum_scatter(mlp_terms.astype(jnp.bfloat16), 'head', scatter_dimensio...  148 us
    all_gather x1, waiting for transfers between devices, shards(): normed_one = lax.all_gather(normed_one_local, 'head', axis=1, tiled=True)  131 us
    all_gather x1, waiting for transfers between devices, shards(): normed_two = lax.all_gather(normed_two_local, 'head', axis=1, tiled=True)  121 us
    all_gather x1, waiting for transfers between devices, shards(): grad_attn = lax.all_gather(grad_attn_local, 'head', axis=1, tiled=True)  118 us
    all_gather x1, waiting for transfers between devices, shards(): grad_mlp = lax.all_gather(grad_mlp_local, 'head', axis=1, tiled=True)  114 us
    dot_general x16, matrix products, one_block(): jnp.einsum('rqhd,rkhd->rhqk', query_block, key_low, preferred_element_typ...  105 us
  transfers between devices with their start and end apart: 10, of which 10 were waited for; matrix products, arithmetic and copies ran while one was open for 4% of the time, Pallas kernels for 0%

commit v1 on v0

v1 whole, which is shorter than its diff:
```python
import functools

import jax
import jax.numpy as jnp
import numpy as np
from jax import lax
from jax.experimental import pallas as pl
from jax.experimental.pallas import tpu as pltpu
from jax.sharding import PartitionSpec as P

HD = 64
CODES = 4096
BLK = 256
EPS_NORM = 1e-06
HIGH = lax.Precision.HIGHEST
F32 = jnp.float32
BF16 = jnp.bfloat16
BIG_LEN = 2240
BIG_CUMS = (1, 5, 14, 30, 66, 147, 316, 640, 1216, 2240)
SMALL_CUMS = (1, 5, 14, 30, 55, 91, 155, 255, 424, 680)
ORDER = (0, 2, 1, 3)


def normalize(values):
    mean_val = jnp.mean(values, -1, keepdims=True)
    centered = values - mean_val
    variance = jnp.mean(centered * centered, -1, keepdims=True)
    recip = lax.rsqrt(variance + EPS_NORM)
    return (centered * recip, recip)


def norm_back(unit, recip, upstream):
    mean_up = jnp.mean(upstream, -1, keepdims=True)
    mean_cross = jnp.mean(upstream * unit, -1, keepdims=True)
    return recip * (upstream - mean_up - unit * mean_cross)


def gelu_tanh(values):
    return jax.nn.gelu(values, approximate=True)


def dot(left, right, left_dim, right_dim):
    return lax.dot_general(
        left, right, (((left_dim,), (right_dim,)), ((), ())), preferred_element_type=F32
    )


def head_pad(part, head, heads):
    pieces = [part if other == head else jnp.zeros_like(part) for other in range(heads)]
    return pieces[0] if heads == 1 else jnp.concatenate(pieces, 0)


def unit_rows(raw):
    recip = lax.rsqrt(jnp.sum(raw * raw, 0, keepdims=True) + EPS_NORM)
    return raw * recip, recip


def key_loops(span_ref, step, body, carry):
    first, full_first = span_ref[4 * step], span_ref[4 * step + 1]
    full_last, last = span_ref[4 * step + 2], span_ref[4 * step + 3]
    carry = lax.fori_loop(first, full_first, functools.partial(body, True), carry)
    carry = lax.fori_loop(full_first, full_last, functools.partial(body, False), carry)
    return lax.fori_loop(full_last, last, functools.partial(body, True), carry)


def allowed_block(block, low_row, high_row):
    places = block * BLK + lax.broadcasted_iota(jnp.int32, (BLK, BLK), 0)
    return (places >= low_row) & (places < high_row)


def forward_kernel(
    heads, span_ref, scale_ref, low_ref, high_ref, raw_ref, out_ref, outlow_ref, lse_ref, key_s, value_s
):
    step = pl.program_id(0)
    width = heads * HD
    slots = raw_ref.shape[1]

    @pl.when(step == 0)
    def _():
        def prepare(block, carry):
            cols = pl.ds(pl.multiple_of(block * BLK, BLK), BLK)
            parts = []
            for head in range(heads):
                unit, _ = unit_rows(raw_ref[width + head * HD : width + (head + 1) * HD, cols])
                parts.append(unit)
            keys = parts[0] if heads == 1 else jnp.concatenate(parts, 0)
            key_s[cols, :] = jnp.transpose(keys).astype(BF16)
            value_s[:, cols] = raw_ref[2 * width :, cols].astype(BF16)
            return carry

        lax.fori_loop(0, slots // BLK, prepare, 0)

    cols = pl.ds(pl.multiple_of(step * BLK, BLK), BLK)
    queries = []
    for head in range(heads):
        unit, _ = unit_rows(raw_ref[head * HD : (head + 1) * HD, cols])
        queries.append(head_pad((unit * scale_ref[head]).astype(BF16), head, heads))
    low_row, high_row = low_ref[...], high_ref[...]

    def body(masked, block, carry):
        rows = pl.ds(pl.multiple_of(block * BLK, BLK), BLK)
        keys = key_s[rows, :]
        if masked:
            allowed = allowed_block(block, low_row, high_row)
        result = []
        for head in range(heads):
            total, acc = carry[head]
            probs = jnp.exp(dot(keys, queries[head], 1, 0))
            if masked:
                probs = jnp.where(allowed, probs, 0.0)
            total = total + jnp.sum(probs.reshape(BLK // 8, 8, BLK), 0)
            acc = acc + dot(value_s[head * HD : (head + 1) * HD, rows], probs.astype(BF16), 1, 0)
            result.append((total, acc))
        return tuple(result)

    start = tuple((jnp.zeros((8, BLK), F32), jnp.zeros((HD, BLK), F32)) for _ in range(heads))
    final = key_loops(span_ref, step, body, start)
    for head in range(heads):
        total, acc = final[head]
        denom = jnp.sum(total, 0, keepdims=True)
        result = acc / denom
        out_ref[head * HD : (head + 1) * HD, :] = result
        outlow_ref[head * HD : (head + 1) * HD, :] = result.astype(BF16)
        lse_ref[head : head + 1, :] = jnp.log(denom)


def backward_kernel(
    heads,
    span_ref,
    scale_ref,
    low_ref,
    high_ref,
    raw_ref,
    out_ref,
    lse_ref,
    up_ref,
    grad_ref,
    qsum_ref,
    key_s,
    keyt_s,
    value_s,
    gkey_s,
    gvalue_s,
):
    step = pl.program_id(0)
    width = heads * HD
    slots = raw_ref.shape[1]

    @pl.when(step == 0)
    def _():
        def prepare(block, carry):
            cols = pl.ds(pl.multiple_of(block * BLK, BLK), BLK)
            parts = []
            for head in range(heads):
                unit, _ = unit_rows(raw_ref[width + head * HD : width + (head + 1) * HD, cols])
                parts.append(unit)
            keys = parts[0] if heads == 1 else jnp.concatenate(parts, 0)
            keyt_s[:, cols] = keys.astype(BF16)
            key_s[cols, :] = jnp.transpose(keys).astype(BF16)
            value_s[cols, :] = jnp.transpose(raw_ref[2 * width :, cols]).astype(BF16)
            gkey_s[cols, :] = jnp.zeros((BLK, width), F32)
            gvalue_s[cols, :] = jnp.zeros((BLK, width), F32)
            return carry

        lax.fori_loop(0, slots // BLK, prepare, 0)

    cols = pl.ds(pl.multiple_of(step * BLK, BLK), BLK)
    units, recips, queries, query_rows, ups, up_rows, deltas, lses = [], [], [], [], [], [], [], []
    for head in range(heads):
        part = slice(head * HD, (head + 1) * HD)
        unit, recip = unit_rows(raw_ref[part, cols])
        units.append(unit)
        recips.append(recip)
        padded = head_pad(unit * scale_ref[head], head, heads)
        queries.append(padded.astype(BF16))
        query_rows.append(jnp.transpose(padded).astype(BF16))
        up = up_ref[part, :].astype(F32)
        padded = head_pad(up, head, heads)
        ups.append(padded.astype(BF16))
        up_rows.append(jnp.transpose(padded).astype(BF16))
        deltas.append(jnp.sum(up * out_ref[part, :], 0, keepdims=True))
        lses.append(lse_ref[head : head + 1, :])
    low_row, high_row = low_ref[...], high_ref[...]

    def body(masked, block, carry):
        rows = pl.ds(pl.multiple_of(block * BLK, BLK), BLK)
        keys, values = key_s[rows, :], value_s[rows, :]
        if masked:
            allowed = allowed_block(block, low_row, high_row)
        result = []
        gkey, gvalue = gkey_s[rows, :], gvalue_s[rows, :]
        for head in range(heads):
            probs = jnp.exp(dot(keys, queries[head], 1, 0) - lses[head])
            if masked:
                probs = jnp.where(allowed, probs, 0.0)
            grad_probs = dot(values, ups[head], 1, 0)
            grad_scores = (probs * (grad_probs - deltas[head])).astype(BF16)
            gvalue = gvalue + dot(probs.astype(BF16), up_rows[head], 1, 0)
            gkey = gkey + dot(grad_scores, query_rows[head], 1, 0)
            result.append(
                carry[head] + dot(keyt_s[head * HD : (head + 1) * HD, rows], grad_scores, 1, 0)
            )
        gkey_s[rows, :] = gkey
        gvalue_s[rows, :] = gvalue
        return tuple(result)

    start = tuple(jnp.zeros((HD, BLK), F32) for _ in range(heads))
    final = key_loops(span_ref, step, body, start)
    for head in range(heads):
        grad, unit = final[head], units[head]
        cross = grad * unit
        qsum_ref[head : head + 1, :] = jnp.sum(cross, 0, keepdims=True)
        scaled = scale_ref[head] * grad
        back = recips[head] * (scaled - unit * jnp.sum(scaled * unit, 0, keepdims=True))
        grad_ref[head * HD : (head + 1) * HD, cols] = back.astype(BF16)

    @pl.when(step == pl.num_programs(0) - 1)
    def _():
        def finish(block, carry):
            cols = pl.ds(pl.multiple_of(block * BLK, BLK), BLK)
            gkey = jnp.transpose(gkey_s[cols, :])
            for head in range(heads):
                unit, recip = unit_rows(raw_ref[width + head * HD : width + (head + 1) * HD, cols])
                grad = gkey[head * HD : (head + 1) * HD, :]
                back = recip * (grad - unit * jnp.sum(grad * unit, 0, keepdims=True))
                grad_ref[width + head * HD : width + (head + 1) * HD, cols] = back.astype(BF16)
            grad_ref[2 * width :, cols] = jnp.transpose(gvalue_s[cols, :]).astype(BF16)
            return carry

        lax.fori_loop(0, slots // BLK, finish, 0)


def whole_spec(shape):
    return pl.BlockSpec(shape, lambda step, *_: (0,) * len(shape))


def column_spec(rows):
    return pl.BlockSpec((rows, BLK), lambda step, *_: (0, step))


def attention_forward(raw, spans, scales, low, high, heads):
    width, slots = heads * HD, raw.shape[1]
    return pl.pallas_call(
        functools.partial(forward_kernel, heads),
        grid_spec=pltpu.PrefetchScalarGridSpec(
            num_scalar_prefetch=2,
            grid=(slots // BLK,),
            in_specs=[column_spec(1), column_spec(1), whole_spec(raw.shape)],
            out_specs=[column_spec(width), column_spec(width), column_spec(heads)],
            scratch_shapes=[pltpu.VMEM((slots, width), BF16), pltpu.VMEM((width, slots), BF16)],
        ),
        out_shape=[
            jax.ShapeDtypeStruct((width, slots), F32),
            jax.ShapeDtypeStruct((width, slots), BF16),
            jax.ShapeDtypeStruct((heads, slots), F32),
        ],
        compiler_params=pltpu.CompilerParams(
            dimension_semantics=("arbitrary",), vmem_limit_bytes=48 * 2**20
        ),
        cost_estimate=pl.CostEstimate(
            flops=heads * slots * slots * 64, bytes_accessed=12 * 2**20, transcendentals=heads * slots * slots // 3
        ),
        name="attend",
    )(spans, scales, low, high, raw)


def attention_backward(raw, out, lse, up, spans, scales, low, high, heads):
    width, slots = heads * HD, raw.shape[1]
    return pl.pallas_call(
        functools.partial(backward_kernel, heads),
        grid_spec=pltpu.PrefetchScalarGridSpec(
            num_scalar_prefetch=2,
            grid=(slots // BLK,),
            in_specs=[
                column_spec(1),
                column_spec(1),
                whole_spec(raw.shape),
                column_spec(width),
                column_spec(heads),
                column_spec(width),
            ],
            out_specs=[whole_spec(raw.shape), column_spec(heads)],
            scratch_shapes=[
                pltpu.VMEM((slots, width), BF16),
                pltpu.VMEM((width, slots), BF16),
                pltpu.VMEM((slots, width), BF16),
                pltpu.VMEM((slots, width), F32),
                pltpu.VMEM((slots, width), F32),
            ],
        ),
        out_shape=[
            jax.ShapeDtypeStruct(raw.shape, BF16),
            jax.ShapeDtypeStruct((heads, slots), F32),
        ],
        compiler_params=pltpu.CompilerParams(
            dimension_semantics=("arbitrary",), vmem_limit_bytes=56 * 2**20
        ),
        cost_estimate=pl.CostEstimate(
            flops=heads * slots * slots * 160, bytes_accessed=16 * 2**20, transcendentals=heads * slots * slots // 3
        ),
        name="attend_back",
    )(spans, scales, low, high, raw, out, lse, up)


def intervals(lengths_row, slots):
    places = jnp.arange(slots, dtype=jnp.int32)
    ends = jnp.cumsum(lengths_row)
    low = jnp.zeros((slots,), jnp.int32)
    high = jnp.zeros((slots,), jnp.int32)
    for item in range(3):
        begin, finish = ends[item] - lengths_row[item], ends[item]
        table = jnp.where(
            lengths_row[item] == BIG_LEN, jnp.array(BIG_CUMS, jnp.int32), jnp.array(SMALL_CUMS, jnp.int32)
        )
        inside = (places >= begin) & (places < finish)
        reach = jnp.full((slots,), table[0], jnp.int32)
        for level in range(1, len(BIG_CUMS)):
            reach = jnp.where(places - begin >= table[level - 1], table[level], reach)
        low = jnp.where(inside, begin, low)
        high = jnp.where(inside, begin + reach, high)
    padding = places >= ends[2]
    low = jnp.where(padding, ends[2], low)
    high = jnp.where(padding, slots, high)
    blocks_low, blocks_high = low.reshape(-1, BLK), high.reshape(-1, BLK)
    first = blocks_low[:, 0] // BLK
    last = (blocks_high[:, -1] + BLK - 1) // BLK
    full_first = jnp.minimum((blocks_low[:, -1] + BLK - 1) // BLK, last)
    full_last = jnp.maximum(blocks_high[:, 0] // BLK, full_first)
    spans = jnp.stack([first, full_first, full_last, last], 1).reshape(-1)
    return low[None, :], high[None, :], spans


def shards(
    block_input,
    lengths,
    scale_ids,
    class_ids,
    code_ids,
    cotangent,
    class_table,
    ada_weight,
    ada_bias,
    qkv_weight,
    qv_bias,
    qk_scale,
    proj_weight,
    proj_bias,
    fc1_weight,
    fc1_bias,
    fc2_weight,
    fc2_bias,
):
    count, data_count = lax.axis_size("head"), lax.axis_size("dp")
    me, data_me = lax.axis_index("head"), lax.axis_index("dp")
    _, local, width = block_input.shape
    slots = local * count
    heads = qk_scale.shape[0]
    feats = heads * HD
    hidden_here = fc1_weight.shape[1]
    quarter = jnp.bitwise_and(data_me, 3)
    order = jnp.array(ORDER, jnp.int32)
    rel_quarters = jnp.bitwise_xor(quarter, order)
    abs_to_rel = jnp.take(order, jnp.bitwise_xor(quarter, jnp.arange(4, dtype=jnp.int32)))

    ring = list(range(0, count, 2)) + list(range(count - 1, 0, -2))
    half_count = count // 2
    offsets = [0]
    for away in range(1, half_count):
        offsets += [away, -away]
    offsets.append(half_count)
    my_pos = jnp.where(me % 2 == 0, me // 2, count - 1 - me // 2)

    def at(away):
        pos = (my_pos + away + count) % count
        return jnp.where(pos < half_count, 2 * pos, 2 * (count - 1 - pos) + 1)

    def rot(value, away):
        pairs = [(ring[(i + away) % count], ring[i]) for i in range(count)]
        return lax.ppermute(value, "head", pairs)

    def swap(value, mask):
        return lax.ppermute(value, "dp", [(i, i ^ mask) for i in range(data_count)])

    def xor_head(value, mask):
        return lax.ppermute(value, "head", [(i, i ^ mask) for i in range(count)])

    def ring_gather(value):
        half = value.shape[0] // 2
        got = {0: value}
        for away in range(1, half_count):
            got[away] = rot(got[away - 1], 1)
            got[-away] = rot(got[1 - away], -1)
        got[half_count] = jnp.concatenate(
            [rot(got[half_count - 1][:half], 1), rot(got[1 - half_count][half:], -1)], 0
        )
        return got

    def ring_reduce(block):
        far = block(half_count)
        half = far.shape[0] // 2
        up, down = rot(far[:half], -1), rot(far[half:], 1)
        near = block(half_count - 1)
        ups = jnp.concatenate([near[:half].astype(F32) + up, near[half:].astype(F32)], 0)
        near = block(1 - half_count)
        downs = jnp.concatenate([near[:half].astype(F32), near[half:].astype(F32) + down], 0)
        for away in range(half_count - 1, 0, -1):
            up, down = rot(ups.astype(BF16), -1), rot(downs.astype(BF16), 1)
            if away > 1:
                ups = block(away - 1).astype(F32) + up
                downs = block(1 - away).astype(F32) + down
        return block(0).astype(F32) + up.astype(F32) + down.astype(F32)

    cond = jnp.take(class_table, class_ids, axis=0).astype(F32)
    act = jax.nn.silu(cond).astype(BF16)
    mod_local = jnp.dot(act, ada_weight, preferred_element_type=F32)[0] + ada_bias.astype(F32)
    small = jnp.concatenate([mod_local, fc1_bias.astype(F32)])[None, :]
    small_all = jnp.concatenate(
        [small] + [xor_head(small, mask) for mask in range(1, count)], 0
    )
    small_all = jnp.take(
        small_all, jnp.bitwise_xor(me, jnp.arange(count, dtype=jnp.int32)), axis=0
    )
    mod_here = mod_local.shape[0]
    modulation = small_all[:, :mod_here].reshape(6, width)
    shift_one, scale_one, gate_one, shift_two, scale_two, gate_two = [
        modulation[i : i + 1] for i in range(6)
    ]
    class_rows = jnp.concatenate(
        [class_ids] + [swap(class_ids, mask) for mask in range(1, data_count)], 0
    )

    def quarters(value):
        return value.reshape(4, value.shape[0] // 4, width)

    fc1_rows, fc2_rows, proj_rows = quarters(fc1_weight.T), quarters(fc2_weight), quarters(proj_weight)
    fc_part, proj_part = fc1_rows.shape[1], proj_rows.shape[1]

    def pick(rows):
        return lax.dynamic_index_in_dim(rows, quarter, 0, keepdims=False)

    def spread(own, own_all):
        got = ring_gather(own)
        result = [own_all[i : i + 1] for i in range(4)]
        pairs = [(away, -away) for away in range(1, half_count)] + [(half_count,)]
        for group in pairs:
            mine = jnp.stack([got[away] for away in group], 0)
            both = jnp.stack([mine, swap(mine, 2)], 0)
            other = swap(both, 1)
            for i in range(2):
                result[i] = jnp.concatenate([result[i], both[i]], 0)
                result[2 + i] = jnp.concatenate([result[2 + i], other[i]], 0)
        return jnp.stack(result, 0)

    first_own = jnp.concatenate([fc1_rows, proj_rows], 1)
    first_full = spread(pick(first_own), jnp.take(first_own, rel_quarters, axis=0))
    second_full = spread(pick(fc2_rows), jnp.take(fc2_rows, rel_quarters, axis=0))
    fc1_full = first_full[:, :, :fc_part].reshape(-1, width)
    proj_full = jnp.take(first_full[:, :, fc_part:], abs_to_rel, axis=0)
    proj_full = jnp.transpose(proj_full, (1, 0, 2, 3)).reshape(-1, width)
    fc2_full = second_full.reshape(-1, width)
    offset_heads = jnp.stack([at(away) for away in offsets])
    bias_full = jnp.take(small_all[:, mod_here:], offset_heads, axis=0).reshape(count, 4, fc_part)
    bias_full = jnp.transpose(jnp.take(bias_full, rel_quarters, axis=1), (1, 0, 2)).reshape(1, -1)

    inputs_full = block_input[0].astype(F32)
    unit_one, recip_one = normalize(inputs_full)
    unit_low = unit_one.astype(BF16)
    qkv_rows = jnp.transpose(qkv_weight.T.reshape(heads, 3, HD, width), (1, 0, 2, 3)).reshape(
        3 * feats, width
    )
    qkv_mod = (qkv_rows.astype(F32) * (1.0 + scale_one)).astype(BF16)
    bias_pair = qv_bias.astype(F32).reshape(heads, 2, HD)
    qkv_bias = jnp.stack([bias_pair[:, 0], jnp.zeros_like(bias_pair[:, 0]), bias_pair[:, 1]], 0)
    qkv_bias = qkv_bias.reshape(3 * feats, 1) + jnp.sum(
        qkv_rows.astype(F32) * shift_one, 1, keepdims=True
    )
    units = ring_gather(unit_low)
    unit_all = jnp.zeros((slots, width), BF16)
    raw = jnp.zeros((3 * feats, slots), F32)
    for away in offsets:
        piece = units[away]
        start = at(away) * local
        unit_all = lax.dynamic_update_slice(unit_all, piece, (start, 0))
        raw = lax.dynamic_update_slice(raw, dot(qkv_mod, piece, 1, 1) + qkv_bias, (0, start))
    low, high, spans = intervals(lengths[0], slots)
    scale_exp = jnp.exp(qk_scale)
    out, out_low, lse = attention_forward(raw, spans, scale_exp, low, high, heads)

    attended = []
    for away in offsets:
        piece = lax.dynamic_slice(out_low, (0, at(-away) * local), (feats, local))
        attended.append(piece if away == 0 else rot(piece, away))
    attended = jnp.concatenate(attended, 0)
    attn_branch = dot(attended, proj_full, 0, 0) + proj_bias.astype(F32)
    resid = inputs_full + gate_one * attn_branch
    unit_two, recip_two = normalize(resid)
    normed_two = (unit_two * (1.0 + scale_two) + shift_two).astype(BF16)
    pre_act = dot(normed_two, fc1_full, 1, 1) + bias_full
    hidden = gelu_tanh(pre_act).astype(BF16)
    mlp_branch = dot(hidden, fc2_full, 1, 0) + fc2_bias.astype(F32)
    block_output = (resid + gate_two * mlp_branch).astype(BF16)

    cot_full = cotangent[0].astype(F32)
    grad_mlp = (cot_full * gate_two).astype(BF16)
    grad_gate_two = jnp.sum(cot_full * mlp_branch, 0)
    fc2_bias_sum = jnp.sum(grad_mlp.astype(F32), 0)
    grad_hidden = dot(grad_mlp, fc2_full, 1, 1)
    _, gelu_pull = jax.vjp(gelu_tanh, pre_act)
    grad_pre = gelu_pull(grad_hidden)[0].astype(BF16)
    fc1_bias_sum = jnp.sum(grad_pre.astype(F32), 0)
    grad_normed_two = dot(grad_pre, fc1_full, 1, 0)
    grad_shift_two = jnp.sum(grad_normed_two, 0)
    grad_scale_two = jnp.sum(grad_normed_two * unit_two, 0)
    grad_resid = cot_full + norm_back(unit_two, recip_two, grad_normed_two * (1.0 + scale_two))
    grad_attn = (grad_resid * gate_one).astype(BF16)
    grad_gate_one = jnp.sum(grad_resid * attn_branch, 0)
    proj_bias_sum = jnp.sum(grad_attn.astype(F32), 0)
    grad_attended = dot(proj_full, grad_attn, 1, 1).astype(BF16)
    up = jnp.zeros((feats, slots), BF16)
    for index, away in enumerate(offsets):
        piece = grad_attended[index * feats : (index + 1) * feats]
        piece = piece if away == 0 else rot(piece, -away)
        up = lax.dynamic_update_slice(up, piece, (0, at(-away) * local))

    half_cols = 2 * count * fc_part

    def reduce_rows(send, keep, part):
        kept = keep.astype(F32) + swap(send.astype(BF16), 1)
        kept = kept.reshape(2, count, part, width)
        mine = (kept[0] + swap(kept[1].astype(BF16), 2)).astype(BF16)
        return mine

    fc2_mine = reduce_rows(
        dot(hidden[:, half_cols:], grad_mlp, 0, 0), dot(hidden[:, :half_cols], grad_mlp, 0, 0), fc_part
    )
    fc1_mine = reduce_rows(
        dot(grad_pre[:, half_cols:], normed_two, 0, 0),
        dot(grad_pre[:, :half_cols], normed_two, 0, 0),
        fc_part,
    )
    proj_grad = dot(attended, grad_attn, 1, 0).astype(BF16)
    proj_grad = jnp.transpose(proj_grad.reshape(count, 4, proj_part, width), (1, 0, 2, 3))
    proj_grad = jnp.take(proj_grad, rel_quarters, axis=0)
    proj_mine = reduce_rows(proj_grad[2:], proj_grad[:2], proj_part)

    def ring_rest(mine):
        total = ring_reduce(lambda away: mine[offsets.index(away)])
        mask = 4
        while mask < data_count:
            total = total + swap(total.astype(BF16), mask)
            mask *= 2
        total = total.astype(BF16)
        both = jnp.stack([total, swap(total, 2)], 0)
        return jnp.take(jnp.concatenate([both, swap(both, 1)], 0), abs_to_rel, axis=0)

    fc2_rows_grad = ring_rest(fc2_mine)
    first_grad = ring_rest(jnp.concatenate([fc1_mine, proj_mine], 1))
    fc2_weight_grad = fc2_rows_grad.reshape(-1, width).astype(F32)
    fc1_weight_grad = first_grad[:, :fc_part].reshape(-1, width).astype(F32).T
    proj_weight_grad = first_grad[:, fc_part:].reshape(-1, width).astype(F32)

    bounds = jnp.sum(lengths[0])
    slot_places = me * local + jnp.arange(local, dtype=jnp.int32)
    valid = slot_places < bounds
    code_range = jnp.arange(CODES, dtype=jnp.int32)
    code_hits = (code_ids[0][:, None] == code_range[None, :]) & valid[:, None]
    local_counts = jnp.sum(code_hits.astype(F32), 0)
    fc1_bias_blocks = jnp.take(fc1_bias_sum.reshape(4, count, fc_part), abs_to_rel, axis=0)
    fc1_bias_blocks = jnp.transpose(fc1_bias_blocks, (1, 0, 2)).reshape(count, hidden_here)
    common = jnp.concatenate([local_counts, fc2_bias_sum, proj_bias_sum])
    parts = []
    for index, away in enumerate(offsets):
        piece = jnp.concatenate([fc1_bias_blocks[index], common])[None, :]
        parts.append(piece if away == 0 else rot(piece, -away))
    sums = functools.reduce(lambda a, b: a + b, parts)
    mask = 1
    while mask < data_count:
        sums = sums + swap(sums, mask)
        mask *= 2
    sums = sums[0]
    fc1_bias_grad = sums[:hidden_here]
    code_hist = sums[hidden_here : hidden_here + CODES].astype(jnp.int32)
    fc2_bias_grad = sums[hidden_here + CODES : hidden_here + CODES + width]
    proj_bias_grad = sums[hidden_here + CODES + width :]

    grad_raw, query_sums = attention_backward(
        raw, out, lse, up, spans, scale_exp, low, high, heads
    )

    def one_terms(away):
        piece = lax.dynamic_slice(grad_raw, (0, at(away) * local), (3 * feats, local))
        return dot(piece, qkv_rows, 0, 0).astype(BF16)

    grad_normed_one = ring_reduce(one_terms)
    bias_sums = jnp.sum(grad_raw.astype(F32), 1)
    qkv_grad = dot(grad_raw, unit_all, 1, 0) * (1.0 + scale_one) + bias_sums[:, None] * shift_one
    qkv_grad = qkv_grad.astype(BF16)
    scale_sums = scale_exp * jnp.sum(query_sums, 1)
    tail = jnp.concatenate([bias_sums, scale_sums])[None, :]
    mask = 1
    while mask < data_count:
        qkv_grad = (qkv_grad.astype(F32) + swap(qkv_grad, mask)).astype(BF16)
        tail = tail + swap(tail, mask)
        mask *= 2
    qkv_weight_grad = (
        jnp.transpose(qkv_grad.reshape(3, heads, HD, width), (1, 0, 2, 3))
        .reshape(3 * feats, width)
        .astype(F32)
        .T
    )
    tail = tail[0]
    qk_scale_grad = tail[3 * feats :]
    bias_sums = tail[: 3 * feats].reshape(3, heads, HD)
    qv_bias_grad = jnp.stack([bias_sums[0], bias_sums[2]], 1).reshape(-1)

    grad_shift_one = jnp.sum(grad_normed_one, 0)
    grad_scale_one = jnp.sum(grad_normed_one * unit_one, 0)
    input_grad = (
        grad_resid + norm_back(unit_one, recip_one, grad_normed_one * (1.0 + scale_one))
    ).astype(BF16)

    grad_mod = jnp.concatenate(
        [
            grad_shift_one,
            grad_scale_one,
            grad_gate_one,
            grad_shift_two,
            grad_scale_two,
            grad_gate_two,
        ]
    ).reshape(count, mod_here)
    mod_sum = lax.dynamic_slice_in_dim(grad_mod, me, 1, 0)
    for mask in range(1, count):
        mine = lax.dynamic_slice_in_dim(grad_mod, jnp.bitwise_xor(me, mask), 1, 0)
        mod_sum = mod_sum + xor_head(mine, mask)
    mod_rows = jnp.concatenate(
        [mod_sum] + [swap(mod_sum, mask) for mask in range(1, data_count)], 0
    )
    cond_rows = jnp.take(class_table, class_rows, axis=0).astype(F32)
    act_rows = jax.nn.silu(cond_rows).astype(BF16).astype(F32)
    ada_weight_grad = lax.dot_general(
        act_rows, mod_rows, (((0,), (0,)), ((), ())), precision=HIGH
    )
    ada_bias_grad = jnp.sum(mod_rows, 0)
    cond_terms = lax.dot_general(
        mod_rows, ada_weight.astype(F32), (((1,), (1,)), ((), ())), precision=HIGH
    )
    cond_sums = cond_terms
    for mask in range(1, count):
        cond_sums = cond_sums + xor_head(cond_terms, mask)
    _, silu_pull = jax.vjp(jax.nn.silu, cond_rows)
    grad_rows = silu_pull(cond_sums)[0]
    class_range = jnp.arange(class_table.shape[0], dtype=jnp.int32)
    class_table_grad = jnp.zeros(class_table.shape, F32)
    for row in range(data_count):
        hit = class_range[:, None] == class_rows[row]
        class_table_grad = class_table_grad + jnp.where(hit, grad_rows[row][None, :], 0.0)
    return (
        block_output[None],
        input_grad[None],
        class_table_grad,
        ada_weight_grad,
        ada_bias_grad,
        qkv_weight_grad,
        qv_bias_grad,
        qk_scale_grad,
        proj_weight_grad,
        proj_bias_grad,
        fc1_weight_grad,
        fc1_bias_grad,
        fc2_weight_grad,
        fc2_bias_grad,
        code_hist,
    )


def solution(mesh):
    placed = (
        P("dp", "head", None),
        P("dp", None),
        P("dp", None),
        P("dp"),
        P("dp", "head"),
        P("dp", "head", None),
        P(),
        P(None, "head"),
        P("head"),
        P(None, "head"),
        P("head"),
        P("head"),
        P("head", None),
        P(),
        P(None, "head"),
        P("head"),
        P("head", None),
        P(),
    )
    return jax.shard_map(
        shards,
        mesh=mesh,
        in_specs=placed,
        out_specs=(
            P("dp", "head", None),
            P("dp", "head", None),
            P(),
            P(None, "head"),
            P("head"),
            P(None, "head"),
            P("head"),
            P("head"),
            P("head", None),
            P(),
            P(None, "head"),
            P("head"),
            P("head", None),
            P(),
            P(),
        ),
        check_vma=False,
    )
```

time: 2320 us -> 916 us (0.39)
  waiting for transfers between devices: 1280 us -> 208 us
  matrix products: 492 us -> 114 us
  starting transfers between devices: 0.59 us -> 217 us
  blocking collectives: 178 us -> 0 us
  Pallas kernels: 0 us -> 121 us
  other arithmetic: 227 us -> 127 us
    reduce_scatter x4 -> x0, waiting for transfers between devices: 725 us -> none  [the longest x1 281 us: shards(): lax.psum_scatter(attn_terms, 'head', scatter_dimension=1, tiled=True)]
    all_gather x4 -> x0, waiting for transfers between devices: 485 us -> none  [the longest x1 131 us: shards(): normed_one = lax.all_gather(normed_one_local, 'head', axis=1, tiled=True)]
    dot_general x71 -> x31, matrix products: 492 us -> 114 us  [the longest x28 109 us: dot(): lax.dot_general(left, right, (((left_dim,), (right_dim,)), ((), ())), pre...]
    ppermute x0 -> x128, starting transfers between devices: none -> 217 us  [the longest x38 121 us: swap(): return lax.ppermute(value, 'dp', [(i, i ^ mask) for i in range(data_count)])]
    ppermute x0 -> x128, waiting for transfers between devices: none -> 208 us  [the longest x69 121 us: rot(): return lax.ppermute(value, 'head', pairs)]
    pallas_call x0 -> x2, Pallas kernels: none -> 121 us  [the longest x1 66.4 us: attention_backward(): pl.pallas_call(functools.partial(backward_kernel, heads), grid_spec=pltpu...]
    convert_element_type x33 -> x23, other arithmetic: 124 us -> 17.1 us  [the longest x3 6.57 us: reduce_rows(): mine = (kept[0] + swap(kept[1].astype(BF16), 2)).astype(BF16)]
    all_gather x2 -> x0, blocking collectives: 85.5 us -> none  [the longest x1 60.4 us: shards(): lax.all_gather(cond_terms, ('dp', 'head'), axis=0, tiled=True)]
  transfers between devices with their start and end apart: 10 -> 128, of which waited for: 10 -> 36; matrix products, arithmetic and copies ran while one was open for 4% -> 29% of each run, Pallas kernels for 0% -> 7%
where the time goes in v1:
time: 916 us; the launch traced here: 907 us
  starting transfers between devices  217 us (24%)
  waiting for transfers between devices  208 us (23%)
  other arithmetic  127 us (14%)
  Pallas kernels  121 us (13%)
  matrix products  114 us (12%)
  local copies, waits for them, and re-layouts  111 us (12%)
  between operations  9.71 us (1%)
    ppermute x69, waiting for transfers between devices, rot(): return lax.ppermute(value, 'head', pairs)  121 us
    ppermute x38, starting transfers between devices, swap(): return lax.ppermute(value, 'dp', [(i, i ^ mask) for i in range(data_count)])  121 us
    dot_general x28, matrix products, dot(): lax.dot_general(left, right, (((left_dim,), (right_dim,)), ((), ())), pre...  109 us
    ppermute x38, waiting for transfers between devices, swap(): return lax.ppermute(value, 'dp', [(i, i ^ mask) for i in range(data_count)])  80.1 us
    ppermute x69, starting transfers between devices, rot(): return lax.ppermute(value, 'head', pairs)  66.5 us
    pallas_call x1, Pallas kernels, attention_backward(): pl.pallas_call(functools.partial(backward_kernel, heads), grid_spec=pltpu...  66.4 us
    pallas_call x1, Pallas kernels, attention_forward(): pl.pallas_call(functools.partial(forward_kernel, heads), grid_spec=pltpu....  54.3 us
    select_n x2, other arithmetic, intervals(): high = jnp.where(padding, slots, high)  42.1 us
  transfers between devices with their start and end apart: 128, of which 36 were waited for; matrix products, arithmetic and copies ran while one was open for 29% of the time, Pallas kernels for 7%

profile of v1, /device:TPU:1, one launch (start us, length us, event | category | flops | bytes accessed | tf_op | source)
XLA Modules:
  0.0 906.8 jit_solution(2131650637326354052)
XLA Ops:
  25.3 21.1 %compare_select_fusion.27.high_ref = s32[1,4096]{1,0:T(1,128)S(1)} fusion(s32[]{:T(128)} %bitcast.42, s32[]{:T(128)} %bitcast.41, s32[]{:T(128)} %bitcast.40, s32[]{:T(128)} %bitcast.39, s32[]{:T(128)} %bitcast.38, s32[]{:T(128)} %bitcast.37, s32[]{:T(128)} %bitcast.36, s32[]{:T(128)} %bitcast.35, s32[]{:T(128)} %bitcast.34, s32[]{:T(128)} %bitcast.33, ...), kind=kLoop, calls=%fused_computation.433 | loop fusion | flops 303104 | bytes 16528 | tf_op jit(solution)/shard_map/jit(_where)/select_n | solution.py:323
  46.4 21.1 %select_select_fusion = s32[16,256]{0,1:T(8,128)S(1)} fusion(s32[]{:T(128)} %bitcast.42, s32[]{:T(128)} %bitcast.41, s32[]{:T(128)} %bitcast.40, s32[]{:T(128)} %bitcast.39, s32[]{:T(128)} %bitcast.38, s32[]{:T(128)} %bitcast.37, s32[]{:T(128)} %bitcast.36, s32[]{:T(128)} %bitcast.35, s32[]{:T(128)} %bitcast.34, s32[]{:T(128)} %bitcast.33, s32[]{:T(128)} %bitcast.32, ...), kind=kLoop, calls=%fused_computation.300 | loop fusion | flops 311296 | bytes 16528 | tf_op jit(solution)/shard_map/jit(_where)/select_n | solution.py:323
  151.9 17.2 %collective-permute-done.40 = bf16[128,1024]{1,0:T(8,128)(2,1)S(1)} collective-permute-done((bf16[128,1024]{1,0:T(8,128)(2,1)}, bf16[128,1024]{1,0:T(8,128)(2,1)S(1)}, u32[]{:S(2)}, u32[]{:S(2)}) %collective-permute-start.40) | collective-permute-done | bytes 262176 | tf_op jit(solution)/shard_map/ppermute | solution.py:379
  206.5 16.1 %collective-permute-start.50 = (bf16[2,2,128,1024]{3,2,1,0:T(8,128)(2,1)S(1)}, bf16[2,2,128,1024]{3,2,1,0:T(8,128)(2,1)S(1)}, u32[]{:S(2)}, u32[]{:S(2)}) collective-permute-start(bf16[2,2,128,1024]{3,2,1,0:T(8,128)(2,1)S(1)} %pad_maximum_fusion.10), channel_id=1, source_target_pairs={{0,8},{8,0},{16,24},{24,16},{1,9},{9,1},{17,25},{25,17},{2,10},{10... | collective-permute-start | bytes 3145736 | tf_op jit(solution)/shard_map/ppermute | solution.py:382
  233.9 6.8 collective-permute-done.49
  248.1 13.7 %collective-permute-done.33 = bf16[1,160,1024]{2,1,0:T(8,128)(2,1)S(1)} collective-permute-done((bf16[1,160,1024]{2,1,0:T(8,128)(2,1)S(1)}, bf16[1,160,1024]{2,1,0:T(8,128)(2,1)S(1)}, u32[]{:S(2)}, u32[]{:S(2)}) %collective-permute-start.33) | collective-permute-done | bytes 327712 | tf_op jit(solution)/shard_map/ppermute | solution.py:382
  268.0 15.3 %collective-permute-done.9 = bf16[512,1024]{1,0:T(8,128)(2,1)} collective-permute-done((bf16[512,1024]{1,0:T(8,128)(2,1)S(1)}, bf16[512,1024]{1,0:T(8,128)(2,1)}, u32[]{:S(2)}, u32[]{:S(2)}) %collective-permute-start.9) | collective-permute-done | bytes 1048608 | tf_op jit(solution)/shard_map/ppermute | solution.py:379
  342.2 54.3 %attend.1 = (f32[128,4096]{1,0:T(8,128)S(1)}, bf16[128,4096]{1,0:T(8,128)(2,1)S(1)}, f32[2,4096]{1,0:T(2,128)S(1)}) custom-call(s32[64]{0:T(128)S(1)} %reshape.1262.span_ref, f32[2]{0:T(128)S(1)} %exp.17.scale_ref, s32[1,4096]{1,0:T(1,128)S(1)} %compare_select_fusion.28.low_ref, s32[1,4096]{1,0:T(1,128)S(1)} %compare_select_fusion.27.high_ref, ...), custom_call_target="tpu_custom_call" | custom-call | flops 2147483648 | bytes 12582912 | tf_op jit(solution)/shard_map/attend/pallas_call | solution.py:243
  406.6 14.3 %collective-permute-done.17 = bf16[128,512]{1,0:T(8,128)(2,1)S(1)} collective-permute-done((bf16[128,512]{1,0:T(8,128)(2,1)S(1)}, bf16[128,512]{1,0:T(8,128)(2,1)S(1)}, u32[]{:S(2)}, u32[]{:S(2)}) %collective-permute-start.17) | collective-permute-done | bytes 131104 | tf_op jit(solution)/shard_map/ppermute | solution.py:379
  424.4 10.0 %multiply_convert_fusion = (bf16[512,4096]{1,0:T(8,128)(2,1)}, f32[512,4096]{1,0:T(8,128)}) fusion(f32[4096]{0:T(1024)S(1)} %copy-done.63, bf16[4096,1024]{1,0:T(8,128)(2,1)S(1)} %bitcast.505, f32[512,1024]{1,0:T(8,128)S(1)} %get-tuple-element.132, f32[1024]{0:T(1024)S(1)} %bitcast.584, f32[1024]{0:T(1024)S(1)} %bitcast.587, f32[512]{0:T(512)S(1)} %add_rsqrt_fusion, ...), kind=kOutput, calls=%fused_computation.30 | convolution fusion | flops 4318560256 | bytes 23097344 | tf_op jit(solution)/shard_map/dot_general | solution.py:43
  434.4 13.6 %convert_reduce_fusion.1 = (f32[4096]{0:T(1024)S(1)}, bf16[512,4096]{1,0:T(8,128)(2,1)}) fusion(f32[512,4096]{1,0:T(8,128)} %get-tuple-element.299, f32[4096]{0:T(1024)S(1)} %copy-done.63, bf16[4096,1024]{1,0:T(8,128)(2,1)S(1)} %bitcast.504, bf16[1,512,1024]{2,1,0:T(8,128)(2,1)} %param.35, f32[1024]{0:T(1024)S(1)} %bitcast.592), kind=kOutput, calls=%fused_computation.28 | convolution fusion | flops 4344770560 | bytes 22056960 | tf_op jit(solution)/shard_map/dot_general | solution.py:43
  448.0 9.5 %multiply_reduce_fusion = (f32[1024]{0:T(1024)}, f32[512]{0:T(512)S(1)}, f32[512]{0:T(512)S(1)}, f32[1024]{0:T(1024)}, f32[512,1024]{1,0:T(8,128)}) fusion(f32[512,1024]{1,0:T(8,128)} %copy-done.37, f32[512]{0:T(512)S(1)} %add_rsqrt_fusion, f32[512]{0:T(512)S(1)} %broadcast_multiply_fusion.4, f32[1024]{0:T(1024)S(1)} %bitcast.588, ...), kind=kOutput, calls=%fused_computation.93 | convolution fusion | flops 4299682816 | bytes 16797696 | tf_op jit(solution)/shard_map/dot_general | solution.py:43
  469.4 11.2 %convert_reduce_fusion.5 = (f32[1024]{0:T(1024)S(1)}, f32[1024]{0:T(1024)}, bf16[1,512,1024]{2,1,0:T(8,128)(2,1)}, f32[1024]{0:T(1024)S(1)}, bf16[512,1024]{1,0:T(8,128)(2,1)S(1)}, /*index=5*/f32[512,1024]{1,0:T(8,128)}) fusion(f32[1024]{0:T(1024)S(1)} %bitcast.594, bf16[1,512,1024]{2,1,0:T(8,128)(2,1)S(1)} %copy-done.95, f32[1024]{0:T(1024)S(1)} %copy-done.80, ...), kind=kOutput, calls=%fused_computation.91 | convolution fusion | flops 4307022848 | bytes 22056960 | tf_op jit(solution)/shard_map/dot_general | solution.py:43
  537.6 66.4 %attend_back.1 = (bf16[384,4096]{1,0:T(8,128)(2,1)}, f32[2,4096]{1,0:T(2,128)}) custom-call(s32[64]{0:T(128)} %copy-done.3, f32[2]{0:T(128)} %copy-done.4, s32[1,4096]{1,0:T(1,128)} %copy-done.1, s32[1,4096]{1,0:T(1,128)} %copy-done.2, f32[384,4096]{1,0:T(8,128)} %fusion.43.raw_ref, f32[128,4096]{1,0:T(8,128)} %copy-done.5, f32[2,4096]{1,0:T(2,128)} %copy-done.6, ...), custom_call_target="tpu_custom_call" | custom-call | flops 5368709120 | bytes 16777216 | tf_op jit(solution)/shard_map/attend_back/pallas_call | solution.py:269
  622.3 6.8 add_convert_fusion.10
  629.1 10.4 %collective-permute-done.66 = bf16[512,1024]{1,0:T(8,128)(2,1)S(1)} collective-permute-done((bf16[512,1024]{1,0:T(8,128)(2,1)S(1)}, bf16[512,1024]{1,0:T(8,128)(2,1)S(1)}, u32[]{:S(2)}, u32[]{:S(2)}) %collective-permute-start.66) | collective-permute-done | bytes 1048608 | tf_op jit(solution)/shard_map/ppermute | solution.py:379
  642.8 14.5 %collective-permute-start.91 = (f32[1,386]{1,0:T(1,128)S(1)}, f32[1,386]{1,0:T(1,128)S(1)}, u32[]{:S(2)}, u32[]{:S(2)}) collective-permute-start(f32[1,386]{1,0:T(1,128)S(1)} %bitcast.581), channel_id=1, source_target_pairs={{0,8},{8,0},{16,24},{24,16},{1,9},{9,1},{17,25},{25,17},{2,10},{10... | collective-permute-start | bytes 4640 | tf_op jit(solution)/shard_map/ppermute | solution.py:382
  661.1 9.8 %collective-permute-start.93 = (bf16[2048,1024]{1,0:T(8,128)(2,1)}, bf16[2048,1024]{1,0:T(8,128)(2,1)}, u32[]{:S(2)}, u32[]{:S(2)}) collective-permute-start(bf16[2048,1024]{1,0:T(8,128)(2,1)} %convolution_convert_fusion.1), channel_id=1, source_target_pairs={{0,8},{8,0},{16,24},{24,16},{1,9},{9,1},{17,25},{25,17},{2,10},{10... | collective-permute-start | bytes 12582920 | tf_op jit(solution)/shard_map/ppermute | solution.py:382
  671.4 12.5 %collective-permute-start.92 = (f32[1,386]{1,0:T(1,128)S(1)}, f32[1,386]{1,0:T(1,128)S(1)}, u32[]{:S(2)}, u32[]{:S(2)}) collective-permute-start(f32[1,386]{1,0:T(1,128)S(1)} %add.980), channel_id=1, source_target_pairs={{0,16},{8,24},{16,0},{24,8},{1,17},{9,25},{17,1},{25,9},{2,18},{10... | collective-permute-start | bytes 4640 | tf_op jit(solution)/shard_map/ppermute | solution.py:382
  691.0 16.2 %collective-permute-done.68 = bf16[512,1024]{1,0:T(8,128)(2,1)S(1)} collective-permute-done((bf16[512,1024]{1,0:T(8,128)(2,1)S(1)}, bf16[512,1024]{1,0:T(8,128)(2,1)S(1)}, u32[]{:S(2)}, u32[]{:S(2)}) %collective-permute-start.68) | collective-permute-done | bytes 1048608 | tf_op jit(solution)/shard_map/ppermute | solution.py:379
  747.6 8.1 collective-permute-start.78
  762.1 52.0 %collective-permute-done.78 = f32[1,768]{1,0:T(1,128)S(1)} collective-permute-done((f32[1,768]{1,0:T(1,128)S(1)}, f32[1,768]{1,0:T(1,128)S(1)}, u32[]{:S(2)}, u32[]{:S(2)}) %collective-permute-start.78) | collective-permute-done | bytes 3104 | tf_op jit(solution)/shard_map/ppermute | solution.py:382
  869.5 8.7 collective-permute-start.127
  885.3 6.4 collective-permute-start.106
  (762 shorter events, 461.4 us)
Async XLA Ops:
  0.7 105.1 %collective-permute-start.86 = (s32[1]{0:T(128)}, s32[1]{0:T(128)}, u32[]{:S(2)}, u32[]{:S(2)}) collective-permute-start(s32[1]{0:T(128)} %param.33), channel_id=1, source_target_pairs={{0,8},{8,0},{16,24},{24,16},{1,9},{9,1},{17,25},{25,17},{2,10},{10... | collective-permute-start | bytes 20 | tf_op jit(solution)/shard_map/ppermute | solution.py:382
  0.9 106.6 %collective-permute-start.87 = (s32[1]{0:T(128)}, s32[1]{0:T(128)}, u32[]{:S(2)}, u32[]{:S(2)}) collective-permute-start(s32[1]{0:T(128)} %param.33), channel_id=1, source_target_pairs={{0,16},{8,24},{16,0},{24,8},{1,17},{9,25},{17,1},{25,9},{2,18},{10... | collective-permute-start | bytes 20 | tf_op jit(solution)/shard_map/ppermute | solution.py:382
  3.5 107.1 %collective-permute-start.88 = (s32[1]{0:T(128)}, s32[1]{0:T(128)}, u32[]{:S(2)}, u32[]{:S(2)}) collective-permute-start(s32[1]{0:T(128)} %param.33), channel_id=1, source_target_pairs={{0,24},{8,16},{16,8},{24,0},{1,25},{9,17},{17,9},{25,1},{2,26},{10... | collective-permute-start | bytes 20 | tf_op jit(solution)/shard_map/ppermute | solution.py:382
  6.8 109.2 %collective-permute-start.6 = (f32[1,1280]{1,0:T(1,128)S(1)}, f32[1,1280]{1,0:T(1,128)S(1)}, u32[]{:S(2)}, u32[]{:S(2)}) collective-permute-start(f32[1,1280]{1,0:T(1,128)S(1)} %broadcast_in_dim.274), channel_id=1, source_target_pairs={{0,7},{1,6},{2,5},{3,4},{4,3},{5,2},{6,1},{7,0},{8,15},{9,14},{10,... | collective-permute-start | bytes 15368 | tf_op jit(solution)/shard_map/ppermute | solution.py:385
  11.6 104.7 %collective-permute-start.5 = (f32[1,1280]{1,0:T(1,128)S(1)}, f32[1,1280]{1,0:T(1,128)S(1)}, u32[]{:S(2)}, u32[]{:S(2)}) collective-permute-start(f32[1,1280]{1,0:T(1,128)S(1)} %broadcast_in_dim.274), channel_id=1, source_target_pairs={{0,6},{1,7},{2,4},{3,5},{4,2},{5,3},{6,0},{7,1},{8,14},{9,15},{10,... | collective-permute-start | bytes 15368 | tf_op jit(solution)/shard_map/ppermute | solution.py:385
  125.8 101.1 %collective-permute-start.8 = (bf16[512,1024]{1,0:T(8,128)(2,1)}, bf16[512,1024]{1,0:T(8,128)(2,1)}, u32[]{:S(2)}, u32[]{:S(2)}) collective-permute-start(bf16[512,1024]{1,0:T(8,128)(2,1)} %get-tuple-element.130), channel_id=1, source_target_pairs={{1,0},{0,2},{2,4},{4,6},{6,7},{7,5},{5,3},{3,1},{9,8},{8,10},{10,1... | collective-permute-start | bytes 3145736 | tf_op jit(solution)/shard_map/ppermute | solution.py:379
  142.0 80.7 %collective-permute-start.7 = (bf16[512,1024]{1,0:T(8,128)(2,1)S(1)}, bf16[512,1024]{1,0:T(8,128)(2,1)S(1)}, u32[]{:S(2)}, u32[]{:S(2)}) collective-permute-start(bf16[512,1024]{1,0:T(8,128)(2,1)S(1)} %copy-done.50), channel_id=1, source_target_pairs={{2,0},{4,2},{6,4},{7,6},{5,7},{3,5},{1,3},{0,1},{10,8},{12,10},{14... | collective-permute-start | bytes 3145736 | tf_op jit(solution)/shard_map/ppermute | solution.py:379
  143.8 42.0 %collective-permute-start.46 = (bf16[2,128,1024]{2,1,0:T(8,128)(2,1)S(1)}, bf16[2,128,1024]{2,1,0:T(8,128)(2,1)S(1)}, u32[]{:S(2)}, u32[]{:S(2)}) collective-permute-start(bf16[2,128,1024]{2,1,0:T(8,128)(2,1)S(1)} %get-tuple-element.219), channel_id=1, source_target_pairs={{0,16},{8,24},{16,0},{24,8},{1,17},{9,25},{17,1},{25,9},{2,18},{10... | collective-permute-start | bytes 1572872 | tf_op jit(solution)/shard_map/ppermute | solution.py:382
  199.2 46.6 %collective-permute-start.31 = (bf16[2,160,1024]{2,1,0:T(8,128)(2,1)S(1)}, bf16[2,160,1024]{2,1,0:T(8,128)(2,1)S(1)}, u32[]{:S(2)}, u32[]{:S(2)}) collective-permute-start(bf16[2,160,1024]{2,1,0:T(8,128)(2,1)S(1)} %get-tuple-element.209), channel_id=1, source_target_pairs={{0,16},{8,24},{16,0},{24,8},{1,17},{9,25},{17,1},{25,9},{2,18},{10... | collective-permute-start | bytes 1966088 | tf_op jit(solution)/shard_map/ppermute | solution.py:382
  199.8 46.1 %collective-permute-start.48 = (bf16[2,128,1024]{2,1,0:T(8,128)(2,1)S(1)}, bf16[2,128,1024]{2,1,0:T(8,128)(2,1)S(1)}, u32[]{:S(2)}, u32[]{:S(2)}) collective-permute-start(bf16[2,128,1024]{2,1,0:T(8,128)(2,1)S(1)} %get-tuple-element.215), channel_id=1, source_target_pairs={{0,16},{8,24},{16,0},{24,8},{1,17},{9,25},{17,1},{25,9},{2,18},{10... | collective-permute-start | bytes 1572872 | tf_op jit(solution)/shard_map/ppermute | solution.py:382
  206.5 57.1 %collective-permute-start.50 = (bf16[2,2,128,1024]{3,2,1,0:T(8,128)(2,1)S(1)}, bf16[2,2,128,1024]{3,2,1,0:T(8,128)(2,1)S(1)}, u32[]{:S(2)}, u32[]{:S(2)}) collective-permute-start(bf16[2,2,128,1024]{3,2,1,0:T(8,128)(2,1)S(1)} %pad_maximum_fusion.10), channel_id=1, source_target_pairs={{0,8},{8,0},{16,24},{24,16},{1,9},{9,1},{17,25},{25,17},{2,10},{10... | collective-permute-start | bytes 3145736 | tf_op jit(solution)/shard_map/ppermute | solution.py:382
  240.7 57.2 %collective-permute-start.34 = (bf16[2,2,160,1024]{3,2,1,0:T(8,128)(2,1)S(1)}, bf16[2,2,160,1024]{3,2,1,0:T(8,128)(2,1)S(1)}, u32[]{:S(2)}, u32[]{:S(2)}) collective-permute-start(bf16[2,2,160,1024]{3,2,1,0:T(8,128)(2,1)S(1)} %pad_maximum_fusion.6), channel_id=1, source_target_pairs={{0,8},{8,0},{16,24},{24,16},{1,9},{9,1},{17,25},{25,17},{2,10},{10... | collective-permute-start | bytes 3932168 | tf_op jit(solution)/shard_map/ppermute | solution.py:382
  263.6 36.3 %collective-permute-start.53 = (bf16[2,1,128,1024]{3,2,1,0:T(8,128)(2,1)S(1)}, bf16[2,1,128,1024]{3,2,1,0:T(8,128)(2,1)S(1)}, u32[]{:S(2)}, u32[]{:S(2)}) collective-permute-start(bf16[2,1,128,1024]{3,2,1,0:T(8,128)(2,1)S(1)} %pad_maximum_fusion.24), channel_id=1, source_target_pairs={{0,8},{8,0},{16,24},{24,16},{1,9},{9,1},{17,25},{25,17},{2,10},{10... | collective-permute-start | bytes 1572872 | tf_op jit(solution)/shard_map/ppermute | solution.py:382
  267.6 31.0 %collective-permute-start.52 = (bf16[2,2,128,1024]{3,2,1,0:T(8,128)(2,1)S(1)}, bf16[2,2,128,1024]{3,2,1,0:T(8,128)(2,1)S(1)}, u32[]{:S(2)}, u32[]{:S(2)}) collective-permute-start(bf16[2,2,128,1024]{3,2,1,0:T(8,128)(2,1)S(1)} %pad_maximum_fusion.12), channel_id=1, source_target_pairs={{0,8},{8,0},{16,24},{24,16},{1,9},{9,1},{17,25},{25,17},{2,10},{10... | collective-permute-start | bytes 3145736 | tf_op jit(solution)/shard_map/ppermute | solution.py:382
  502.3 33.4 %collective-permute-start.60 = (bf16[128,512]{1,0:T(8,128)(2,1)}, bf16[128,512]{1,0:T(8,128)(2,1)}, u32[]{:S(2)}, u32[]{:S(2)}) collective-permute-start(bf16[128,512]{1,0:T(8,128)(2,1)} %get-tuple-element.176), channel_id=1, source_target_pairs={{7,0},{5,2},{3,4},{1,6},{0,7},{2,5},{4,3},{6,1},{15,8},{13,10},{11... | collective-permute-start | bytes 393224 | tf_op jit(solution)/shard_map/ppermute | solution.py:379
  504.6 30.2 %collective-permute-start.59 = (bf16[128,512]{1,0:T(8,128)(2,1)}, bf16[128,512]{1,0:T(8,128)(2,1)}, u32[]{:S(2)}, u32[]{:S(2)}) collective-permute-start(bf16[128,512]{1,0:T(8,128)(2,1)} %get-tuple-element.177), channel_id=1, source_target_pairs={{6,0},{7,2},{5,4},{3,6},{1,7},{0,5},{2,3},{4,1},{14,8},{15,10},{13... | collective-permute-start | bytes 393224 | tf_op jit(solution)/shard_map/ppermute | solution.py:379
  529.9 183.8 %collective-permute-start.116 = (bf16[2048,1024]{1,0:T(8,128)(2,1)}, bf16[2048,1024]{1,0:T(8,128)(2,1)}, u32[]{:S(2)}, u32[]{:S(2)}) collective-permute-start(bf16[2048,1024]{1,0:T(8,128)(2,1)} %convolution_convert_fusion), channel_id=1, source_target_pairs={{0,8},{8,0},{16,24},{24,16},{1,9},{9,1},{17,25},{25,17},{2,10},{10... | collective-permute-start | bytes 12582920 | tf_op jit(solution)/shard_map/ppermute | solution.py:382
  661.1 62.5 %collective-permute-start.93 = (bf16[2048,1024]{1,0:T(8,128)(2,1)}, bf16[2048,1024]{1,0:T(8,128)(2,1)}, u32[]{:S(2)}, u32[]{:S(2)}) collective-permute-start(bf16[2048,1024]{1,0:T(8,128)(2,1)} %convolution_convert_fusion.1), channel_id=1, source_target_pairs={{0,8},{8,0},{16,24},{24,16},{1,9},{9,1},{17,25},{25,17},{2,10},{10... | collective-permute-start | bytes 12582920 | tf_op jit(solution)/shard_map/ppermute | solution.py:382
  688.1 67.6 %collective-permute-start.90 = (bf16[384,1024]{1,0:T(8,128)(2,1)}, bf16[384,1024]{1,0:T(8,128)(2,1)}, u32[]{:S(2)}, u32[]{:S(2)}) collective-permute-start(bf16[384,1024]{1,0:T(8,128)(2,1)} %add_convert_fusion.9), channel_id=1, source_target_pairs={{0,16},{8,24},{16,0},{24,8},{1,17},{9,25},{17,1},{25,9},{2,18},{10... | collective-permute-start | bytes 2359304 | tf_op jit(solution)/shard_map/ppermute | solution.py:382
  721.1 94.6 %collective-permute-start.117 = (bf16[8,128,1024]{2,1,0:T(8,128)(2,1)}, bf16[8,128,1024]{2,1,0:T(8,128)(2,1)}, u32[]{:S(2)}, u32[]{:S(2)}) collective-permute-start(bf16[8,128,1024]{2,1,0:T(8,128)(2,1)} %bitcast.205), channel_id=1, source_target_pairs={{0,16},{8,24},{16,0},{24,8},{1,17},{9,25},{17,1},{25,9},{2,18},{10... | collective-permute-start | bytes 6291464 | tf_op jit(solution)/shard_map/ppermute | solution.py:382
  733.4 88.7 %collective-permute-start.94 = (bf16[8,128,1024]{2,1,0:T(8,128)(2,1)}, bf16[8,128,1024]{2,1,0:T(8,128)(2,1)}, u32[]{:S(2)}, u32[]{:S(2)}) collective-permute-start(bf16[8,128,1024]{2,1,0:T(8,128)(2,1)} %bitcast.168), channel_id=1, source_target_pairs={{0,16},{8,24},{16,0},{24,8},{1,17},{9,25},{17,1},{25,9},{2,18},{10... | collective-permute-start | bytes 6291464 | tf_op jit(solution)/shard_map/ppermute | solution.py:382
  747.6 66.6 %collective-permute-start.78 = (f32[1,768]{1,0:T(1,128)S(1)}, f32[1,768]{1,0:T(1,128)S(1)}, u32[]{:S(2)}, u32[]{:S(2)}) collective-permute-start(f32[1,768]{1,0:T(1,128)S(1)} %add_add_fusion.1), channel_id=1, source_target_pairs={{0,24},{8,16},{16,8},{24,0},{1,25},{9,17},{17,9},{25,1},{2,26},{10... | collective-permute-start | bytes 9224 | tf_op jit(solution)/shard_map/ppermute | solution.py:382
  755.6 58.5 %collective-permute-start.77 = (f32[1,768]{1,0:T(1,128)S(1)}, f32[1,768]{1,0:T(1,128)S(1)}, u32[]{:S(2)}, u32[]{:S(2)}) collective-permute-start(f32[1,768]{1,0:T(1,128)S(1)} %add_add_fusion.1), channel_id=1, source_target_pairs={{0,16},{8,24},{16,0},{24,8},{1,17},{9,25},{17,1},{25,9},{2,18},{10... | collective-permute-start | bytes 9224 | tf_op jit(solution)/shard_map/ppermute | solution.py:382
  755.7 58.4 %collective-permute-start.76 = (f32[1,768]{1,0:T(1,128)S(1)}, f32[1,768]{1,0:T(1,128)S(1)}, u32[]{:S(2)}, u32[]{:S(2)}) collective-permute-start(f32[1,768]{1,0:T(1,128)S(1)} %add_add_fusion.1), channel_id=1, source_target_pairs={{0,8},{8,0},{16,24},{24,16},{1,9},{9,1},{17,25},{25,17},{2,10},{10... | collective-permute-start | bytes 9224 | tf_op jit(solution)/shard_map/ppermute | solution.py:382
  (213 other events, 4849.6 us)

commit v2 on v1

v2 whole, which is shorter than its diff:
```python
import functools

import jax
import jax.numpy as jnp
from jax import lax
from jax.experimental import pallas as pl
from jax.experimental.pallas import tpu as pltpu
from jax.sharding import PartitionSpec as P

HD = 64
CODES = 4096
BLK = 256
FORWARD_BLOCK = (512, 512)
BACKWARD_BLOCK = (256, 512)
EPS_NORM = 1e-06
HIGH = lax.Precision.HIGHEST
F32 = jnp.float32
BF16 = jnp.bfloat16
BIG_LEN = 2240
BIG_CUMS = (1, 5, 14, 30, 66, 147, 316, 640, 1216, 2240)
SMALL_CUMS = (1, 5, 14, 30, 55, 91, 155, 255, 424, 680)


def normalize(values):
    mean_val = jnp.mean(values, -1, keepdims=True)
    centered = values - mean_val
    variance = jnp.mean(centered * centered, -1, keepdims=True)
    recip = lax.rsqrt(variance + EPS_NORM)
    return (centered * recip, recip)


def norm_back(unit, recip, upstream):
    mean_up = jnp.mean(upstream, -1, keepdims=True)
    mean_cross = jnp.mean(upstream * unit, -1, keepdims=True)
    return recip * (upstream - mean_up - unit * mean_cross)


def gelu_tanh(values):
    return jax.nn.gelu(values, approximate=True)


def dot(left, right, left_dim, right_dim):
    return lax.dot_general(
        left, right, (((left_dim,), (right_dim,)), ((), ())), preferred_element_type=F32
    )


def head_pad(part, head, heads):
    pieces = [part if other == head else jnp.zeros_like(part) for other in range(heads)]
    return pieces[0] if heads == 1 else jnp.concatenate(pieces, 0)


def unit_rows(raw):
    recip = lax.rsqrt(jnp.sum(raw * raw, 0, keepdims=True) + EPS_NORM)
    return raw * recip, recip


def interval(places, lengths_ref, slots):
    first, second, third = lengths_ref[0], lengths_ref[1], lengths_ref[2]
    end_one, end_two = first + second, first + second + third
    low = jnp.where(places >= end_one, end_one, jnp.where(places >= first, first, 0))
    size = jnp.where(places >= end_one, third, jnp.where(places >= first, second, first))
    big, offset = size == BIG_LEN, places - low
    reach = jnp.where(big, BIG_CUMS[0], SMALL_CUMS[0])
    for level in range(1, len(BIG_CUMS)):
        passed = offset >= jnp.where(big, BIG_CUMS[level - 1], SMALL_CUMS[level - 1])
        reach = jnp.where(passed, jnp.where(big, BIG_CUMS[level], SMALL_CUMS[level]), reach)
    padding = places >= end_two
    return jnp.where(padding, end_two, low), jnp.where(padding, slots, low + reach)


def key_spans(step, lengths_ref, slots, rows_q, rows_k):
    first_low, first_high = interval(step * rows_q, lengths_ref, slots)
    last_low, last_high = interval(step * rows_q + rows_q - 1, lengths_ref, slots)
    first = lax.div(first_low, rows_k)
    last = lax.div(last_high + rows_k - 1, rows_k)
    full_first = jnp.minimum(lax.div(last_low + rows_k - 1, rows_k), last)
    full_last = jnp.maximum(lax.div(first_high, rows_k), full_first)
    rows = interval(
        step * rows_q + lax.broadcasted_iota(jnp.int32, (1, rows_q), 1), lengths_ref, slots
    )
    return (first, full_first, full_last, last), rows


def key_loops(spans, body, carry):
    first, full_first, full_last, last = spans
    carry = lax.fori_loop(first, full_first, functools.partial(body, True), carry)
    carry = lax.fori_loop(full_first, full_last, functools.partial(body, False), carry)
    return lax.fori_loop(full_last, last, functools.partial(body, True), carry)


def allowed_block(block, rows_k, low_row, high_row):
    places = block * rows_k + lax.broadcasted_iota(jnp.int32, (rows_k, low_row.shape[1]), 0)
    return (places >= low_row) & (places < high_row)


def project_kernel(
    heads, place_ref, scale_ref, piece_ref, weight_ref, mod_ref, bias_ref, *refs
):
    width = heads * HD
    raw_ref, query_ref, key_ref, keyt_ref, value_ref, valuet_ref, unit_ref = refs[-7:]
    piece = piece_ref[...]
    unit_ref[...] = piece
    normed = (piece.astype(F32) * (1.0 + mod_ref[1:2, :]) + mod_ref[0:1, :]).astype(BF16)
    raw = dot(weight_ref[...], normed, 1, 1) + bias_ref[...]
    raw_ref[...] = raw
    for head in range(heads):
        part = slice(head * HD, (head + 1) * HD)
        unit, _ = unit_rows(raw[part])
        query_ref[part, :] = (unit * scale_ref[head]).astype(BF16)
    keys = [unit_rows(raw[width + head * HD : width + (head + 1) * HD])[0] for head in range(heads)]
    keys = keys[0] if heads == 1 else jnp.concatenate(keys, 0)
    values = raw[2 * width :]
    keyt_ref[...] = keys.astype(BF16)
    key_ref[...] = jnp.transpose(keys).astype(BF16)
    valuet_ref[...] = values.astype(BF16)
    value_ref[...] = jnp.transpose(values).astype(BF16)


def project(place, piece, weight, mod, bias, scales, held, heads, slots):
    width, local, depth = heads * HD, piece.shape[0], piece.shape[1]

    def fixed(shape):
        return pl.BlockSpec(shape, lambda step, *_: (0, 0))

    def columns(rows):
        return pl.BlockSpec((rows, local), lambda step, place, scales: (0, place[0]))

    def lines(cols):
        return pl.BlockSpec((local, cols), lambda step, place, scales: (place[0], 0))

    shapes = [
        jax.ShapeDtypeStruct((3 * width, slots), F32),
        jax.ShapeDtypeStruct((width, slots), BF16),
        jax.ShapeDtypeStruct((slots, width), BF16),
        jax.ShapeDtypeStruct((width, slots), BF16),
        jax.ShapeDtypeStruct((slots, width), BF16),
        jax.ShapeDtypeStruct((width, slots), BF16),
        jax.ShapeDtypeStruct((slots, depth), BF16),
    ]
    held = list(held)
    return pl.pallas_call(
        functools.partial(project_kernel, heads),
        grid_spec=pltpu.PrefetchScalarGridSpec(
            num_scalar_prefetch=2,
            grid=(1,),
            in_specs=[
                fixed((local, depth)),
                fixed((3 * width, depth)),
                fixed((2, depth)),
                fixed((3 * width, 1)),
            ]
            + [pl.BlockSpec(memory_space=pl.ANY)] * len(held),
            out_specs=[
                columns(3 * width),
                columns(width),
                lines(width),
                columns(width),
                lines(width),
                columns(width),
                lines(depth),
            ],
        ),
        out_shape=shapes,
        input_output_aliases={6 + i: i for i in range(len(held))},
        compiler_params=pltpu.CompilerParams(vmem_limit_bytes=40 * 2**20),
        cost_estimate=pl.CostEstimate(
            flops=2 * 3 * width * local * depth, bytes_accessed=8 * 2**20, transcendentals=0
        ),
        name="project",
    )(place, scales, piece, weight, mod, bias, *held)


def forward_kernel(heads, rows_k, lengths_ref, query_ref, key_ref, valuet_ref, out_ref, lse_ref):
    step = pl.program_id(0)
    slots, rows_q = key_ref.shape[0], query_ref.shape[1]
    queries = [
        head_pad(query_ref[head * HD : (head + 1) * HD, :], head, heads) for head in range(heads)
    ]
    spans, (low_row, high_row) = key_spans(step, lengths_ref, slots, rows_q, rows_k)

    def body(masked, block, carry):
        rows = pl.ds(pl.multiple_of(block * rows_k, rows_k), rows_k)
        keys = key_ref[rows, :]
        if masked:
            allowed = allowed_block(block, rows_k, low_row, high_row)
        result = []
        for head in range(heads):
            total, acc = carry[head]
            probs = jnp.exp(dot(keys, queries[head], 1, 0))
            if masked:
                probs = jnp.where(allowed, probs, 0.0)
            total = total + jnp.sum(probs.reshape(rows_k // 8, 8, rows_q), 0)
            acc = acc + dot(
                valuet_ref[head * HD : (head + 1) * HD, rows], probs.astype(BF16), 1, 0
            )
            result.append((total, acc))
        return tuple(result)

    start = tuple(
        (jnp.zeros((8, rows_q), F32), jnp.zeros((HD, rows_q), F32)) for _ in range(heads)
    )
    final = key_loops(spans, body, start)
    for head in range(heads):
        total, acc = final[head]
        denom = jnp.sum(total, 0, keepdims=True)
        out_ref[head * HD : (head + 1) * HD, :] = (acc / denom).astype(BF16)
        lse_ref[head : head + 1, :] = jnp.log(denom)


def backward_kernel(
    heads,
    rows_k,
    lengths_ref,
    scale_ref,
    raw_ref,
    query_ref,
    key_ref,
    keyt_ref,
    value_ref,
    lse_ref,
    up_ref,
    grad_ref,
    qsum_ref,
    gkey_s,
    gvalue_s,
    probs_s,
    gprobs_s,
):
    step = pl.program_id(0)
    width = heads * HD
    slots, rows_q = raw_ref.shape[1], query_ref.shape[1]

    @pl.when(step == 0)
    def _():
        gkey_s[...] = jnp.zeros_like(gkey_s)
        gvalue_s[...] = jnp.zeros_like(gvalue_s)

    queries, query_rows, ups, up_rows, lses = [], [], [], [], []
    for head in range(heads):
        part = slice(head * HD, (head + 1) * HD)
        padded = head_pad(query_ref[part, :], head, heads)
        queries.append(padded)
        query_rows.append(jnp.transpose(padded.astype(F32)).astype(BF16))
        padded = head_pad(up_ref[part, :], head, heads)
        ups.append(padded)
        up_rows.append(jnp.transpose(padded.astype(F32)).astype(BF16))
        lses.append(lse_ref[head : head + 1, :])
    spans, (low_row, high_row) = key_spans(step, lengths_ref, slots, rows_q, rows_k)

    def first(masked, block, carry):
        rows = pl.ds(pl.multiple_of(block * rows_k, rows_k), rows_k)
        keys, values = key_ref[rows, :], value_ref[rows, :]
        if masked:
            allowed = allowed_block(block, rows_k, low_row, high_row)
        result = []
        for head in range(heads):
            probs = jnp.exp(dot(keys, queries[head], 1, 0) - lses[head])
            if masked:
                probs = jnp.where(allowed, probs, 0.0)
            grad_probs = dot(values, ups[head], 1, 0)
            probs_s[head, rows, :] = probs
            gprobs_s[head, rows, :] = grad_probs
            terms = (probs * grad_probs).reshape(rows_k // 8, 8, rows_q)
            result.append(carry[head] + jnp.sum(terms, 0))
        return tuple(result)

    deltas = key_loops(spans, first, tuple(jnp.zeros((8, rows_q), F32) for _ in range(heads)))
    deltas = [jnp.sum(delta, 0, keepdims=True) for delta in deltas]

    def second(block, carry):
        rows = pl.ds(pl.multiple_of(block * rows_k, rows_k), rows_k)
        result = []
        gkey, gvalue = gkey_s[rows, :], gvalue_s[rows, :]
        for head in range(heads):
            probs = probs_s[head, rows, :]
            grad_scores = (probs * (gprobs_s[head, rows, :] - deltas[head])).astype(BF16)
            gvalue = gvalue + dot(probs.astype(BF16), up_rows[head], 1, 0)
            gkey = gkey + dot(grad_scores, query_rows[head], 1, 0)
            keyt = keyt_ref[head * HD : (head + 1) * HD, rows]
            result.append(carry[head] + dot(keyt, grad_scores, 1, 0))
        gkey_s[rows, :] = gkey
        gvalue_s[rows, :] = gvalue
        return tuple(result)

    start = tuple(jnp.zeros((HD, rows_q), F32) for _ in range(heads))
    final = lax.fori_loop(spans[0], spans[3], second, start)
    cols = pl.ds(pl.multiple_of(step * rows_q, rows_q), rows_q)
    for head in range(heads):
        part = slice(head * HD, (head + 1) * HD)
        grad = final[head]
        unit, recip = unit_rows(raw_ref[part, cols])
        qsum_ref[head : head + 1, :] = jnp.sum(grad * unit, 0, keepdims=True)
        scaled = scale_ref[head] * grad
        back = recip * (scaled - unit * jnp.sum(scaled * unit, 0, keepdims=True))
        grad_ref[part, cols] = back.astype(BF16)

    @pl.when(step == pl.num_programs(0) - 1)
    def _():
        def finish(block, carry):
            cols = pl.ds(pl.multiple_of(block * BLK, BLK), BLK)
            gkey = jnp.transpose(gkey_s[cols, :])
            for head in range(heads):
                part = slice(width + head * HD, width + (head + 1) * HD)
                unit, recip = unit_rows(raw_ref[part, cols])
                grad = gkey[head * HD : (head + 1) * HD, :]
                back = recip * (grad - unit * jnp.sum(grad * unit, 0, keepdims=True))
                grad_ref[part, cols] = back.astype(BF16)
            grad_ref[2 * width :, cols] = jnp.transpose(gvalue_s[cols, :]).astype(BF16)
            return carry

        lax.fori_loop(0, slots // BLK, finish, 0)


def whole_spec(shape):
    return pl.BlockSpec(shape, lambda step, *_: (0,) * len(shape))


def column_spec(rows, cols):
    return pl.BlockSpec((rows, cols), lambda step, *_: (0, step))


def attention_forward(query, key, valuet, lengths, heads):
    width, slots = query.shape
    rows_q, rows_k = FORWARD_BLOCK
    return pl.pallas_call(
        functools.partial(forward_kernel, heads, rows_k),
        grid_spec=pltpu.PrefetchScalarGridSpec(
            num_scalar_prefetch=1,
            grid=(slots // rows_q,),
            in_specs=[column_spec(width, rows_q), whole_spec(key.shape), whole_spec(valuet.shape)],
            out_specs=[column_spec(width, rows_q), column_spec(heads, rows_q)],
        ),
        out_shape=[
            jax.ShapeDtypeStruct((width, slots), BF16),
            jax.ShapeDtypeStruct((heads, slots), F32),
        ],
        compiler_params=pltpu.CompilerParams(
            dimension_semantics=("arbitrary",), vmem_limit_bytes=32 * 2**20
        ),
        cost_estimate=pl.CostEstimate(
            flops=heads * slots * slots * 1000, bytes_accessed=4 * 2**20, transcendentals=0
        ),
        name="attend",
    )(lengths, query, key, valuet)


def attention_backward(raw, query, key, keyt, value, lse, up, lengths, scales, heads):
    width, slots = query.shape
    rows_q, rows_k = BACKWARD_BLOCK
    return pl.pallas_call(
        functools.partial(backward_kernel, heads, rows_k),
        grid_spec=pltpu.PrefetchScalarGridSpec(
            num_scalar_prefetch=2,
            grid=(slots // rows_q,),
            in_specs=[
                whole_spec(raw.shape),
                column_spec(width, rows_q),
                whole_spec(key.shape),
                whole_spec(keyt.shape),
                whole_spec(value.shape),
                column_spec(heads, rows_q),
                column_spec(width, rows_q),
            ],
            out_specs=[whole_spec(raw.shape), column_spec(heads, rows_q)],
            scratch_shapes=[
                pltpu.VMEM((slots, width), F32),
                pltpu.VMEM((slots, width), F32),
                pltpu.VMEM((heads, slots, rows_q), F32),
                pltpu.VMEM((heads, slots, rows_q), F32),
            ],
        ),
        out_shape=[
            jax.ShapeDtypeStruct(raw.shape, BF16),
            jax.ShapeDtypeStruct((heads, slots), F32),
        ],
        compiler_params=pltpu.CompilerParams(
            dimension_semantics=("arbitrary",), vmem_limit_bytes=56 * 2**20
        ),
        cost_estimate=pl.CostEstimate(
            flops=heads * slots * slots * 2000, bytes_accessed=14 * 2**20, transcendentals=0
        ),
        name="attend_back",
    )(lengths, scales, raw, query, key, keyt, value, lse, up)


def after(value, *others):
    return lax.optimization_barrier((value, *others))[0]


def shards(
    block_input,
    lengths,
    scale_ids,
    class_ids,
    code_ids,
    cotangent,
    class_table,
    ada_weight,
    ada_bias,
    qkv_weight,
    qv_bias,
    qk_scale,
    proj_weight,
    proj_bias,
    fc1_weight,
    fc1_bias,
    fc2_weight,
    fc2_bias,
):
    count, data_count = lax.axis_size("head"), lax.axis_size("dp")
    me, data_me = lax.axis_index("head"), lax.axis_index("dp")
    _, local, width = block_input.shape
    slots = local * count
    heads = qk_scale.shape[0]
    feats = heads * HD
    hidden_here = fc1_weight.shape[1]
    data_masks = [1 << bit for bit in range(data_count.bit_length() - 1)]
    both_axes = ("dp", "head")

    ring = list(range(0, count, 2)) + list(range(count - 1, 0, -2))
    half_count = count // 2
    offsets = [0]
    for away in range(1, half_count):
        offsets += [away, -away]
    offsets.append(half_count)
    my_pos = jnp.where(me % 2 == 0, me // 2, count - 1 - me // 2)

    def at(away):
        pos = (my_pos + away + count) % count
        return jnp.where(pos < half_count, 2 * pos, 2 * (count - 1 - pos) + 1)

    def rot(value, away):
        pairs = [(ring[(i + away) % count], ring[i]) for i in range(count)]
        return lax.ppermute(value, "head", pairs)

    def swap(value, mask):
        return lax.ppermute(value, "dp", [(i, i ^ mask) for i in range(data_count)])

    def xor_head(value, mask):
        return lax.ppermute(value, "head", [(i, i ^ mask) for i in range(count)])

    def head_sum_far(value):
        total = value
        for mask in range(2, count, 2):
            total = total + xor_head(value, mask)
        return total

    def head_sum_near(value):
        return value + xor_head(value, 1)

    inputs_full = block_input[0].astype(F32)
    unit_one, recip_one = normalize(inputs_full)
    unit_low = unit_one.astype(BF16)

    hidden_part, feat_part = hidden_here // data_count, feats // data_count
    fc1_part = lax.dynamic_slice(fc1_weight, (0, data_me * hidden_part), (width, hidden_part)).T
    proj_part = lax.dynamic_slice(proj_weight, (data_me * feat_part, 0), (feat_part, width))
    fc2_part = lax.dynamic_slice(fc2_weight, (data_me * hidden_part, 0), (hidden_part, width))
    first_full = lax.all_gather(
        jnp.concatenate([fc1_part, proj_part], 0), both_axes, axis=0, tiled=False
    ).reshape(data_count, count, hidden_part + feat_part, width)
    fc2_full = lax.all_gather(fc2_part, both_axes, axis=0, tiled=True)
    fc1_full = first_full[:, :, :hidden_part].reshape(-1, width)
    proj_full = jnp.transpose(first_full[:, :, hidden_part:], (1, 0, 2, 3)).reshape(-1, width)

    cond = jnp.take(class_table, class_ids, axis=0).astype(F32)
    act = jax.nn.silu(cond).astype(BF16)
    mod_local = jnp.dot(act, ada_weight, preferred_element_type=F32)[0] + ada_bias.astype(F32)
    small = jnp.concatenate([mod_local, fc1_bias.astype(F32)])[None, :]
    pieces = [small] + [xor_head(small, mask) for mask in range(2, count, 2)]
    units = {0: unit_low, 1: rot(unit_low, 1), -1: rot(unit_low, -1)}
    units[1], units[-1], pieces = lax.optimization_barrier((units[1], units[-1], pieces))
    pieces = jnp.concatenate(pieces, 0)
    if half_count > 2:
        units[2], units[-2] = rot(units[1], 1), rot(units[-1], -1)
    small_all = jnp.stack([pieces, xor_head(pieces, 1)], 1).reshape(count, -1)
    if half_count > 2:
        units[2], units[-2], small_all = lax.optimization_barrier(
            (units[2], units[-2], small_all)
        )
    small_all = jnp.take(
        small_all, jnp.bitwise_xor(me, jnp.arange(count, dtype=jnp.int32)), axis=0
    )
    mod_here = mod_local.shape[0]
    modulation = small_all[:, :mod_here].reshape(6, width)
    shift_one, scale_one, gate_one, shift_two, scale_two, gate_two = [
        modulation[i : i + 1] for i in range(6)
    ]
    bias_full = small_all[:, mod_here:].reshape(count, data_count, hidden_part)
    bias_full = jnp.transpose(bias_full, (1, 0, 2)).reshape(1, -1)

    qkv_rows = jnp.transpose(
        after(qkv_weight, small_all).T.reshape(heads, 3, HD, width), (1, 0, 2, 3)
    ).reshape(3 * feats, width)
    bias_pair = qv_bias.astype(F32).reshape(heads, 2, HD)
    qkv_bias = jnp.stack([bias_pair[:, 0], jnp.zeros_like(bias_pair[:, 0]), bias_pair[:, 1]], 0)
    qkv_bias = qkv_bias.reshape(3 * feats, 1)
    scale_exp = jnp.exp(qk_scale)

    def put(held, away):
        place = at(away).astype(jnp.int32)[None]
        return project(
            place, units[away], qkv_rows, modulation[:2], qkv_bias, scale_exp, held, heads, slots
        )

    for away in range(3, half_count):
        units[away], units[-away] = rot(units[away - 1], 1), rot(units[1 - away], -1)
    held = put([], 0)
    for away in range(1, half_count - 1):
        held = put(put(held, away), -away)
        if away == 1:
            last, units[half_count - 1], units[1 - half_count] = lax.optimization_barrier(
                (held[1], units[half_count - 1], units[1 - half_count])
            )
            held = [held[0], last] + list(held[2:])
    half = local // 2
    ends = [
        rot(units[half_count - 1][:half], 1),
        rot(units[1 - half_count][half:], -1),
    ]
    held = put(put(held, half_count - 1), 1 - half_count)
    units[half_count] = jnp.concatenate(ends, 0)
    held = put(held, half_count)
    raw, query, key, keyt, value, valuet, unit_all = held
    query, fc1_full, proj_full = lax.optimization_barrier((query, fc1_full, proj_full))
    out_low, lse = attention_forward(query, key, valuet, lengths[0], heads)

    attended = jnp.zeros((feats * count, local), BF16)
    for away in offsets:
        piece = lax.dynamic_slice(out_low, (0, at(-away) * local), (feats, local))
        piece = piece if away == 0 else rot(piece, away)
        attended = lax.dynamic_update_slice(attended, piece, (at(away) * feats, 0))
    cot_full = cotangent[0].astype(F32)
    grad_mlp = (cot_full * gate_two).astype(BF16)
    grad_hidden = dot(grad_mlp, fc2_full, 1, 1)
    attended, grad_hidden = lax.optimization_barrier((attended, grad_hidden))
    attn_branch = dot(attended, proj_full, 0, 0) + proj_bias.astype(F32)
    resid = inputs_full + gate_one * attn_branch
    unit_two, recip_two = normalize(resid)
    normed_two = (unit_two * (1.0 + scale_two) + shift_two).astype(BF16)
    pre_act = dot(normed_two, fc1_full, 1, 1) + bias_full
    hidden_full, gelu_pull = jax.vjp(gelu_tanh, pre_act)
    hidden = hidden_full.astype(BF16)

    grad_pre = gelu_pull(grad_hidden)[0].astype(BF16)
    grad_normed_two = dot(grad_pre, fc1_full, 1, 0)
    grad_shift_two = jnp.sum(grad_normed_two, 0)
    grad_scale_two = jnp.sum(grad_normed_two * unit_two, 0)
    grad_resid = cot_full + norm_back(unit_two, recip_two, grad_normed_two * (1.0 + scale_two))
    grad_attn = (grad_resid * gate_one).astype(BF16)
    grad_gate_one = jnp.sum(grad_resid * attn_branch, 0)
    grad_attended = dot(proj_full, grad_attn, 1, 1).astype(BF16)
    up_pieces = {}
    for away in offsets:
        piece = lax.dynamic_slice(grad_attended, (at(away) * feats, 0), (feats, local))
        up_pieces[away] = piece if away == 0 else rot(piece, -away)

    near = [away for away in offsets if away in (1, -1, 2)]
    hidden_late, grad_pre_late, attended_late, arrived = lax.optimization_barrier(
        (hidden, grad_pre, attended, [up_pieces[away] for away in near])
    )
    for away, piece in zip(near, arrived):
        up_pieces[away] = piece
    block_cols = count * hidden_part

    def core_step(blocks):
        return {
            t: blocks(t).astype(F32) + swap(blocks(t ^ 1).astype(BF16), 1)
            for t in range(0, data_count, 2)
        }

    def fc2_block(t):
        part = jnp.bitwise_xor(data_me, t) * block_cols
        cols = lax.dynamic_slice(hidden_late, (0, part), (local, block_cols))
        return dot(cols, grad_mlp, 0, 0).reshape(count, hidden_part, width)

    def fc1_block(t):
        part = jnp.bitwise_xor(data_me, t) * block_cols
        cols = lax.dynamic_slice(grad_pre_late, (0, part), (local, block_cols))
        return dot(cols, normed_two, 0, 0).reshape(count, hidden_part, width)

    fc2_kept = core_step(fc2_block)
    fc2_stack = jnp.stack([fc2_kept[t].astype(BF16) for t in fc2_kept], 1)
    fc2_stack = fc2_stack.reshape(count, len(fc2_kept) * hidden_part, width)

    proj_grad = dot(attended_late, grad_attn, 1, 0).astype(BF16)
    proj_grad = proj_grad.reshape(count, data_count, feat_part, width)

    def first_block(t):
        part = lax.dynamic_index_in_dim(
            proj_grad, jnp.bitwise_xor(data_me, t), 1, keepdims=False
        )
        return jnp.concatenate([fc1_block(t), part.astype(F32)], 1)

    first_kept = core_step(first_block)

    def fold(kept):
        for mask in data_masks[1:]:
            kept = {
                t: kept[t] + swap(kept[t ^ mask].astype(BF16), mask)
                for t in kept
                if not t & mask
            }
        return kept[0]

    up = jnp.zeros((feats, slots), BF16)
    for away in offsets:
        up = lax.dynamic_update_slice(up, up_pieces[away], (0, at(-away) * local))
    up, first_kept, fc2_stack = lax.optimization_barrier((up, first_kept, fc2_stack))
    fc2_mine = lax.psum_scatter(fc2_stack, "head", scatter_dimension=0, tiled=True)
    fc2_mine = fc2_mine.reshape(len(fc2_kept), hidden_part, width)
    first_blocks = fold(first_kept).astype(BF16)

    def share(value):
        for mask in reversed(data_masks):
            value = jnp.stack([value, swap(value, mask)], 0)
        bits = len(data_masks)
        value = value.reshape((data_count,) + value.shape[bits:])
        table = [int(format(t, "b").zfill(bits)[::-1], 2) for t in range(data_count)]
        places = jnp.take(
            jnp.array(table, jnp.int32),
            jnp.bitwise_xor(data_me, jnp.arange(data_count, dtype=jnp.int32)),
        )
        return jnp.take(value, places, axis=0).astype(F32)

    fc2_bias_sum = jnp.sum(grad_mlp.astype(F32), 0)
    fc1_bias_sum = jnp.sum(grad_pre.astype(F32), 0)
    proj_bias_sum = jnp.sum(grad_attn.astype(F32), 0)
    valid = me * local + jnp.arange(local, dtype=jnp.int32) < jnp.sum(lengths[0])
    code_range = jnp.arange(CODES, dtype=jnp.int32)
    code_hits = (after(code_ids, units[1])[0][:, None] == code_range[None, :]) & valid[:, None]
    local_counts = jnp.sum(code_hits.astype(F32), 0)
    fc1_bias_sum = fc1_bias_sum.reshape(data_count, count, hidden_part)
    fc1_bias_sum = jnp.transpose(fc1_bias_sum, (1, 0, 2)).reshape(-1)
    early = jnp.concatenate(
        [
            local_counts,
            fc2_bias_sum,
            proj_bias_sum,
            fc1_bias_sum,
            grad_gate_one,
            grad_shift_two,
            grad_scale_two,
        ]
    )
    early, up = lax.optimization_barrier((early, up))
    early = head_sum_far(early[None, :])

    grad_raw, query_sums = attention_backward(
        raw, query, key, keyt, value, lse, up, lengths[0], scale_exp, heads
    )
    grad_raw, query_sums, first_blocks, early = lax.optimization_barrier(
        (grad_raw, query_sums, first_blocks, early)
    )

    held_rows = local + first_blocks.shape[1]
    half = held_rows // 2

    def block(away, source):
        piece = lax.dynamic_slice(source, (0, at(away) * local), (3 * feats, local))
        terms = dot(piece, qkv_rows, 0, 0).astype(BF16)
        weights = lax.dynamic_index_in_dim(first_blocks, at(away), 0, keepdims=False)
        return jnp.concatenate([terms, weights], 0).astype(F32)

    def send(ups, downs):
        return rot(ups.astype(BF16), -1), rot(downs.astype(BF16), 1)

    far = block(half_count, grad_raw)
    near_up, near_down = block(half_count - 1, grad_raw), block(1 - half_count, grad_raw)
    got_up, got_down = send(far[:half], far[half:])

    far_late, source = lax.optimization_barrier((far, grad_raw))
    bias_sums = jnp.sum(source.astype(F32), 1)
    unit_grad = dot(source, unit_all, 1, 0)
    qkv_grad = unit_grad * (1.0 + scale_one) + bias_sums[:, None] * shift_one
    qkv_grad = qkv_grad.astype(BF16)
    scale_sums = scale_exp * jnp.sum(query_sums, 1)
    rows_float = qkv_rows.astype(F32)
    grad_shift_one = jnp.sum(rows_float * bias_sums[:, None], 0)
    grad_scale_one = jnp.sum(rows_float * unit_grad, 0)
    mlp_branch = dot(after(hidden, far), fc2_full, 1, 0) + fc2_bias.astype(F32)
    block_output = (resid + gate_two * mlp_branch).astype(BF16)
    grad_gate_two = jnp.sum(cot_full * mlp_branch, 0)
    late = jnp.concatenate([grad_shift_one, grad_scale_one, grad_gate_two])[None, :]

    got_up, got_down, early, late, near_up, near_down = lax.optimization_barrier(
        (got_up, got_down, early, late, near_up, near_down)
    )
    ups = jnp.concatenate([near_up[:half] + got_up, near_up[half:]], 0)
    downs = jnp.concatenate([near_down[:half], near_down[half:] + got_down], 0)
    got_up, got_down = send(ups, downs)
    late = head_sum_far(late)
    early = head_sum_near(early)
    next_up, next_down = block(half_count - 2, source), block(2 - half_count, source)

    for away in range(half_count - 2, 0, -1):
        last = away == 1
        got_up, got_down, late, early, next_up, next_down = lax.optimization_barrier(
            (got_up, got_down, late, early, next_up, next_down)
        )
        if away == half_count - 2:
            got_up, got_down, fc2_mine = lax.optimization_barrier((got_up, got_down, fc2_mine))
        got_up, got_down = send(next_up + got_up, next_down + got_down)
        if away == half_count - 2:
            late = head_sum_near(late)[0]
            early = early[0]
            over_rows = CODES + 2 * width + count * hidden_here
            tail = jnp.concatenate([bias_sums, scale_sums, early[:over_rows]])[None, :]
            mod_all = jnp.concatenate([late[: 2 * width], early[over_rows:], late[2 * width :]])
            mod_rows = lax.dynamic_slice_in_dim(mod_all, me * mod_here, mod_here, 0)
            mod_rows = jnp.concatenate([mod_rows, class_ids.astype(F32)])[None, :]
            for mask in data_masks:
                mod_rows = jnp.concatenate([mod_rows, swap(mod_rows, mask)], 0)
                qkv_grad = (qkv_grad.astype(F32) + swap(qkv_grad, mask)).astype(BF16)
                tail = tail + swap(tail, mask)
        next_up = block(away - 1, source)
        next_down = None if last else block(1 - away, source)
        if last:
            next_down = jnp.zeros_like(next_up)

    tail = tail[0]
    mod_rows = jnp.take(
        mod_rows, jnp.bitwise_xor(data_me, jnp.arange(data_count, dtype=jnp.int32)), axis=0
    )
    class_rows = mod_rows[:, mod_here].astype(jnp.int32)
    mod_rows = mod_rows[:, :mod_here]
    cond_terms = lax.dot_general(
        mod_rows, ada_weight.astype(F32), (((1,), (1,)), ((), ())), precision=HIGH
    )
    cond_sums = head_sum_far(cond_terms)
    got_up, got_down, cond_sums, next_up = lax.optimization_barrier(
        (got_up, got_down, cond_sums, next_up)
    )
    ring_total = next_up + got_up.astype(F32) + got_down.astype(F32)
    grad_normed_one, first_mine = ring_total[:local], ring_total[local:].astype(BF16)
    cond_sums = head_sum_near(cond_sums)
    qkv_weight_grad = (
        jnp.transpose(qkv_grad.reshape(3, heads, HD, width), (1, 0, 2, 3))
        .reshape(3 * feats, width)
        .astype(F32)
        .T
    )
    bias_sums = tail[: 3 * feats].reshape(3, heads, HD)
    qv_bias_grad = jnp.stack([bias_sums[0], bias_sums[2]], 1).reshape(-1)
    qk_scale_grad = tail[3 * feats : 3 * feats + heads]
    tail = tail[3 * feats + heads :]
    code_hist = tail[:CODES].astype(jnp.int32)
    fc2_bias_grad = tail[CODES : CODES + width]
    proj_bias_grad = tail[CODES + width : CODES + 2 * width]
    fc1_bias_grad = lax.dynamic_slice_in_dim(
        tail[CODES + 2 * width :], me * hidden_here, hidden_here, 0
    )

    input_grad = (
        grad_resid + norm_back(unit_one, recip_one, grad_normed_one * (1.0 + scale_one))
    ).astype(BF16)
    fc2_mine = {t: fc2_mine[t // 2].astype(F32) for t in fc2_kept}
    fc2_weight_grad = share(fold(fc2_mine).astype(BF16)).reshape(-1, width)
    first_grad = share(first_mine)
    fc1_weight_grad = first_grad[:, :hidden_part].reshape(-1, width).T
    proj_weight_grad = first_grad[:, hidden_part:].reshape(-1, width)

    cond_rows = jnp.take(class_table, class_rows, axis=0).astype(F32)
    act_rows = jax.nn.silu(cond_rows).astype(BF16).astype(F32)
    ada_weight_grad = lax.dot_general(
        act_rows, mod_rows, (((0,), (0,)), ((), ())), precision=HIGH
    )
    ada_bias_grad = jnp.sum(mod_rows, 0)
    _, silu_pull = jax.vjp(jax.nn.silu, cond_rows)
    grad_rows = silu_pull(cond_sums)[0]
    class_range = jnp.arange(class_table.shape[0], dtype=jnp.int32)
    class_table_grad = jnp.zeros(class_table.shape, F32)
    for row in range(data_count):
        hit = class_range[:, None] == class_rows[row]
        class_table_grad = class_table_grad + jnp.where(hit, grad_rows[row][None, :], 0.0)
    return (
        block_output[None],
        input_grad[None],
        class_table_grad,
        ada_weight_grad,
        ada_bias_grad,
        qkv_weight_grad,
        qv_bias_grad,
        qk_scale_grad,
        proj_weight_grad,
        proj_bias_grad,
        fc1_weight_grad,
        fc1_bias_grad,
        fc2_weight_grad,
        fc2_bias_grad,
        code_hist,
    )


def solution(mesh):
    placed = (
        P("dp", "head", None),
        P("dp", None),
        P("dp", None),
        P("dp"),
        P("dp", "head"),
        P("dp", "head", None),
        P(),
        P(None, "head"),
        P("head"),
        P(None, "head"),
        P("head"),
        P("head"),
        P("head", None),
        P(),
        P(None, "head"),
        P("head"),
        P("head", None),
        P(),
    )
    return jax.shard_map(
        shards,
        mesh=mesh,
        in_specs=placed,
        out_specs=(
            P("dp", "head", None),
            P("dp", "head", None),
            P(),
            P(None, "head"),
            P("head"),
            P(None, "head"),
            P("head"),
            P("head"),
            P("head", None),
            P(),
            P(None, "head"),
            P("head"),
            P("head", None),
            P(),
            P(),
        ),
        check_vma=False,
    )
```

time: 916 us -> 657 us (0.72)
  starting transfers between devices: 217 us -> 87.6 us
  other arithmetic: 127 us -> 85.9 us
  matrix products: 114 us -> 79.3 us
  waiting for transfers between devices: 208 us -> 174 us
  local copies, waits for them, and re-layouts: 111 us -> 88.4 us
    ppermute x38 -> x16, starting transfers between devices: 121 us -> 31.5 us  [swap(): return lax.ppermute(value, 'dp', [(i, i ^ mask) for i in range(data_count)])]
    ppermute x38 -> x16, waiting for transfers between devices: 80.1 us -> 13.6 us  [swap(): return lax.ppermute(value, 'dp', [(i, i ^ mask) for i in range(data_count)])]
    select_n x15 -> x3, other arithmetic: 52 us -> 0.2 us  [shards(): jnp.take(mod_rows, jnp.bitwise_xor(data_me, jnp.arange(data_count, dtype=...]
    dot_general x28 -> x24, matrix products: 109 us -> 74.5 us  [dot(): lax.dot_general(left, right, (((left_dim,), (right_dim,)), ((), ())), pre...]
    ppermute x69 -> x30, starting transfers between devices: 66.5 us -> 31.6 us  [rot(): return lax.ppermute(value, 'head', pairs)]
    ppermute x21 -> x16, waiting for transfers between devices: 6.66 us -> 35.1 us  [xor_head(): return lax.ppermute(value, 'head', [(i, i ^ mask) for i in range(count)])]
    convert_element_type x17 -> x21, other arithmetic: 12.2 us -> 31.4 us  [the longest x7 12.9 us: block(): return jnp.concatenate([terms, weights], 0).astype(F32)]
    gather x10 -> x4, local copies, waits for them, and re-layouts: 19.7 us -> 4.84 us  [the longest x2 3.51 us: share(): return jnp.take(value, places, axis=0).astype(F32)]
  transfers between devices with their start and end apart: 128 -> 65, of which waited for: 36 -> 15; matrix products, arithmetic and copies ran while one was open for 29% -> 29% of each run, Pallas kernels for 7% -> 18%
where the time goes in v2:
time: 657 us; the launch traced here: 649 us
  waiting for transfers between devices  174 us (26%)
  Pallas kernels  118 us (18%)
  local copies, waits for them, and re-layouts  88.4 us (13%)
  starting transfers between devices  87.6 us (13%)
  other arithmetic  85.9 us (13%)
  matrix products  79.3 us (12%)
  between operations  16.6 us (3%)
    ppermute x30, waiting for transfers between devices, rot(): return lax.ppermute(value, 'head', pairs)  122 us
    dot_general x24, matrix products, dot(): lax.dot_general(left, right, (((left_dim,), (right_dim,)), ((), ())), pre...  74.5 us
    pallas_call x1, Pallas kernels, attention_backward(): pl.pallas_call(functools.partial(backward_kernel, heads, rows_k), grid_sp...  62.6 us
    ppermute x16, waiting for transfers between devices, xor_head(): return lax.ppermute(value, 'head', [(i, i ^ mask) for i in range(count)])  35.1 us
    ppermute x30, starting transfers between devices, rot(): return lax.ppermute(value, 'head', pairs)  31.6 us
    ppermute x16, starting transfers between devices, swap(): return lax.ppermute(value, 'dp', [(i, i ^ mask) for i in range(data_count)])  31.5 us
    pallas_call x1, Pallas kernels, attention_forward(): pl.pallas_call(functools.partial(forward_kernel, heads, rows_k), grid_spe...  30.2 us
    pallas_call x8, Pallas kernels, project(): pl.pallas_call(functools.partial(project_kernel, heads), grid_spec=pltpu....  24.7 us
  transfers between devices with their start and end apart: 65, of which 15 were waited for; matrix products, arithmetic and copies ran while one was open for 29% of the time, Pallas kernels for 18%

profile of v2, /device:TPU:1, one launch (start us, length us, event | category | flops | bytes accessed | tf_op | source)
XLA Modules:
  0.0 649.0 jit_solution(8571182696018530123)
XLA Ops:
  23.7 32.1 %collective-permute-done.piece_ref = bf16[512,1024]{1,0:T(8,128)(2,1)} collective-permute-done((bf16[512,1024]{1,0:T(8,128)(2,1)S(1)}, bf16[512,1024]{1,0:T(8,128)(2,1)}, u32[]{:S(2)}, u32[]{:S(2)}) %collective-permute-start) | collective-permute-done | bytes 1048608 | tf_op jit(solution)/shard_map/ppermute | solution.py:435
  62.9 12.7 %collective-permute-done.7 = f32[4,1280]{1,0:T(4,128)S(1)} collective-permute-done((f32[4,1280]{1,0:T(4,128)S(1)}, f32[4,1280]{1,0:T(4,128)S(1)}, u32[]{:S(2)}, u32[]{:S(2)}) %collective-permute-start.7) | collective-permute-done | bytes 20512 | tf_op jit(solution)/shard_map/ppermute | solution.py:441
  75.7 25.7 %collective-permute-done.5.piece_ref = bf16[512,1024]{1,0:T(8,128)(2,1)} collective-permute-done((bf16[512,1024]{1,0:T(8,128)(2,1)}, bf16[512,1024]{1,0:T(8,128)(2,1)}, u32[]{:S(2)}, u32[]{:S(2)}) %collective-permute-start.5) | collective-permute-done | bytes 1048608 | tf_op jit(solution)/shard_map/ppermute | solution.py:435
  120.4 13.3 %collective-permute-done.8.piece_ref = bf16[512,1024]{1,0:T(8,128)(2,1)} collective-permute-done((bf16[512,1024]{1,0:T(8,128)(2,1)}, bf16[512,1024]{1,0:T(8,128)(2,1)}, u32[]{:S(2)}, u32[]{:S(2)}) %collective-permute-start.8) | collective-permute-done | bytes 1048608 | tf_op jit(solution)/shard_map/ppermute | solution.py:435
  160.8 8.7 %slice.275 = bf16[4,8,128,1024]{3,2,1,0:T(8,128)(2,1)} slice(bf16[4,8,160,1024]{3,2,1,0:T(8,128)(2,1)} %bitcast.273), slice={[0:4], [0:8], [0:128], [0:1024]} | slice | bytes 16777216 | tf_op jit(solution)/shard_map/slice | solution.py:464
  173.5 30.2 %attend.1 = (bf16[128,4096]{1,0:T(8,128)(2,1)S(1)}, f32[2,4096]{1,0:T(2,128)S(1)}) custom-call(s32[3]{0:T(128)S(1)} %bitcast.269, bf16[128,4096]{1,0:T(8,128)(2,1)S(1)} %get-tuple-element.199.query_ref, bf16[4096,128]{1,0:T(8,128)(2,1)S(1)} %copy-done.4, bf16[128,4096]{1,0:T(8,128)(2,1)S(1)} %copy-done.8), custom_call_target="tpu_custom_call" | custom-call | flops 33554432000 | bytes 4194304 | tf_op jit(solution)/shard_map/attend/pallas_call | solution.py:326
  210.1 10.4 %fusion.41 = f32[512,4096]{1,0:T(8,128)} fusion(bf16[4096,1024]{1,0:T(8,128)(2,1)} %all-gather.4.cloned.1.call-done, bf16[1,512,1024]{2,1,0:T(8,128)(2,1)S(1)} %copy-done.46, f32[1024]{0:T(1024)} %bitcast.326), kind=kOutput, calls=%fused_computation.130 | convolution fusion | flops 4296540160 | bytes 17829888 | tf_op jit(solution)/shard_map/dot_general | solution.py:43
  231.1 4.9 collective-permute-done.17
  239.9 7.3 %fusion.106 = f32[512,4096]{1,0:T(8,128)} fusion(bf16[512,1024]{1,0:T(8,128)(2,1)S(1)} %add_convert_fusion.8, bf16[4096,1024]{1,0:T(8,128)(2,1)S(1)} %bitcast.277), kind=kOutput, calls=%fused_computation.306 | convolution fusion | flops 4294967296 | bytes 17825792 | tf_op jit(solution)/shard_map/dot_general | solution.py:43
  247.2 10.1 %convert_reduce_fusion = (f32[4096]{0:T(1024)S(1)}, bf16[512,4096]{1,0:T(8,128)(2,1)S(1)}, bf16[512,4096]{1,0:T(8,128)(2,1)S(1)}) fusion(f32[512,4096]{1,0:T(8,128)} %fusion.41, f32[512,4096]{1,0:T(8,128)} %fusion.106, f32[4096]{0:T(1024)S(1)} %slice_bitcast_fusion.2), kind=kLoop, calls=%fused_computation.15 | loop fusion | flops 52424704 | bytes 25198592 | tf_op jit(solution)/shard_map/reduce_sum | solution.py:628
  257.3 5.0 multiply_reduce_fusion
  288.6 13.6 %collective-permute-start.28 = (bf16[8,128,1024]{2,1,0:T(8,128)(2,1)}, bf16[8,128,1024]{2,1,0:T(8,128)(2,1)}, u32[]{:S(2)}, u32[]{:S(2)}) collective-permute-start(bf16[8,128,1024]{2,1,0:T(8,128)(2,1)} %convolution_convert_fusion.1), channel_id=1, source_target_pairs={{0,8},{8,0},{16,24},{24,16},{1,9},{9,1},{17,25},{25,17},{2,10},{10... | collective-permute-start | bytes 6291464 | tf_op jit(solution)/shard_map/ppermute | solution.py:438
  303.6 4.3 convolution_convert_fusion
  350.6 4.3 maximum_add_fusion.1
  354.9 5.0 maximum_add_fusion
  366.9 62.6 %attend_back.1 = (bf16[384,4096]{1,0:T(8,128)(2,1)}, f32[2,4096]{1,0:T(2,128)}) custom-call(s32[3]{0:T(128)} %bitcast.268, f32[2]{0:T(128)} %copy-done.12, f32[384,4096]{1,0:T(8,128)} %copy-done.1, bf16[128,4096]{1,0:T(8,128)(2,1)} %copy-done.2, bf16[4096,128]{1,0:T(8,128)(2,1)} %copy-done.3, bf16[128,4096]{1,0:T(8,128)(2,1)} %copy-done.5, ...), custom_call_target="tpu_custom_call" | custom-call | flops 67108864000 | bytes 14680064 | tf_op jit(solution)/shard_map/attend_back/pallas_call | solution.py:351
  429.7 4.5 add_convert_fusion
  443.5 4.5 add_convert_fusion.11
  458.0 10.5 %fusion.25 = (f32[1024]{0:T(1024)S(1)}, bf16[1,512,1024]{2,1,0:T(8,128)(2,1)}) fusion(bf16[1,512,1024]{2,1,0:T(8,128)(2,1)S(1)} %copy-done.48, f32[1024]{0:T(1024)S(1)} %copy-done.86, f32[512,1024]{1,0:T(8,128)S(1)} %copy-done.23, f32[1024]{0:T(1024)S(1)} %bitcast.332, bf16[512,4096]{1,0:T(8,128)(2,1)} %copy-done.24, ...), kind=kOutput, calls=%fused_computation.56 | convolution fusion | flops 4298636288 | bytes 16789504 | tf_op jit(solution)/shard_map/dot_general | solution.py:43
  486.5 20.9 %collective-permute-done.38 = f32[1,3072]{1,0:T(1,128)S(1)} collective-permute-done((f32[1,3072]{1,0:T(1,128)S(1)}, f32[1,3072]{1,0:T(1,128)S(1)}, u32[]{:S(2)}, u32[]{:S(2)}) %collective-permute-start.38) | collective-permute-done | bytes 12320 | tf_op jit(solution)/shard_map/ppermute | solution.py:441
  519.4 8.4 %collective-permute-done.54 = bf16[384,1024]{1,0:T(8,128)(2,1)S(1)} collective-permute-done((bf16[384,1024]{1,0:T(8,128)(2,1)S(1)}, bf16[384,1024]{1,0:T(8,128)(2,1)S(1)}, u32[]{:S(2)}, u32[]{:S(2)}) %collective-permute-start.54) | collective-permute-done | bytes 786464 | tf_op jit(solution)/shard_map/ppermute | solution.py:438
  558.0 25.0 %collective-permute-done.43 = bf16[672,1024]{1,0:T(8,128)(2,1)S(1)} collective-permute-done((bf16[672,1024]{1,0:T(8,128)(2,1)S(1)}, bf16[672,1024]{1,0:T(8,128)(2,1)S(1)}, u32[]{:S(2)}, u32[]{:S(2)}) %collective-permute-start.43) | collective-permute-done | bytes 1376288 | tf_op jit(solution)/shard_map/ppermute | solution.py:435
  598.5 16.2 %collective-permute-done.45 = bf16[672,1024]{1,0:T(8,128)(2,1)} collective-permute-done((bf16[672,1024]{1,0:T(8,128)(2,1)}, bf16[672,1024]{1,0:T(8,128)(2,1)}, u32[]{:S(2)}, u32[]{:S(2)}) %collective-permute-start.45) | collective-permute-done | bytes 1376288 | tf_op jit(solution)/shard_map/ppermute | solution.py:435
  625.9 4.3 collective-permute-start.58
  (555 shorter events, 288.1 us)
Async XLA Ops:
  7.2 153.6 %all-gather.6.cloned.1.call-start = ((), (), s32[]{:S(2)}) async-start(), calls=%async_computation.3 | async-start | bytes 10813440 | tf_op jit(solution)/shard_map/all_gather | solution.py:460
  10.2 199.8 %all-gather.4.cloned.1.call-start = ((), (), s32[]{:S(2)}) async-start(), calls=%async_computation.1 | async-start | bytes 8650752 | tf_op jit(solution)/shard_map/all_gather | solution.py:463
  12.0 535.6 %reduce-scatter.2.cloned.1.call-start = ((), (), s32[]{:S(2)}) async-start(), calls=%async_computation.2 | async-start | bytes 4718592 | tf_op jit(solution)/shard_map/reduce_scatter | solution.py:611
  19.5 36.3 %collective-permute-start = (bf16[512,1024]{1,0:T(8,128)(2,1)S(1)}, bf16[512,1024]{1,0:T(8,128)(2,1)}, u32[]{:S(2)}, u32[]{:S(2)}) collective-permute-start(bf16[512,1024]{1,0:T(8,128)(2,1)S(1)} %fusion.17.piece_ref), channel_id=1, source_target_pairs={{2,0},{4,2},{6,4},{7,6},{5,7},{3,5},{1,3},{0,1},{10,8},{12,10},{14... | collective-permute-start | bytes 3145736 | tf_op jit(solution)/shard_map/ppermute | solution.py:435
  20.8 35.0 %collective-permute-start.1 = (bf16[512,1024]{1,0:T(8,128)(2,1)S(1)}, bf16[512,1024]{1,0:T(8,128)(2,1)}, u32[]{:S(2)}, u32[]{:S(2)}) collective-permute-start(bf16[512,1024]{1,0:T(8,128)(2,1)S(1)} %fusion.17.piece_ref), channel_id=1, source_target_pairs={{1,0},{0,2},{2,4},{4,6},{6,7},{7,5},{5,3},{3,1},{9,8},{8,10},{10,1... | collective-permute-start | bytes 3145736 | tf_op jit(solution)/shard_map/ppermute | solution.py:435
  55.8 45.6 %collective-permute-start.5 = (bf16[512,1024]{1,0:T(8,128)(2,1)}, bf16[512,1024]{1,0:T(8,128)(2,1)}, u32[]{:S(2)}, u32[]{:S(2)}) collective-permute-start(bf16[512,1024]{1,0:T(8,128)(2,1)} %collective-permute-done.piece_ref), channel_id=1, source_target_pairs={{2,0},{4,2},{6,4},{7,6},{5,7},{3,5},{1,3},{0,1},{10,8},{12,10},{14... | collective-permute-start | bytes 3145736 | tf_op jit(solution)/shard_map/ppermute | solution.py:435
  56.3 45.1 %collective-permute-start.6 = (bf16[512,1024]{1,0:T(8,128)(2,1)}, bf16[512,1024]{1,0:T(8,128)(2,1)}, u32[]{:S(2)}, u32[]{:S(2)}) collective-permute-start(bf16[512,1024]{1,0:T(8,128)(2,1)} %collective-permute-done.1.piece_ref), channel_id=1, source_target_pairs={{1,0},{0,2},{2,4},{4,6},{6,7},{7,5},{5,3},{3,1},{9,8},{8,10},{10,1... | collective-permute-start | bytes 3145736 | tf_op jit(solution)/shard_map/ppermute | solution.py:435
  101.4 32.3 %collective-permute-start.8 = (bf16[512,1024]{1,0:T(8,128)(2,1)}, bf16[512,1024]{1,0:T(8,128)(2,1)}, u32[]{:S(2)}, u32[]{:S(2)}) collective-permute-start(bf16[512,1024]{1,0:T(8,128)(2,1)} %collective-permute-done.5.piece_ref), channel_id=1, source_target_pairs={{2,0},{4,2},{6,4},{7,6},{5,7},{3,5},{1,3},{0,1},{10,8},{12,10},{14... | collective-permute-start | bytes 3145736 | tf_op jit(solution)/shard_map/ppermute | solution.py:435
  101.4 32.3 %collective-permute-start.9 = (bf16[512,1024]{1,0:T(8,128)(2,1)}, bf16[512,1024]{1,0:T(8,128)(2,1)}, u32[]{:S(2)}, u32[]{:S(2)}) collective-permute-start(bf16[512,1024]{1,0:T(8,128)(2,1)} %collective-permute-done.6.piece_ref), channel_id=1, source_target_pairs={{1,0},{0,2},{2,4},{4,6},{6,7},{7,5},{5,3},{3,1},{9,8},{8,10},{10,1... | collective-permute-start | bytes 3145736 | tf_op jit(solution)/shard_map/ppermute | solution.py:435
  273.1 45.5 %collective-permute-start.22 = (bf16[128,512]{1,0:T(8,128)(2,1)}, bf16[128,512]{1,0:T(8,128)(2,1)}, u32[]{:S(2)}, u32[]{:S(2)}) collective-permute-start(bf16[128,512]{1,0:T(8,128)(2,1)} %get-tuple-element.356), channel_id=1, source_target_pairs={{4,0},{6,2},{7,4},{5,6},{3,7},{1,5},{0,3},{2,1},{12,8},{14,10},{15... | collective-permute-start | bytes 393224 | tf_op jit(solution)/shard_map/ppermute | solution.py:435
  274.4 45.3 %collective-permute-start.23 = (bf16[128,512]{1,0:T(8,128)(2,1)}, bf16[128,512]{1,0:T(8,128)(2,1)}, u32[]{:S(2)}, u32[]{:S(2)}) collective-permute-start(bf16[128,512]{1,0:T(8,128)(2,1)} %get-tuple-element.355), channel_id=1, source_target_pairs={{5,0},{3,2},{1,4},{0,6},{2,7},{4,5},{6,3},{7,1},{13,8},{11,10},{9,... | collective-permute-start | bytes 393224 | tf_op jit(solution)/shard_map/ppermute | solution.py:435
  288.6 53.1 %collective-permute-start.28 = (bf16[8,128,1024]{2,1,0:T(8,128)(2,1)}, bf16[8,128,1024]{2,1,0:T(8,128)(2,1)}, u32[]{:S(2)}, u32[]{:S(2)}) collective-permute-start(bf16[8,128,1024]{2,1,0:T(8,128)(2,1)} %convolution_convert_fusion.1), channel_id=1, source_target_pairs={{0,8},{8,0},{16,24},{24,16},{1,9},{9,1},{17,25},{25,17},{2,10},{10... | collective-permute-start | bytes 6291464 | tf_op jit(solution)/shard_map/ppermute | solution.py:438
  307.9 36.9 %collective-permute-start.29 = (bf16[8,128,1024]{2,1,0:T(8,128)(2,1)}, bf16[8,128,1024]{2,1,0:T(8,128)(2,1)}, u32[]{:S(2)}, u32[]{:S(2)}) collective-permute-start(bf16[8,128,1024]{2,1,0:T(8,128)(2,1)} %convolution_convert_fusion), channel_id=1, source_target_pairs={{0,8},{8,0},{16,24},{24,16},{1,9},{9,1},{17,25},{25,17},{2,10},{10... | collective-permute-start | bytes 6291464 | tf_op jit(solution)/shard_map/ppermute | solution.py:438
  313.8 36.8 %collective-permute-start.27 = (bf16[8,160,1024]{2,1,0:T(8,128)(2,1)}, bf16[8,160,1024]{2,1,0:T(8,128)(2,1)}, u32[]{:S(2)}, u32[]{:S(2)}) collective-permute-start(bf16[8,160,1024]{2,1,0:T(8,128)(2,1)} %pad_maximum_fusion.2), channel_id=1, source_target_pairs={{0,8},{8,0},{16,24},{24,16},{1,9},{9,1},{17,25},{25,17},{2,10},{10... | collective-permute-start | bytes 7864328 | tf_op jit(solution)/shard_map/ppermute | solution.py:438
  319.7 35.2 %collective-permute-start.26 = (bf16[8,160,1024]{2,1,0:T(8,128)(2,1)}, bf16[8,160,1024]{2,1,0:T(8,128)(2,1)}, u32[]{:S(2)}, u32[]{:S(2)}) collective-permute-start(bf16[8,160,1024]{2,1,0:T(8,128)(2,1)} %pad_maximum_fusion.1), channel_id=1, source_target_pairs={{0,8},{8,0},{16,24},{24,16},{1,9},{9,1},{17,25},{25,17},{2,10},{10... | collective-permute-start | bytes 7864328 | tf_op jit(solution)/shard_map/ppermute | solution.py:438
  359.9 69.6 %collective-permute-start.31 = (f32[1,13312]{1,0:T(1,128)S(1)}, f32[1,13312]{1,0:T(1,128)S(1)}, u32[]{:S(2)}, u32[]{:S(2)}) collective-permute-start(f32[1,13312]{1,0:T(1,128)S(1)} %bitcast.308), channel_id=1, source_target_pairs={{0,2},{1,3},{2,0},{3,1},{4,6},{5,7},{6,4},{7,5},{8,10},{9,11},{10,... | collective-permute-start | bytes 159752 | tf_op jit(solution)/shard_map/ppermute | solution.py:441
  361.3 68.3 %collective-permute-start.32 = (f32[1,13312]{1,0:T(1,128)S(1)}, f32[1,13312]{1,0:T(1,128)S(1)}, u32[]{:S(2)}, u32[]{:S(2)}) collective-permute-start(f32[1,13312]{1,0:T(1,128)S(1)} %bitcast.309), channel_id=1, source_target_pairs={{0,4},{1,5},{2,6},{3,7},{4,0},{5,1},{6,2},{7,3},{8,12},{9,13},{10,... | collective-permute-start | bytes 159752 | tf_op jit(solution)/shard_map/ppermute | solution.py:441
  364.9 64.6 %collective-permute-start.33 = (f32[1,13312]{1,0:T(1,128)S(1)}, f32[1,13312]{1,0:T(1,128)S(1)}, u32[]{:S(2)}, u32[]{:S(2)}) collective-permute-start(f32[1,13312]{1,0:T(1,128)S(1)} %bitcast.310), channel_id=1, source_target_pairs={{0,6},{1,7},{2,4},{3,5},{4,2},{5,3},{6,0},{7,1},{8,14},{9,15},{10,... | collective-permute-start | bytes 159752 | tf_op jit(solution)/shard_map/ppermute | solution.py:441
  364.9 64.7 %collective-permute-start.30 = (bf16[8,160,1024]{2,1,0:T(8,128)(2,1)}, bf16[8,160,1024]{2,1,0:T(8,128)(2,1)}, u32[]{:S(2)}, u32[]{:S(2)}) collective-permute-start(bf16[8,160,1024]{2,1,0:T(8,128)(2,1)} %maximum_add_fusion.1), channel_id=1, source_target_pairs={{0,16},{8,24},{16,0},{24,8},{1,17},{9,25},{17,1},{25,9},{2,18},{10... | collective-permute-start | bytes 7864328 | tf_op jit(solution)/shard_map/ppermute | solution.py:438
  440.9 31.5 %collective-permute-start.34 = (bf16[336,1024]{1,0:T(8,128)(2,1)}, bf16[336,1024]{1,0:T(8,128)(2,1)}, u32[]{:S(2)}, u32[]{:S(2)}) collective-permute-start(bf16[336,1024]{1,0:T(8,128)(2,1)} %get-tuple-element.352), channel_id=1, source_target_pairs={{1,0},{0,2},{2,4},{4,6},{6,7},{7,5},{5,3},{3,1},{9,8},{8,10},{10,1... | collective-permute-start | bytes 2064392 | tf_op jit(solution)/shard_map/ppermute | solution.py:435
  448.0 36.1 %collective-permute-start.53 = (bf16[384,1024]{1,0:T(8,128)(2,1)}, bf16[384,1024]{1,0:T(8,128)(2,1)}, u32[]{:S(2)}, u32[]{:S(2)}) collective-permute-start(bf16[384,1024]{1,0:T(8,128)(2,1)} %get-tuple-element.349), channel_id=1, source_target_pairs={{0,8},{8,0},{16,24},{24,16},{1,9},{9,1},{17,25},{25,17},{2,10},{10... | collective-permute-start | bytes 2359304 | tf_op jit(solution)/shard_map/ppermute | solution.py:438
  474.0 37.5 %collective-permute-start.37 = (bf16[672,1024]{1,0:T(8,128)(2,1)S(1)}, bf16[672,1024]{1,0:T(8,128)(2,1)S(1)}, u32[]{:S(2)}, u32[]{:S(2)}) collective-permute-start(bf16[672,1024]{1,0:T(8,128)(2,1)S(1)} %pad_maximum_fusion.5), channel_id=1, source_target_pairs={{2,0},{4,2},{6,4},{7,6},{5,7},{3,5},{1,3},{0,1},{10,8},{12,10},{14... | collective-permute-start | bytes 4128776 | tf_op jit(solution)/shard_map/ppermute | solution.py:435
  477.3 34.2 %collective-permute-start.36 = (bf16[672,1024]{1,0:T(8,128)(2,1)S(1)}, bf16[672,1024]{1,0:T(8,128)(2,1)S(1)}, u32[]{:S(2)}, u32[]{:S(2)}) collective-permute-start(bf16[672,1024]{1,0:T(8,128)(2,1)S(1)} %pad_maximum_fusion.4), channel_id=1, source_target_pairs={{1,0},{0,2},{2,4},{4,6},{6,7},{7,5},{5,3},{3,1},{9,8},{8,10},{10,1... | collective-permute-start | bytes 4128776 | tf_op jit(solution)/shard_map/ppermute | solution.py:435
  557.5 31.9 %collective-permute-start.60 = (bf16[128,1024]{1,0:T(8,128)(2,1)S(1)}, bf16[128,1024]{1,0:T(8,128)(2,1)S(1)}, u32[]{:S(2)}, u32[]{:S(2)}) collective-permute-start(bf16[128,1024]{1,0:T(8,128)(2,1)S(1)} %fusion.54), channel_id=1, source_target_pairs={{0,16},{8,24},{16,0},{24,8},{1,17},{9,25},{17,1},{25,9},{2,18},{10... | collective-permute-start | bytes 786440 | tf_op jit(solution)/shard_map/ppermute | solution.py:438
  (144 other events, 1858.3 us)
Sparse Core Ops, SparseCore 0:
  11.5 110.3 all-gather.5
  125.5 84.5 all-gather.3
  367.0 97.0 reduce-scatter.1

commit v3 on v2

--- a/solution.py
+++ b/solution.py
@@ -14,6 +14,8 @@
 BACKWARD_BLOCK = (256, 512)
 EPS_NORM = 1e-06
 HIGH = lax.Precision.HIGHEST
+GELU_ROOT = (2.0 / 3.141592653589793) ** 0.5
+GELU_CUBE = 0.044715
 F32 = jnp.float32
 BF16 = jnp.bfloat16
 BIG_LEN = 2240
@@ -33,10 +35,6 @@
     mean_up = jnp.mean(upstream, -1, keepdims=True)
     mean_cross = jnp.mean(upstream * unit, -1, keepdims=True)
     return recip * (upstream - mean_up - unit * mean_cross)
-
-
-def gelu_tanh(values):
-    return jax.nn.gelu(values, approximate=True)
 
 
 def dot(left, right, left_dim, right_dim):
@@ -384,6 +382,206 @@
     )(lengths, scales, raw, query, key, keyt, value, lse, up)
 
 
+def mlp_kernel(
+    rows,
+    part_ref,
+    normed_ref,
+    up_ref,
+    first_ref,
+    second_ref,
+    bias_ref,
+    sent_one_ref,
+    kept_one_ref,
+    sent_two_ref,
+    kept_two_ref,
+    bias_grad_ref,
+    branch_ref,
+    grad_ref,
+):
+    part, step = pl.program_id(0), pl.program_id(1)
+    start = (part == 0) & (step == 0)
+    group = first_ref.shape[0]
+    normed, up = normed_ref[...], up_ref[...]
+    first = first_ref[:, :rows, :].reshape(group * rows, first_ref.shape[2])
+    second = second_ref[...]
+    pre = dot(normed, first, 1, 1) + bias_ref[...]
+    grad_hidden = dot(up, second, 1, 1)
+    square = pre * pre
+    angle = jnp.tanh(GELU_ROOT * pre * (1.0 + GELU_CUBE * square))
+    half = 0.5 * (1.0 + angle)
+    slope = half + 0.5 * pre * (1.0 - angle * angle) * GELU_ROOT * (1.0 + 3.0 * GELU_CUBE * square)
+    hidden = (pre * half).astype(BF16)
+    grad_pre = (slope * grad_hidden).astype(BF16)
+    bias_grad_ref[...] = jnp.sum(grad_pre.astype(F32), 0, keepdims=True)
+    branch = dot(hidden, second, 1, 0)
+    grad = dot(grad_pre, first, 1, 0)
+
+    @pl.when(start)
+    def _():
+        branch_ref[...] = branch
+        grad_ref[...] = grad
+
+    @pl.when(jnp.logical_not(start))
+    def _():
+        branch_ref[...] += branch
+        grad_ref[...] += grad
+
+    one = dot(grad_pre, normed, 0, 0).astype(BF16).reshape(kept_one_ref.shape)
+    two = dot(hidden, up, 0, 0).astype(BF16).reshape(kept_two_ref.shape)
+    sending = part < pl.num_programs(0) // 2
+
+    @pl.when(sending)
+    def _():
+        sent_one_ref[...] = one
+        sent_two_ref[...] = two
+
+    @pl.when(jnp.logical_not(sending))
+    def _():
+        kept_one_ref[...] = one
+        kept_two_ref[...] = two
+
+
+def mlp(parts, normed, up, first, second, bias, heads_all, rows):
+    local, width = normed.shape
+    total = parts.shape[0]
+    group = max(4, 128 // rows)
+    steps = heads_all // group
+    cols = group * rows
+    full_rows = first.shape[1]
+    half = total // 2
+
+    def fixed(p, j, part):
+        return (0, 0)
+
+    def sent(p, j, part):
+        flat = jnp.minimum(p * steps + j, half * steps - 1)
+        return (flat // steps, flat % steps, 0, 0)
+
+    def kept(p, j, part):
+        flat = jnp.maximum(p * steps + j - half * steps, 0)
+        return (flat // steps, flat % steps, 0, 0)
+
+    grads = jax.ShapeDtypeStruct((half, heads_all, rows, width), BF16)
+    return pl.pallas_call(
+        functools.partial(mlp_kernel, rows),
+        grid_spec=pltpu.PrefetchScalarGridSpec(
+            num_scalar_prefetch=1,
+            grid=(total, steps),
+            in_specs=[
+                pl.BlockSpec((local, width), fixed),
+                pl.BlockSpec((local, width), fixed),
+                pl.BlockSpec((group, full_rows, width), lambda p, j, part: (part[p] * steps + j, 0, 0)),
+                pl.BlockSpec((cols, width), lambda p, j, part: (part[p] * steps + j, 0)),
+                pl.BlockSpec((1, cols), lambda p, j, part: (0, part[p] * steps + j)),
+            ],
+            out_specs=[
+                pl.BlockSpec((1, group, rows, width), sent),
+                pl.BlockSpec((1, group, rows, width), kept),
+                pl.BlockSpec((1, group, rows, width), sent),
+                pl.BlockSpec((1, group, rows, width), kept),
+                pl.BlockSpec((1, cols), lambda p, j, part: (0, part[p] * steps + j)),
+                pl.BlockSpec((local, width), fixed),
+                pl.BlockSpec((local, width), fixed),
+            ],
+        ),
+        out_shape=[
+            grads,
+            grads,
+            grads,
+            grads,
+            jax.ShapeDtypeStruct((1, total * heads_all * rows), F32),
+            jax.ShapeDtypeStruct((local, width), F32),
+            jax.ShapeDtypeStruct((local, width), F32),
+        ],
+        compiler_params=pltpu.CompilerParams(
+            dimension_semantics=("arbitrary", "arbitrary"), vmem_limit_bytes=52 * 2**20
+        ),
+        cost_estimate=pl.CostEstimate(
+            flops=12 * local * width * total * heads_all * rows,
+            bytes_accessed=40 * 2**20,
+            transcendentals=0,
+        ),
+        name="mlp",
+    )(parts, normed, up, first, second, bias)
+
+
+def ring_blocks_kernel(
+    halves, place_ref, grad_ref, weight_ref, one_ref, two_ref, three_ref, four_ref, *out_refs
+):
+    terms = dot(grad_ref[...], weight_ref[...], 0, 0).astype(BF16)
+    rest = (one_ref[0].astype(F32) + two_ref[0].astype(F32)).astype(BF16)
+    last = (three_ref[0].astype(F32) + four_ref[0].astype(F32)).astype(BF16)
+    rest = jnp.concatenate([rest, last], 0)
+    local = terms.shape[0]
+    if halves:
+        half = out_refs[0].shape[0]
+        out_refs[0][...] = terms[:half]
+        out_refs[1][: local - half, :] = terms[half:]
+        out_refs[1][local - half :, :] = rest
+    else:
+        out_refs[0][0, :local, :] = terms
+        out_refs[0][0, local:, :] = rest
+
+
+def ring_blocks(places, grad, weight, pairs, local, halves):
+    depth, width = weight.shape
+    total = local + pairs[0].shape[1] + pairs[2].shape[1]
+    if halves:
+        sizes = [total // 2, total - total // 2]
+        out_specs = [pl.BlockSpec((size, width), lambda step, place: (0, 0)) for size in sizes]
+        out_shape = [jax.ShapeDtypeStruct((size, width), BF16) for size in sizes]
+    else:
+        out_specs = pl.BlockSpec((1, total, width), lambda step, place: (step, 0, 0))
+        out_shape = jax.ShapeDtypeStruct((places.shape[0], total, width), BF16)
+    return pl.pallas_call(
+        functools.partial(ring_blocks_kernel, halves),
+        grid_spec=pltpu.PrefetchScalarGridSpec(
+            num_scalar_prefetch=1,
+            grid=(places.shape[0],),
+            in_specs=[
+                pl.BlockSpec((depth, local), lambda step, place: (0, place[step])),
+                pl.BlockSpec((depth, width), lambda step, place: (0, 0)),
+            ]
+            + [
+                pl.BlockSpec((1, pair.shape[1], width), lambda step, place: (place[step], 0, 0))
+                for pair in pairs
+            ],
+            out_specs=out_specs,
+        ),
+        out_shape=out_shape,
+        compiler_params=pltpu.CompilerParams(vmem_limit_bytes=40 * 2**20),
+        cost_estimate=pl.CostEstimate(flops=1, bytes_accessed=1, transcendentals=0),
+        name="ring_blocks",
+    )(places, grad, weight, *pairs)
+
+
+def finish_kernel(rows, order_ref, value_ref, first_ref, second_ref):
+    value = value_ref[0].astype(F32)
+    first_ref[...] = jnp.transpose(value[:rows])
+    second_ref[...] = value[rows:]
+
+
+def finish_weights(order, value, rows):
+    total, full_rows, width = value.shape
+    return pl.pallas_call(
+        functools.partial(finish_kernel, rows),
+        grid_spec=pltpu.PrefetchScalarGridSpec(
+            num_scalar_prefetch=1,
+            grid=(total,),
+            in_specs=[pl.BlockSpec((1, full_rows, width), lambda step, order: (order[step], 0, 0))],
+            out_specs=[
+                pl.BlockSpec((width, rows), lambda step, order: (0, step)),
+                pl.BlockSpec((full_rows - rows, width), lambda step, order: (step, 0)),
+            ],
+        ),
+        out_shape=[
+            jax.ShapeDtypeStruct((width, total * rows), F32),
+            jax.ShapeDtypeStruct((total * (full_rows - rows), width), F32),
+        ],
+        name="finish_weights",
+    )(order, value)
+
+
 def after(value, *others):
     return lax.optimization_barrier((value, *others))[0]
 
@@ -459,10 +657,10 @@
     fc2_part = lax.dynamic_slice(fc2_weight, (data_me * hidden_part, 0), (hidden_part, width))
     first_full = lax.all_gather(
         jnp.concatenate([fc1_part, proj_part], 0), both_axes, axis=0, tiled=False
-    ).reshape(data_count, count, hidden_part + feat_part, width)
+    )
     fc2_full = lax.all_gather(fc2_part, both_axes, axis=0, tiled=True)
-    fc1_full = first_full[:, :, :hidden_part].reshape(-1, width)
-    proj_full = jnp.transpose(first_full[:, :, hidden_part:], (1, 0, 2, 3)).reshape(-1, width)
+    proj_full = first_full[:, hidden_part:].reshape(data_count, count, feat_part, width)
+    proj_full = jnp.transpose(proj_full, (1, 0, 2, 3)).reshape(-1, width)
 
     cond = jnp.take(class_table, class_ids, axis=0).astype(F32)
     act = jax.nn.silu(cond).astype(BF16)
@@ -514,6 +712,9 @@
                 (held[1], units[half_count - 1], units[1 - half_count])
             )
             held = [held[0], last] + list(held[2:])
+            proj_full, units[half_count - 1] = lax.optimization_barrier(
+                (proj_full, units[half_count - 1])
+            )
     half = local // 2
     ends = [
         rot(units[half_count - 1][:half], 1),
@@ -523,7 +724,6 @@
     units[half_count] = jnp.concatenate(ends, 0)
     held = put(held, half_count)
     raw, query, key, keyt, value, valuet, unit_all = held
-    query, fc1_full, proj_full = lax.optimization_barrier((query, fc1_full, proj_full))
     out_low, lse = attention_forward(query, key, valuet, lengths[0], heads)
 
     attended = jnp.zeros((feats * count, local), BF16)
@@ -533,18 +733,17 @@
         attended = lax.dynamic_update_slice(attended, piece, (at(away) * feats, 0))
     cot_full = cotangent[0].astype(F32)
     grad_mlp = (cot_full * gate_two).astype(BF16)
-    grad_hidden = dot(grad_mlp, fc2_full, 1, 1)
-    attended, grad_hidden = lax.optimization_barrier((attended, grad_hidden))
     attn_branch = dot(attended, proj_full, 0, 0) + proj_bias.astype(F32)
     resid = inputs_full + gate_one * attn_branch
     unit_two, recip_two = normalize(resid)
     normed_two = (unit_two * (1.0 + scale_two) + shift_two).astype(BF16)
-    pre_act = dot(normed_two, fc1_full, 1, 1) + bias_full
-    hidden_full, gelu_pull = jax.vjp(gelu_tanh, pre_act)
-    hidden = hidden_full.astype(BF16)
-
-    grad_pre = gelu_pull(grad_hidden)[0].astype(BF16)
-    grad_normed_two = dot(grad_pre, fc1_full, 1, 0)
+
+    kept_t = list(range(0, data_count, 2))
+    all_t = [t + 1 for t in kept_t] + kept_t
+    parts = jnp.bitwise_xor(data_me, jnp.array(all_t, jnp.int32))
+    sent_one, kept_one, sent_two, kept_two, fc1_bias_sum, mlp_branch, grad_normed_two = mlp(
+        parts, normed_two, grad_mlp, first_full, fc2_full, bias_full, count, hidden_part
+    )
     grad_shift_two = jnp.sum(grad_normed_two, 0)
     grad_scale_two = jnp.sum(grad_normed_two * unit_two, 0)
     grad_resid = cot_full + norm_back(unit_two, recip_two, grad_normed_two * (1.0 + scale_two))
@@ -556,61 +755,45 @@
         piece = lax.dynamic_slice(grad_attended, (at(away) * feats, 0), (feats, local))
         up_pieces[away] = piece if away == 0 else rot(piece, -away)
 
-    near = [away for away in offsets if away in (1, -1, 2)]
-    hidden_late, grad_pre_late, attended_late, arrived = lax.optimization_barrier(
-        (hidden, grad_pre, attended, [up_pieces[away] for away in near])
-    )
-    for away, piece in zip(near, arrived):
-        up_pieces[away] = piece
-    block_cols = count * hidden_part
-
-    def core_step(blocks):
-        return {
-            t: blocks(t).astype(F32) + swap(blocks(t ^ 1).astype(BF16), 1)
-            for t in range(0, data_count, 2)
-        }
-
-    def fc2_block(t):
-        part = jnp.bitwise_xor(data_me, t) * block_cols
-        cols = lax.dynamic_slice(hidden_late, (0, part), (local, block_cols))
-        return dot(cols, grad_mlp, 0, 0).reshape(count, hidden_part, width)
-
-    def fc1_block(t):
-        part = jnp.bitwise_xor(data_me, t) * block_cols
-        cols = lax.dynamic_slice(grad_pre_late, (0, part), (local, block_cols))
-        return dot(cols, normed_two, 0, 0).reshape(count, hidden_part, width)
-
-    fc2_kept = core_step(fc2_block)
-    fc2_stack = jnp.stack([fc2_kept[t].astype(BF16) for t in fc2_kept], 1)
-    fc2_stack = fc2_stack.reshape(count, len(fc2_kept) * hidden_part, width)
-
-    proj_grad = dot(attended_late, grad_attn, 1, 0).astype(BF16)
+    sent_one, sent_two = lax.optimization_barrier((sent_one, sent_two))
+    got_one, got_two = swap(sent_one, 1), swap(sent_two, 1)
+
+    def add(left, right):
+        return (left.astype(F32) + right.astype(F32)).astype(BF16)
+
+    def split_pair(kept):
+        kept = {t: kept[i] for i, t in enumerate(kept_t)}
+        for mask in data_masks[1:-1]:
+            kept = {
+                t: add(kept[t], swap(kept[t ^ mask], mask)) for t in kept if not t & mask
+            }
+        return kept[0], swap(kept[data_masks[-1]], data_masks[-1])
+
+    kept_one = [add(kept_one[i], got_one[i]) for i in range(len(kept_t))]
+    fc2_stack = jnp.stack([add(kept_two[i], got_two[i]) for i in range(len(kept_t))], 1)
+    fc2_stack = fc2_stack.reshape(count, len(kept_t) * hidden_part, width)
+    proj_grad = dot(attended, grad_attn, 1, 0).astype(BF16)
     proj_grad = proj_grad.reshape(count, data_count, feat_part, width)
-
-    def first_block(t):
-        part = lax.dynamic_index_in_dim(
-            proj_grad, jnp.bitwise_xor(data_me, t), 1, keepdims=False
-        )
-        return jnp.concatenate([fc1_block(t), part.astype(F32)], 1)
-
-    first_kept = core_step(first_block)
-
-    def fold(kept):
-        for mask in data_masks[1:]:
-            kept = {
-                t: kept[t] + swap(kept[t ^ mask].astype(BF16), mask)
-                for t in kept
-                if not t & mask
-            }
-        return kept[0]
+    proj_parts = [
+        lax.dynamic_index_in_dim(proj_grad, parts[i], 1, keepdims=False) for i in range(data_count)
+    ]
+    got_three = swap(jnp.stack(proj_parts[: len(kept_t)], 0), 1)
+    kept_three = [add(proj_parts[len(kept_t) + i], got_three[i]) for i in range(len(kept_t))]
+    mlp_branch = mlp_branch + fc2_bias.astype(F32)
+    block_output = (resid + gate_two * mlp_branch).astype(BF16)
+    grad_gate_two = jnp.sum(cot_full * mlp_branch, 0)
 
     up = jnp.zeros((feats, slots), BF16)
     for away in offsets:
         up = lax.dynamic_update_slice(up, up_pieces[away], (0, at(-away) * local))
-    up, first_kept, fc2_stack = lax.optimization_barrier((up, first_kept, fc2_stack))
+    up, kept_one, kept_three, fc2_stack = lax.optimization_barrier(
+        (up, kept_one, kept_three, fc2_stack)
+    )
     fc2_mine = lax.psum_scatter(fc2_stack, "head", scatter_dimension=0, tiled=True)
-    fc2_mine = fc2_mine.reshape(len(fc2_kept), hidden_part, width)
-    first_blocks = fold(first_kept).astype(BF16)
+    fc2_mine = fc2_mine.reshape(len(kept_t), hidden_part, width)
+
+    one_here, one_got = split_pair(kept_one)
+    three_here, three_got = split_pair(kept_three)
 
     def share(value):
         for mask in reversed(data_masks):
@@ -622,10 +805,9 @@
             jnp.array(table, jnp.int32),
             jnp.bitwise_xor(data_me, jnp.arange(data_count, dtype=jnp.int32)),
         )
-        return jnp.take(value, places, axis=0).astype(F32)
+        return value, places
 
     fc2_bias_sum = jnp.sum(grad_mlp.astype(F32), 0)
-    fc1_bias_sum = jnp.sum(grad_pre.astype(F32), 0)
     proj_bias_sum = jnp.sum(grad_attn.astype(F32), 0)
     valid = me * local + jnp.arange(local, dtype=jnp.int32) < jnp.sum(lengths[0])
     code_range = jnp.arange(CODES, dtype=jnp.int32)
@@ -642,6 +824,7 @@
             grad_gate_one,
             grad_shift_two,
             grad_scale_two,
+            grad_gate_two,
         ]
     )
     early, up = lax.optimization_barrier((early, up))
@@ -650,27 +833,31 @@
     grad_raw, query_sums = attention_backward(
         raw, query, key, keyt, value, lse, up, lengths[0], scale_exp, heads
     )
-    grad_raw, query_sums, first_blocks, early = lax.optimization_barrier(
-        (grad_raw, query_sums, first_blocks, early)
-    )
-
-    held_rows = local + first_blocks.shape[1]
-    half = held_rows // 2
-
-    def block(away, source):
-        piece = lax.dynamic_slice(source, (0, at(away) * local), (3 * feats, local))
-        terms = dot(piece, qkv_rows, 0, 0).astype(BF16)
-        weights = lax.dynamic_index_in_dim(first_blocks, at(away), 0, keepdims=False)
-        return jnp.concatenate([terms, weights], 0).astype(F32)
+    grad_raw, query_sums, one_got, three_got, early = lax.optimization_barrier(
+        (grad_raw, query_sums, one_got, three_got, early)
+    )
+    pairs = [one_here, one_got, three_here, three_got]
 
     def send(ups, downs):
-        return rot(ups.astype(BF16), -1), rot(downs.astype(BF16), 1)
-
-    far = block(half_count, grad_raw)
-    near_up, near_down = block(half_count - 1, grad_raw), block(1 - half_count, grad_raw)
-    got_up, got_down = send(far[:half], far[half:])
-
-    far_late, source = lax.optimization_barrier((far, grad_raw))
+        return rot(ups, -1), rot(downs, 1)
+
+    places = jnp.stack([at(away) for away in offsets]).astype(jnp.int32)
+    far_up, far_down = ring_blocks(places[-1:], grad_raw, qkv_rows, pairs, local, True)
+    got_up, got_down = send(far_up, far_down)
+    half = far_up.shape[0]
+
+    source, _ = lax.optimization_barrier((grad_raw, far_up))
+    blocks = ring_blocks(places[:-1], source, qkv_rows, pairs, local, False)
+
+    got_up, got_down, blocks, source = lax.optimization_barrier(
+        (got_up, got_down, blocks, source)
+    )
+    blocks = {away: blocks[i] for i, away in enumerate(offsets[:-1])}
+    near_up, near_down = blocks[half_count - 1], blocks[1 - half_count]
+    ups = jnp.concatenate([add(near_up[:half], got_up), near_up[half:]], 0)
+    downs = jnp.concatenate([near_down[:half], add(near_down[half:], got_down)], 0)
+    ups, downs, source = lax.optimization_barrier((ups, downs, source))
+    got_up, got_down = send(ups, downs)
     bias_sums = jnp.sum(source.astype(F32), 1)
     unit_grad = dot(source, unit_all, 1, 0)
     qkv_grad = unit_grad * (1.0 + scale_one) + bias_sums[:, None] * shift_one
@@ -679,68 +866,77 @@
     rows_float = qkv_rows.astype(F32)
     grad_shift_one = jnp.sum(rows_float * bias_sums[:, None], 0)
     grad_scale_one = jnp.sum(rows_float * unit_grad, 0)
-    mlp_branch = dot(after(hidden, far), fc2_full, 1, 0) + fc2_bias.astype(F32)
-    block_output = (resid + gate_two * mlp_branch).astype(BF16)
-    grad_gate_two = jnp.sum(cot_full * mlp_branch, 0)
-    late = jnp.concatenate([grad_shift_one, grad_scale_one, grad_gate_two])[None, :]
-
-    got_up, got_down, early, late, near_up, near_down = lax.optimization_barrier(
-        (got_up, got_down, early, late, near_up, near_down)
-    )
-    ups = jnp.concatenate([near_up[:half] + got_up, near_up[half:]], 0)
-    downs = jnp.concatenate([near_down[:half], near_down[half:] + got_down], 0)
-    got_up, got_down = send(ups, downs)
-    late = head_sum_far(late)
-    early = head_sum_near(early)
-    next_up, next_down = block(half_count - 2, source), block(2 - half_count, source)
+    late = head_sum_far(jnp.concatenate([grad_shift_one, grad_scale_one])[None, :])
+    over_rows = CODES + 2 * width + count * hidden_here
 
     for away in range(half_count - 2, 0, -1):
-        last = away == 1
-        got_up, got_down, late, early, next_up, next_down = lax.optimization_barrier(
-            (got_up, got_down, late, early, next_up, next_down)
+        got_up, got_down, late, qkv_grad = lax.optimization_barrier(
+            (got_up, got_down, late, qkv_grad)
         )
+        ups, downs = add(blocks[away], got_up), add(blocks[-away], got_down)
+        ups, downs, late, early, qkv_grad, fc2_mine = lax.optimization_barrier(
+            (ups, downs, late, early, qkv_grad, fc2_mine)
+        )
+        got_up, got_down = send(ups, downs)
         if away == half_count - 2:
-            got_up, got_down, fc2_mine = lax.optimization_barrier((got_up, got_down, fc2_mine))
-        got_up, got_down = send(next_up + got_up, next_down + got_down)
-        if away == half_count - 2:
-            late = head_sum_near(late)[0]
-            early = early[0]
-            over_rows = CODES + 2 * width + count * hidden_here
-            tail = jnp.concatenate([bias_sums, scale_sums, early[:over_rows]])[None, :]
-            mod_all = jnp.concatenate([late[: 2 * width], early[over_rows:], late[2 * width :]])
-            mod_rows = lax.dynamic_slice_in_dim(mod_all, me * mod_here, mod_here, 0)
-            mod_rows = jnp.concatenate([mod_rows, class_ids.astype(F32)])[None, :]
+            late = head_sum_near(jnp.concatenate([late, early], 1))
             for mask in data_masks:
-                mod_rows = jnp.concatenate([mod_rows, swap(mod_rows, mask)], 0)
-                qkv_grad = (qkv_grad.astype(F32) + swap(qkv_grad, mask)).astype(BF16)
-                tail = tail + swap(tail, mask)
-        next_up = block(away - 1, source)
-        next_down = None if last else block(1 - away, source)
-        if last:
-            next_down = jnp.zeros_like(next_up)
-
-    tail = tail[0]
-    mod_rows = jnp.take(
-        mod_rows, jnp.bitwise_xor(data_me, jnp.arange(data_count, dtype=jnp.int32)), axis=0
-    )
-    class_rows = mod_rows[:, mod_here].astype(jnp.int32)
-    mod_rows = mod_rows[:, :mod_here]
-    cond_terms = lax.dot_general(
-        mod_rows, ada_weight.astype(F32), (((1,), (1,)), ((), ())), precision=HIGH
-    )
-    cond_sums = head_sum_far(cond_terms)
-    got_up, got_down, cond_sums, next_up = lax.optimization_barrier(
-        (got_up, got_down, cond_sums, next_up)
-    )
-    ring_total = next_up + got_up.astype(F32) + got_down.astype(F32)
-    grad_normed_one, first_mine = ring_total[:local], ring_total[local:].astype(BF16)
-    cond_sums = head_sum_near(cond_sums)
+                qkv_grad = add(qkv_grad, swap(qkv_grad, mask))
+            fc2_pair = {t: fc2_mine[i].astype(F32) for i, t in enumerate(kept_t)}
+            for mask in data_masks[1:]:
+                fc2_pair = {
+                    t: fc2_pair[t] + swap(fc2_pair[t ^ mask].astype(BF16), mask).astype(F32)
+                    for t in fc2_pair
+                    if not t & mask
+                }
+            fc2_mine = fc2_pair[0].astype(BF16)
+        if away == 1:
+            sums = late[0]
+            mod_all = jnp.concatenate([sums[: 2 * width], sums[2 * width + over_rows :]])
+            rows = jnp.concatenate(
+                [
+                    lax.dynamic_slice_in_dim(mod_all, me * mod_here, mod_here, 0),
+                    class_ids.astype(F32),
+                    bias_sums,
+                    scale_sums,
+                    sums[2 * width : 2 * width + over_rows],
+                ]
+            )[None, :]
+            rows = jnp.concatenate(
+                [rows] + [swap(rows, mask) for mask in range(1, data_count)], 0
+            )
+            rows = jnp.take(
+                rows, jnp.bitwise_xor(data_me, jnp.arange(data_count, dtype=jnp.int32)), axis=0
+            )
+            class_rows = rows[:, mod_here].astype(jnp.int32)
+            mod_rows = rows[:, :mod_here]
+            tail = jnp.sum(rows[:, mod_here + 1 :], 0)
+            cond_terms = lax.dot_general(
+                mod_rows, ada_weight.astype(F32), (((1,), (1,)), ((), ())), precision=HIGH
+            )
+            cond_sums = head_sum_far(cond_terms)
+            fc2_all, order = share(fc2_mine)
+            fc2_weight_grad = jnp.take(fc2_all, order, axis=0).astype(F32).reshape(-1, width)
+
     qkv_weight_grad = (
         jnp.transpose(qkv_grad.reshape(3, heads, HD, width), (1, 0, 2, 3))
         .reshape(3 * feats, width)
         .astype(F32)
         .T
     )
+    cond_rows = jnp.take(class_table, class_rows, axis=0).astype(F32)
+    act_rows = jax.nn.silu(cond_rows).astype(BF16).astype(F32)
+    ada_weight_grad = lax.dot_general(
+        act_rows, mod_rows, (((0,), (0,)), ((), ())), precision=HIGH
+    )
+    ada_bias_grad = jnp.sum(mod_rows, 0)
+    got_up, got_down, tail, cond_sums, qkv_weight_grad, ada_weight_grad, fc2_weight_grad = (
+        lax.optimization_barrier(
+            (got_up, got_down, tail, cond_sums, qkv_weight_grad, ada_weight_grad, fc2_weight_grad)
+        )
+    )
+    ring_total = blocks[0].astype(F32) + got_up.astype(F32) + got_down.astype(F32)
+    grad_normed_one, first_mine = ring_total[:local], ring_total[local:].astype(BF16)
     bias_sums = tail[: 3 * feats].reshape(3, heads, HD)
     qv_bias_grad = jnp.stack([bias_sums[0], bias_sums[2]], 1).reshape(-1)
     qk_scale_grad = tail[3 * feats : 3 * feats + heads]
@@ -755,18 +951,8 @@
     input_grad = (
         grad_resid + norm_back(unit_one, recip_one, grad_normed_one * (1.0 + scale_one))
     ).astype(BF16)
-    fc2_mine = {t: fc2_mine[t // 2].astype(F32) for t in fc2_kept}
-    fc2_weight_grad = share(fold(fc2_mine).astype(BF16)).reshape(-1, width)
-    first_grad = share(first_mine)
-    fc1_weight_grad = first_grad[:, :hidden_part].reshape(-1, width).T
-    proj_weight_grad = first_grad[:, hidden_part:].reshape(-1, width)
-
-    cond_rows = jnp.take(class_table, class_rows, axis=0).astype(F32)
-    act_rows = jax.nn.silu(cond_rows).astype(BF16).astype(F32)
-    ada_weight_grad = lax.dot_general(
-        act_rows, mod_rows, (((0,), (0,)), ((), ())), precision=HIGH
-    )
-    ada_bias_grad = jnp.sum(mod_rows, 0)
+    first_grad, order = share(first_mine)
+    cond_sums = head_sum_near(cond_sums)
     _, silu_pull = jax.vjp(jax.nn.silu, cond_rows)
     grad_rows = silu_pull(cond_sums)[0]
     class_range = jnp.arange(class_table.shape[0], dtype=jnp.int32)
@@ -774,6 +960,13 @@
     for row in range(data_count):
         hit = class_range[:, None] == class_rows[row]
         class_table_grad = class_table_grad + jnp.where(hit, grad_rows[row][None, :], 0.0)
+    if hidden_part % 128 == 0:
+        fc1_weight_grad, proj_weight_grad = finish_weights(order, first_grad, hidden_part)
+    else:
+        first_grad = jnp.take(first_grad, order, axis=0).astype(F32)
+        fc1_weight_grad = first_grad[:, :hidden_part].reshape(-1, width).T
+        proj_weight_grad = first_grad[:, hidden_part:].reshape(-1, width)
+
     return (
         block_output[None],
         input_grad[None],

time: 657 us -> 621 us (0.945); the launches traced: 649 us -> 621 us
  Pallas kernels: 118 us -> 187 us
  matrix products: 79.3 us -> 18 us
  local copies, waits for them, and re-layouts: 88.4 us -> 59 us
  waiting for transfers between devices: 174 us -> 203 us
  other arithmetic: 85.9 us -> 62.5 us
  starting transfers between devices: 87.6 us -> 68.1 us
  between operations: 16.6 us -> 23.8 us
    ppermute x16 -> x15, waiting for transfers between devices: 35.1 us -> 113 us  [xor_head(): return lax.ppermute(value, 'head', [(i, i ^ mask) for i in range(count)])]
    dot_general x24 -> x4, matrix products: 74.5 us -> 13.2 us  [dot(): lax.dot_general(left, right, (((left_dim,), (right_dim,)), ((), ())), pre...]
    pallas_call x0 -> x4, Pallas kernels: none -> 59.4 us  [the longest x1 42.6 us: mlp(): pl.pallas_call(functools.partial(mlp_kernel, rows), grid_spec=pltpu.Prefe...]
    ppermute x30, waiting for transfers between devices: 122 us -> 89.9 us  [rot(): return lax.ppermute(value, 'head', pairs)]
    ppermute x16 -> x15, starting transfers between devices: 31.5 us -> 15.3 us  [swap(): return lax.ppermute(value, 'dp', [(i, i ^ mask) for i in range(data_count)])]
    ppermute x16 -> x15, waiting for transfers between devices: 13.6 us -> 0.04 us  [swap(): return lax.ppermute(value, 'dp', [(i, i ^ mask) for i in range(data_count)])]
    dot_general x5 -> x0, local copies, waits for them, and re-layouts: 9.95 us -> none  [dot(): lax.dot_general(left, right, (((left_dim,), (right_dim,)), ((), ())), pre...]
    convert_element_type x20 -> x12, other arithmetic: 32 us -> 22.5 us  [the longest x8 19.7 us: add(): return (left.astype(F32) + right.astype(F32)).astype(BF16)]
  transfers between devices with their start and end apart: 65 -> 63, of which waited for: 15 -> 23; matrix products, arithmetic and copies ran while one was open for 29% -> 16% of each run, Pallas kernels for 18% -> 22%
where the time goes in v3:
time: 621 us
  waiting for transfers between devices  203 us (33%)
  Pallas kernels  187 us (30%)
  starting transfers between devices  68.1 us (11%)
  other arithmetic  62.5 us (10%)
  local copies, waits for them, and re-layouts  59 us (10%)
  between operations  23.8 us (4%)
  matrix products  18 us (3%)
    ppermute x15, waiting for transfers between devices, xor_head(): return lax.ppermute(value, 'head', [(i, i ^ mask) for i in range(count)])  113 us
    ppermute x30, waiting for transfers between devices, rot(): return lax.ppermute(value, 'head', pairs)  89.9 us
    pallas_call x1, Pallas kernels, attention_backward(): pl.pallas_call(functools.partial(backward_kernel, heads, rows_k), grid_sp...  69 us
    pallas_call x1, Pallas kernels, mlp(): pl.pallas_call(functools.partial(mlp_kernel, rows), grid_spec=pltpu.Prefe...  42.6 us
    ppermute x30, starting transfers between devices, rot(): return lax.ppermute(value, 'head', pairs)  33.6 us
    pallas_call x1, Pallas kernels, attention_forward(): pl.pallas_call(functools.partial(forward_kernel, heads, rows_k), grid_spe...  33.2 us
    unnamed x146, local copies, waits for them, and re-layouts  29.2 us
    pallas_call x8, Pallas kernels, project(): pl.pallas_call(functools.partial(project_kernel, heads), grid_spec=pltpu....  24.9 us
  transfers between devices with their start and end apart: 63, of which 23 were waited for; matrix products, arithmetic and copies ran while one was open for 16% of the time, Pallas kernels for 22%

profile of v3, /device:TPU:1, one launch (start us, length us, event | category | flops | bytes accessed | tf_op | source)
XLA Modules:
  0.0 621.1 jit_solution(9749330287452561588)
XLA Ops:
  21.6 24.2 %collective-permute-done.2 = f32[1,1280]{1,0:T(1,128)S(1)} collective-permute-done((f32[1,1280]{1,0:T(1,128)S(1)}, f32[1,1280]{1,0:T(1,128)S(1)}, u32[]{:S(2)}, u32[]{:S(2)}) %collective-permute-start.2) | collective-permute-done | bytes 5152 | tf_op jit(solution)/shard_map/ppermute | solution.py:639
  51.5 19.5 %collective-permute-done.7 = f32[4,1280]{1,0:T(4,128)S(1)} collective-permute-done((f32[4,1280]{1,0:T(4,128)S(1)}, f32[4,1280]{1,0:T(4,128)S(1)}, u32[]{:S(2)}, u32[]{:S(2)}) %collective-permute-start.7) | collective-permute-done | bytes 20512 | tf_op jit(solution)/shard_map/ppermute | solution.py:639
  71.1 17.1 %collective-permute-done.5.piece_ref = bf16[512,1024]{1,0:T(8,128)(2,1)} collective-permute-done((bf16[512,1024]{1,0:T(8,128)(2,1)}, bf16[512,1024]{1,0:T(8,128)(2,1)}, u32[]{:S(2)}, u32[]{:S(2)}) %collective-permute-start.5) | collective-permute-done | bytes 1048608 | tf_op jit(solution)/shard_map/ppermute | solution.py:633
  111.7 3.6 project.10
  121.8 12.1 %collective-permute-done.8.piece_ref = bf16[512,1024]{1,0:T(8,128)(2,1)} collective-permute-done((bf16[512,1024]{1,0:T(8,128)(2,1)}, bf16[512,1024]{1,0:T(8,128)(2,1)}, u32[]{:S(2)}, u32[]{:S(2)}) %collective-permute-start.8) | collective-permute-done | bytes 1048608 | tf_op jit(solution)/shard_map/ppermute | solution.py:633
  165.2 33.2 %attend.1 = (bf16[128,4096]{1,0:T(8,128)(2,1)S(1)}, f32[2,4096]{1,0:T(2,128)S(1)}) custom-call(s32[3]{0:T(128)S(1)} %bitcast.222, bf16[128,4096]{1,0:T(8,128)(2,1)S(1)} %get-tuple-element.215.query_ref, bf16[4096,128]{1,0:T(8,128)(2,1)S(1)} %get-tuple-element.216.key_ref, bf16[128,4096]{1,0:T(8,128)(2,1)S(1)} %get-tuple-element.217.valuet_ref), custom_call_target="tpu_custom_call" | custom-call | flops 33554432000 | bytes 4194304 | tf_op jit(solution)/shard_map/attend/pallas_call | solution.py:324
  211.8 7.8 %collective-permute-done.14 = bf16[128,512]{1,0:T(8,128)(2,1)S(1)} collective-permute-done((bf16[128,512]{1,0:T(8,128)(2,1)S(1)}, bf16[128,512]{1,0:T(8,128)(2,1)S(1)}, u32[]{:S(2)}, u32[]{:S(2)}) %collective-permute-start.14) | collective-permute-done | bytes 131104 | tf_op jit(solution)/shard_map/ppermute | solution.py:633
  223.5 10.9 %collective-permute-done.17 = bf16[128,512]{1,0:T(8,128)(2,1)S(1)} collective-permute-done((bf16[128,512]{1,0:T(8,128)(2,1)S(1)}, bf16[128,512]{1,0:T(8,128)(2,1)S(1)}, u32[]{:S(2)}, u32[]{:S(2)}) %collective-permute-start.17) | collective-permute-done | bytes 131104 | tf_op jit(solution)/shard_map/ppermute | solution.py:633
  238.9 42.6 %mlp.1 = (bf16[2,8,128,1024]{3,2,1,0:T(8,128)(2,1)}, bf16[2,8,128,1024]{3,2,1,0:T(8,128)(2,1)}, bf16[2,8,128,1024]{3,2,1,0:T(8,128)(2,1)}, bf16[2,8,128,1024]{3,...) custom-call(s32[4]{0:T(128)S(1)} %broadcast_xor_fusion.part_ref, ...), custom_call_target="tpu_custom_call" | custom-call | flops 25769803776 | bytes 41943040 | tf_op jit(solution)/shard_map/mlp/pallas_call | solution.py:465
  285.3 4.1 fusion.20
  303.4 4.6 collective-permute-done.21
  313.4 6.9 %collective-permute-done.23 = bf16[128,512]{1,0:T(8,128)(2,1)S(1)} collective-permute-done((bf16[128,512]{1,0:T(8,128)(2,1)S(1)}, bf16[128,512]{1,0:T(8,128)(2,1)S(1)}, u32[]{:S(2)}, u32[]{:S(2)}) %collective-permute-start.23) | collective-permute-done | bytes 131104 | tf_op jit(solution)/shard_map/ppermute | solution.py:633
  320.3 6.5 %collective-permute-done.25 = bf16[128,512]{1,0:T(8,128)(2,1)S(1)} collective-permute-done((bf16[128,512]{1,0:T(8,128)(2,1)S(1)}, bf16[128,512]{1,0:T(8,128)(2,1)S(1)}, u32[]{:S(2)}, u32[]{:S(2)}) %collective-permute-start.25) | collective-permute-done | bytes 131104 | tf_op jit(solution)/shard_map/ppermute | solution.py:633
  342.7 69.0 %attend_back.1 = (bf16[384,4096]{1,0:T(8,128)(2,1)}, f32[2,4096]{1,0:T(2,128)}) custom-call(s32[3]{0:T(128)} %bitcast.221, f32[2]{0:T(128)} %copy-done.24, f32[384,4096]{1,0:T(8,128)} %copy-done.3, bf16[128,4096]{1,0:T(8,128)(2,1)} %copy-done.4, bf16[4096,128]{1,0:T(8,128)(2,1)} %copy-done.7, bf16[128,4096]{1,0:T(8,128)(2,1)} %copy-done.10, ...), custom_call_target="tpu_custom_call" | custom-call | flops 67108864000 | bytes 14680064 | tf_op jit(solution)/shard_map/attend_back/pallas_call | solution.py:349
  424.0 9.6 %ring_blocks.3 = bf16[7,672,1024]{2,1,0:T(8,128)(2,1)} custom-call(s32[7]{0:T(128)S(1)} %stack.84.place_ref, bf16[384,4096]{1,0:T(8,128)(2,1)S(1)} %copy-done.17, bf16[384,1024]{1,0:T(8,128)(2,1)S(1)} %bitcast.218, bf16[8,128,1024]{2,1,0:T(8,128)(2,1)S(1)} %copy-done.19, bf16[8,128,1024]{2,1,0:T(8,128)(2,1)} %collective-permute-done.29.two_ref, ...), custom_call_target="tpu_custom_call" | custom-call | flops 1 | bytes 1 | tf_op jit(solution)/shard_map/ring_blocks/pallas_call | solution.py:536
  433.6 12.5 %collective-permute-done.34 = bf16[336,1024]{1,0:T(8,128)(2,1)} collective-permute-done((bf16[336,1024]{1,0:T(8,128)(2,1)}, bf16[336,1024]{1,0:T(8,128)(2,1)}, u32[]{:S(2)}, u32[]{:S(2)}) %collective-permute-start.34) | collective-permute-done | bytes 688160 | tf_op jit(solution)/shard_map/ppermute | solution.py:633
  456.8 7.9 %add_convert_fusion.8 = (bf16[384,1024]{1,0:T(8,128)(2,1)S(1)}, f32[1024]{0:T(1024)S(1)}) fusion(f32[1024]{0:T(1024)S(1)} %bitcast.272, f32[384]{0:T(512)S(1)} %convert_reduce_fusion.1, f32[1024]{0:T(1024)S(1)} %bitcast.256, bf16[3,2,64,1024]{3,2,1,0:T(8,128)(2,1)S(1)} %copy.157, bf16[384,4096]{1,0:T(8,128)(2,1)} %get-tuple-element.255.grad_ref, ...), kind=kOutput, calls=%fused_computation.65 | convolution fusion | flops 3223976960 | bytes 13121024 | tf_op jit(solution)/shard_map/dot_general | solution.py:41
  468.5 19.7 %collective-permute-done.38 = f32[1,2048]{1,0:T(1,128)S(1)} collective-permute-done((f32[1,2048]{1,0:T(1,128)S(1)}, f32[1,2048]{1,0:T(1,128)S(1)}, u32[]{:S(2)}, u32[]{:S(2)}) %collective-permute-start.38) | collective-permute-done | bytes 8224 | tf_op jit(solution)/shard_map/ppermute | solution.py:639
  489.1 5.5 fusion.2
  501.0 30.9 %collective-permute-done.43 = f32[1,16384]{1,0:T(1,128)S(1)} collective-permute-done((f32[1,16384]{1,0:T(1,128)S(1)}, f32[1,16384]{1,0:T(1,128)S(1)}, u32[]{:S(2)}, u32[]{:S(2)}) %collective-permute-start.43) | collective-permute-done | bytes 65568 | tf_op jit(solution)/shard_map/ppermute | solution.py:639
  532.3 4.6 fusion.1
  559.0 14.9 %collective-permute-done.52 = f32[4,1024]{1,0:T(4,128)S(1)} collective-permute-done((f32[4,1024]{1,0:T(4,128)S(1)}, f32[4,1024]{1,0:T(4,128)S(1)}, u32[]{:S(2)}, u32[]{:S(2)}) %collective-permute-start.52) | collective-permute-done | bytes 16416 | tf_op jit(solution)/shard_map/ppermute | solution.py:639
  597.3 3.9 fusion.32
  609.8 4.5 finish_weights.1
  (440 shorter events, 221.1 us)
Async XLA Ops:
  7.2 129.4 %all-gather.6.cloned.1.call-start = ((), (), s32[]{:S(2)}) async-start(), calls=%async_computation.3 | async-start | bytes 10813440 | tf_op jit(solution)/shard_map/all_gather | solution.py:658
  10.2 228.7 %all-gather.4.cloned.1.call-start = ((), (), s32[]{:S(2)}) async-start(), calls=%async_computation.1 | async-start | bytes 8650752 | tf_op jit(solution)/shard_map/all_gather | solution.py:661
  11.9 482.7 %reduce-scatter.2.cloned.1.call-start = ((), (), s32[]{:S(2)}) async-start(), calls=%async_computation.2 | async-start | bytes 4718592 | tf_op jit(solution)/shard_map/reduce_scatter | solution.py:792
  13.6 34.0 %collective-permute-start = (bf16[512,1024]{1,0:T(8,128)(2,1)S(1)}, bf16[512,1024]{1,0:T(8,128)(2,1)}, u32[]{:S(2)}, u32[]{:S(2)}) collective-permute-start(bf16[512,1024]{1,0:T(8,128)(2,1)S(1)} %fusion.12.piece_ref), channel_id=1, source_target_pairs={{2,0},{4,2},{6,4},{7,6},{5,7},{3,5},{1,3},{0,1},{10,8},{12,10},{14... | collective-permute-start | bytes 3145736 | tf_op jit(solution)/shard_map/ppermute | solution.py:633
  15.7 31.8 %collective-permute-start.1 = (bf16[512,1024]{1,0:T(8,128)(2,1)S(1)}, bf16[512,1024]{1,0:T(8,128)(2,1)}, u32[]{:S(2)}, u32[]{:S(2)}) collective-permute-start(bf16[512,1024]{1,0:T(8,128)(2,1)S(1)} %fusion.12.piece_ref), channel_id=1, source_target_pairs={{1,0},{0,2},{2,4},{4,6},{6,7},{7,5},{5,3},{3,1},{9,8},{8,10},{10,1... | collective-permute-start | bytes 3145736 | tf_op jit(solution)/shard_map/ppermute | solution.py:633
  47.5 40.6 %collective-permute-start.5 = (bf16[512,1024]{1,0:T(8,128)(2,1)}, bf16[512,1024]{1,0:T(8,128)(2,1)}, u32[]{:S(2)}, u32[]{:S(2)}) collective-permute-start(bf16[512,1024]{1,0:T(8,128)(2,1)} %collective-permute-done.piece_ref), channel_id=1, source_target_pairs={{2,0},{4,2},{6,4},{7,6},{5,7},{3,5},{1,3},{0,1},{10,8},{12,10},{14... | collective-permute-start | bytes 3145736 | tf_op jit(solution)/shard_map/ppermute | solution.py:633
  49.8 38.3 %collective-permute-start.6 = (bf16[512,1024]{1,0:T(8,128)(2,1)}, bf16[512,1024]{1,0:T(8,128)(2,1)}, u32[]{:S(2)}, u32[]{:S(2)}) collective-permute-start(bf16[512,1024]{1,0:T(8,128)(2,1)} %collective-permute-done.1.piece_ref), channel_id=1, source_target_pairs={{1,0},{0,2},{2,4},{4,6},{6,7},{7,5},{5,3},{3,1},{9,8},{8,10},{10,1... | collective-permute-start | bytes 3145736 | tf_op jit(solution)/shard_map/ppermute | solution.py:633
  88.2 45.8 %collective-permute-start.8 = (bf16[512,1024]{1,0:T(8,128)(2,1)}, bf16[512,1024]{1,0:T(8,128)(2,1)}, u32[]{:S(2)}, u32[]{:S(2)}) collective-permute-start(bf16[512,1024]{1,0:T(8,128)(2,1)} %collective-permute-done.5.piece_ref), channel_id=1, source_target_pairs={{2,0},{4,2},{6,4},{7,6},{5,7},{3,5},{1,3},{0,1},{10,8},{12,10},{14... | collective-permute-start | bytes 3145736 | tf_op jit(solution)/shard_map/ppermute | solution.py:633
  90.5 43.4 %collective-permute-start.9 = (bf16[512,1024]{1,0:T(8,128)(2,1)}, bf16[512,1024]{1,0:T(8,128)(2,1)}, u32[]{:S(2)}, u32[]{:S(2)}) collective-permute-start(bf16[512,1024]{1,0:T(8,128)(2,1)} %collective-permute-done.6.piece_ref), channel_id=1, source_target_pairs={{1,0},{0,2},{2,4},{4,6},{6,7},{7,5},{5,3},{3,1},{9,8},{8,10},{10,1... | collective-permute-start | bytes 3145736 | tf_op jit(solution)/shard_map/ppermute | solution.py:633
  281.5 46.6 %collective-permute-start.28 = (bf16[2,8,128,1024]{3,2,1,0:T(8,128)(2,1)}, bf16[2,8,128,1024]{3,2,1,0:T(8,128)(2,1)S(1)}, u32[]{:S(2)}, u32[]{:S(2)}) collective-permute-start(bf16[2,8,128,1024]{3,2,1,0:T(8,128)(2,1)} %get-tuple-element.233), channel_id=1, source_target_pairs={{0,8},{8,0},{16,24},{24,16},{1,9},{9,1},{17,25},{25,17},{2,10},{10... | collective-permute-start | bytes 12582920 | tf_op jit(solution)/shard_map/ppermute | solution.py:636
  282.6 50.5 %collective-permute-start.26 = (bf16[2,8,128,1024]{3,2,1,0:T(8,128)(2,1)}, bf16[2,8,128,1024]{3,2,1,0:T(8,128)(2,1)S(1)}, u32[]{:S(2)}, u32[]{:S(2)}) collective-permute-start(bf16[2,8,128,1024]{3,2,1,0:T(8,128)(2,1)} %get-tuple-element.231), channel_id=1, source_target_pairs={{0,8},{8,0},{16,24},{24,16},{1,9},{9,1},{17,25},{25,17},{2,10},{10... | collective-permute-start | bytes 12582920 | tf_op jit(solution)/shard_map/ppermute | solution.py:636
  292.8 34.0 %collective-permute-start.27 = (bf16[2,8,32,1024]{3,2,1,0:T(8,128)(2,1)S(1)}, bf16[2,8,32,1024]{3,2,1,0:T(8,128)(2,1)S(1)}, u32[]{:S(2)}, u32[]{:S(2)}) collective-permute-start(bf16[2,8,32,1024]{3,2,1,0:T(8,128)(2,1)S(1)} %pad_maximum_fusion.5), channel_id=1, source_target_pairs={{0,8},{8,0},{16,24},{24,16},{1,9},{9,1},{17,25},{25,17},{2,10},{10... | collective-permute-start | bytes 3145736 | tf_op jit(solution)/shard_map/ppermute | solution.py:636
  337.6 74.0 %collective-permute-start.31 = (f32[1,14336]{1,0:T(1,128)S(1)}, f32[1,14336]{1,0:T(1,128)S(1)}, u32[]{:S(2)}, u32[]{:S(2)}) collective-permute-start(f32[1,14336]{1,0:T(1,128)S(1)} %bitcast.245), channel_id=1, source_target_pairs={{0,2},{1,3},{2,0},{3,1},{4,6},{5,7},{6,4},{7,5},{8,10},{9,11},{10,... | collective-permute-start | bytes 172040 | tf_op jit(solution)/shard_map/ppermute | solution.py:639
  337.6 74.1 %collective-permute-start.32 = (f32[1,14336]{1,0:T(1,128)S(1)}, f32[1,14336]{1,0:T(1,128)}, u32[]{:S(2)}, u32[]{:S(2)}) collective-permute-start(f32[1,14336]{1,0:T(1,128)S(1)} %bitcast.246), channel_id=1, source_target_pairs={{0,4},{1,5},{2,6},{3,7},{4,0},{5,1},{6,2},{7,3},{8,12},{9,13},{10,... | collective-permute-start | bytes 172040 | tf_op jit(solution)/shard_map/ppermute | solution.py:639
  339.2 73.1 %collective-permute-start.33 = (f32[1,14336]{1,0:T(1,128)S(1)}, f32[1,14336]{1,0:T(1,128)}, u32[]{:S(2)}, u32[]{:S(2)}) collective-permute-start(f32[1,14336]{1,0:T(1,128)S(1)} %bitcast.247), channel_id=1, source_target_pairs={{0,6},{1,7},{2,4},{3,5},{4,2},{5,3},{6,0},{7,1},{8,14},{9,15},{10,... | collective-permute-start | bytes 172040 | tf_op jit(solution)/shard_map/ppermute | solution.py:639
  341.2 72.1 %collective-permute-start.29 = (bf16[8,128,1024]{2,1,0:T(8,128)(2,1)}, bf16[8,128,1024]{2,1,0:T(8,128)(2,1)}, u32[]{:S(2)}, u32[]{:S(2)}) collective-permute-start(bf16[8,128,1024]{2,1,0:T(8,128)(2,1)} %get-tuple-element.238), channel_id=1, source_target_pairs={{0,16},{8,24},{16,0},{24,8},{1,17},{9,25},{17,1},{25,9},{2,18},{10... | collective-permute-start | bytes 6291464 | tf_op jit(solution)/shard_map/ppermute | solution.py:636
  341.4 71.8 %collective-permute-start.30 = (bf16[8,32,1024]{2,1,0:T(8,128)(2,1)}, bf16[8,32,1024]{2,1,0:T(8,128)(2,1)S(1)}, u32[]{:S(2)}, u32[]{:S(2)}) collective-permute-start(bf16[8,32,1024]{2,1,0:T(8,128)(2,1)} %get-tuple-element.239), channel_id=1, source_target_pairs={{0,16},{8,24},{16,0},{24,8},{1,17},{9,25},{17,1},{25,9},{2,18},{10... | collective-permute-start | bytes 1572872 | tf_op jit(solution)/shard_map/ppermute | solution.py:636
  454.7 34.4 %collective-permute-start.36 = (bf16[672,1024]{1,0:T(8,128)(2,1)}, bf16[672,1024]{1,0:T(8,128)(2,1)}, u32[]{:S(2)}, u32[]{:S(2)}) collective-permute-start(bf16[672,1024]{1,0:T(8,128)(2,1)} %pad_maximum_fusion.1), channel_id=1, source_target_pairs={{1,0},{0,2},{2,4},{4,6},{6,7},{7,5},{5,3},{3,1},{9,8},{8,10},{10,1... | collective-permute-start | bytes 4128776 | tf_op jit(solution)/shard_map/ppermute | solution.py:633
  455.9 33.1 %collective-permute-start.37 = (bf16[672,1024]{1,0:T(8,128)(2,1)}, bf16[672,1024]{1,0:T(8,128)(2,1)}, u32[]{:S(2)}, u32[]{:S(2)}) collective-permute-start(bf16[672,1024]{1,0:T(8,128)(2,1)} %pad_maximum_fusion.2), channel_id=1, source_target_pairs={{2,0},{4,2},{6,4},{7,6},{5,7},{3,5},{1,3},{0,1},{10,8},{12,10},{14... | collective-permute-start | bytes 4128776 | tf_op jit(solution)/shard_map/ppermute | solution.py:633
  497.5 34.4 %collective-permute-start.46 = (bf16[128,1024]{1,0:T(8,128)(2,1)S(1)}, bf16[128,1024]{1,0:T(8,128)(2,1)S(1)}, u32[]{:S(2)}, u32[]{:S(2)}) collective-permute-start(bf16[128,1024]{1,0:T(8,128)(2,1)S(1)} %slice_bitcast_fusion.4), channel_id=1, source_target_pairs={{0,16},{8,24},{16,0},{24,8},{1,17},{9,25},{17,1},{25,9},{2,18},{10... | collective-permute-start | bytes 786440 | tf_op jit(solution)/shard_map/ppermute | solution.py:636
  498.7 33.6 %collective-permute-start.41 = (bf16[672,1024]{1,0:T(8,128)(2,1)}, bf16[672,1024]{1,0:T(8,128)(2,1)S(1)}, u32[]{:S(2)}, u32[]{:S(2)}) collective-permute-start(bf16[672,1024]{1,0:T(8,128)(2,1)} %get-tuple-element.263), channel_id=1, source_target_pairs={{1,0},{0,2},{2,4},{4,6},{6,7},{7,5},{5,3},{3,1},{9,8},{8,10},{10,1... | collective-permute-start | bytes 4128776 | tf_op jit(solution)/shard_map/ppermute | solution.py:633
  499.1 33.3 %collective-permute-start.42 = (bf16[672,1024]{1,0:T(8,128)(2,1)}, bf16[672,1024]{1,0:T(8,128)(2,1)S(1)}, u32[]{:S(2)}, u32[]{:S(2)}) collective-permute-start(bf16[672,1024]{1,0:T(8,128)(2,1)} %get-tuple-element.264), channel_id=1, source_target_pairs={{2,0},{4,2},{6,4},{7,6},{5,7},{3,5},{1,3},{0,1},{10,8},{12,10},{14... | collective-permute-start | bytes 4128776 | tf_op jit(solution)/shard_map/ppermute | solution.py:633
  541.7 41.0 %collective-permute-start.47 = (bf16[672,1024]{1,0:T(8,128)(2,1)}, bf16[672,1024]{1,0:T(8,128)(2,1)}, u32[]{:S(2)}, u32[]{:S(2)}) collective-permute-start(bf16[672,1024]{1,0:T(8,128)(2,1)} %get-tuple-element.273), channel_id=1, source_target_pairs={{1,0},{0,2},{2,4},{4,6},{6,7},{7,5},{5,3},{3,1},{9,8},{8,10},{10,1... | collective-permute-start | bytes 4128776 | tf_op jit(solution)/shard_map/ppermute | solution.py:633
  541.7 41.0 %collective-permute-start.48 = (bf16[672,1024]{1,0:T(8,128)(2,1)}, bf16[672,1024]{1,0:T(8,128)(2,1)}, u32[]{:S(2)}, u32[]{:S(2)}) collective-permute-start(bf16[672,1024]{1,0:T(8,128)(2,1)} %get-tuple-element.274), channel_id=1, source_target_pairs={{2,0},{4,2},{6,4},{7,6},{5,7},{3,5},{1,3},{0,1},{10,8},{12,10},{14... | collective-permute-start | bytes 4128776 | tf_op jit(solution)/shard_map/ppermute | solution.py:633
  (107 other events, 1841.5 us)
Sparse Core Ops, SparseCore 0:
  11.5 117.6 all-gather.5
  132.8 100.5 all-gather.3
  342.8 103.0 reduce-scatter.1

commit v4 on v3

--- a/solution.py
+++ b/solution.py
@@ -16,6 +16,7 @@
 HIGH = lax.Precision.HIGHEST
 GELU_ROOT = (2.0 / 3.141592653589793) ** 0.5
 GELU_CUBE = 0.044715
+GAIN_LEAST = 0.25
 F32 = jnp.float32
 BF16 = jnp.bfloat16
 BIG_LEN = 2240
@@ -97,9 +98,12 @@
 ):
     width = heads * HD
     raw_ref, query_ref, key_ref, keyt_ref, value_ref, valuet_ref, unit_ref = refs[-7:]
-    piece = piece_ref[...]
-    unit_ref[...] = piece
-    normed = (piece.astype(F32) * (1.0 + mod_ref[1:2, :]) + mod_ref[0:1, :]).astype(BF16)
+    piece = piece_ref[...].astype(F32)
+    shift, gain = mod_ref[0:1, :], 1.0 + mod_ref[1:2, :]
+    sent_normed = jnp.abs(gain) >= GAIN_LEAST
+    inverse = 1.0 / jnp.where(sent_normed, gain, 1.0)
+    unit_ref[...] = jnp.where(sent_normed, (piece - shift) * inverse, piece).astype(BF16)
+    normed = jnp.where(sent_normed, piece, piece * gain + shift).astype(BF16)
     raw = dot(weight_ref[...], normed, 1, 1) + bias_ref[...]
     raw_ref[...] = raw
     for head in range(heads):
@@ -444,7 +448,7 @@
 def mlp(parts, normed, up, first, second, bias, heads_all, rows):
     local, width = normed.shape
     total = parts.shape[0]
-    group = max(4, 128 // rows)
+    group = max(8, 128 // rows)
     steps = heads_all // group
     cols = group * rows
     full_rows = first.shape[1]
@@ -549,10 +553,36 @@
             out_specs=out_specs,
         ),
         out_shape=out_shape,
-        compiler_params=pltpu.CompilerParams(vmem_limit_bytes=40 * 2**20),
+        compiler_params=pltpu.CompilerParams(vmem_limit_bytes=60 * 2**20),
         cost_estimate=pl.CostEstimate(flops=1, bytes_accessed=1, transcendentals=0),
         name="ring_blocks",
     )(places, grad, weight, *pairs)
+
+
+def add_half_kernel(index, lower, blocks_ref, got_ref, out_ref):
+    half = got_ref.shape[0]
+    block = blocks_ref[0]
+    part = slice(0, half) if lower else slice(block.shape[0] - half, block.shape[0])
+    rest = slice(half, block.shape[0]) if lower else slice(0, block.shape[0] - half)
+    out_ref[rest, :] = block[rest]
+    out_ref[part, :] = (block[part].astype(F32) + got_ref[...].astype(F32)).astype(BF16)
+
+
+def add_half(blocks, index, got, lower):
+    _, rows, width = blocks.shape
+    return pl.pallas_call(
+        functools.partial(add_half_kernel, index, lower),
+        grid=(1,),
+        in_specs=[
+            pl.BlockSpec((1, rows, width), lambda step: (index, 0, 0)),
+            pl.BlockSpec(got.shape, lambda step: (0, 0)),
+        ],
+        out_specs=pl.BlockSpec((rows, width), lambda step: (0, 0)),
+        out_shape=jax.ShapeDtypeStruct((rows, width), BF16),
+        compiler_params=pltpu.CompilerParams(vmem_limit_bytes=60 * 2**20),
+        cost_estimate=pl.CostEstimate(flops=1, bytes_accessed=1, transcendentals=0),
+        name="add_half",
+    )(blocks, got)
 
 
 def finish_kernel(rows, order_ref, value_ref, first_ref, second_ref):
@@ -649,7 +679,6 @@
 
     inputs_full = block_input[0].astype(F32)
     unit_one, recip_one = normalize(inputs_full)
-    unit_low = unit_one.astype(BF16)
 
     hidden_part, feat_part = hidden_here // data_count, feats // data_count
     fc1_part = lax.dynamic_slice(fc1_weight, (0, data_me * hidden_part), (width, hidden_part)).T
@@ -667,16 +696,8 @@
     mod_local = jnp.dot(act, ada_weight, preferred_element_type=F32)[0] + ada_bias.astype(F32)
     small = jnp.concatenate([mod_local, fc1_bias.astype(F32)])[None, :]
     pieces = [small] + [xor_head(small, mask) for mask in range(2, count, 2)]
-    units = {0: unit_low, 1: rot(unit_low, 1), -1: rot(unit_low, -1)}
-    units[1], units[-1], pieces = lax.optimization_barrier((units[1], units[-1], pieces))
     pieces = jnp.concatenate(pieces, 0)
-    if half_count > 2:
-        units[2], units[-2] = rot(units[1], 1), rot(units[-1], -1)
     small_all = jnp.stack([pieces, xor_head(pieces, 1)], 1).reshape(count, -1)
-    if half_count > 2:
-        units[2], units[-2], small_all = lax.optimization_barrier(
-            (units[2], units[-2], small_all)
-        )
     small_all = jnp.take(
         small_all, jnp.bitwise_xor(me, jnp.arange(count, dtype=jnp.int32)), axis=0
     )
@@ -685,6 +706,11 @@
     shift_one, scale_one, gate_one, shift_two, scale_two, gate_two = [
         modulation[i : i + 1] for i in range(6)
     ]
+    gain_one = 1.0 + scale_one
+    ring_low = jnp.where(
+        jnp.abs(gain_one) >= GAIN_LEAST, unit_one * gain_one + shift_one, unit_one
+    ).astype(BF16)
+    units = {0: ring_low, 1: rot(ring_low, 1), -1: rot(ring_low, -1)}
     bias_full = small_all[:, mod_here:].reshape(count, data_count, hidden_part)
     bias_full = jnp.transpose(bias_full, (1, 0, 2)).reshape(1, -1)
 
@@ -702,7 +728,7 @@
             place, units[away], qkv_rows, modulation[:2], qkv_bias, scale_exp, held, heads, slots
         )
 
-    for away in range(3, half_count):
+    for away in range(2, half_count):
         units[away], units[-away] = rot(units[away - 1], 1), rot(units[1 - away], -1)
     held = put([], 0)
     for away in range(1, half_count - 1):
@@ -784,19 +810,22 @@
     grad_gate_two = jnp.sum(cot_full * mlp_branch, 0)
 
     up = jnp.zeros((feats, slots), BF16)
-    for away in offsets:
+    for away in offsets[:5]:
         up = lax.dynamic_update_slice(up, up_pieces[away], (0, at(-away) * local))
     up, kept_one, kept_three, fc2_stack = lax.optimization_barrier(
         (up, kept_one, kept_three, fc2_stack)
     )
+    for away in offsets[5:]:
+        up = lax.dynamic_update_slice(up, up_pieces[away], (0, at(-away) * local))
     fc2_mine = lax.psum_scatter(fc2_stack, "head", scatter_dimension=0, tiled=True)
     fc2_mine = fc2_mine.reshape(len(kept_t), hidden_part, width)
 
     one_here, one_got = split_pair(kept_one)
     three_here, three_got = split_pair(kept_three)
 
-    def share(value):
-        for mask in reversed(data_masks):
+    def share(value, hop):
+        value = jnp.stack([value, hop], 0)
+        for mask in reversed(data_masks[:-1]):
             value = jnp.stack([value, swap(value, mask)], 0)
         bits = len(data_masks)
         value = value.reshape((data_count,) + value.shape[bits:])
@@ -852,10 +881,9 @@
     got_up, got_down, blocks, source = lax.optimization_barrier(
         (got_up, got_down, blocks, source)
     )
+    ups = add_half(blocks, offsets.index(half_count - 1), got_up, True)
+    downs = add_half(blocks, offsets.index(1 - half_count), got_down, False)
     blocks = {away: blocks[i] for i, away in enumerate(offsets[:-1])}
-    near_up, near_down = blocks[half_count - 1], blocks[1 - half_count]
-    ups = jnp.concatenate([add(near_up[:half], got_up), near_up[half:]], 0)
-    downs = jnp.concatenate([near_down[:half], add(near_down[half:], got_down)], 0)
     ups, downs, source = lax.optimization_barrier((ups, downs, source))
     got_up, got_down = send(ups, downs)
     bias_sums = jnp.sum(source.astype(F32), 1)
@@ -882,14 +910,15 @@
             late = head_sum_near(jnp.concatenate([late, early], 1))
             for mask in data_masks:
                 qkv_grad = add(qkv_grad, swap(qkv_grad, mask))
-            fc2_pair = {t: fc2_mine[i].astype(F32) for i, t in enumerate(kept_t)}
             for mask in data_masks[1:]:
-                fc2_pair = {
-                    t: fc2_pair[t] + swap(fc2_pair[t ^ mask].astype(BF16), mask).astype(F32)
-                    for t in fc2_pair
-                    if not t & mask
-                }
-            fc2_mine = fc2_pair[0].astype(BF16)
+                got = swap(fc2_mine, mask)
+                fc2_mine = jnp.stack(
+                    [add(fc2_mine[i], got[kept_t.index(t ^ mask)]) for i, t in enumerate(kept_t)], 0
+                )
+            fc2_all = jnp.concatenate([fc2_mine, swap(fc2_mine, 1)], 0)
+            fc2_order = jnp.bitwise_xor(data_me, jnp.arange(data_count, dtype=jnp.int32))
+            fc2_order = fc2_order // 2 + (fc2_order % 2) * len(kept_t)
+            fc2_mine = jnp.take(fc2_all, fc2_order, axis=0).astype(F32).reshape(-1, width)
         if away == 1:
             sums = late[0]
             mod_all = jnp.concatenate([sums[: 2 * width], sums[2 * width + over_rows :]])
@@ -915,8 +944,6 @@
                 mod_rows, ada_weight.astype(F32), (((1,), (1,)), ((), ())), precision=HIGH
             )
             cond_sums = head_sum_far(cond_terms)
-            fc2_all, order = share(fc2_mine)
-            fc2_weight_grad = jnp.take(fc2_all, order, axis=0).astype(F32).reshape(-1, width)
 
     qkv_weight_grad = (
         jnp.transpose(qkv_grad.reshape(3, heads, HD, width), (1, 0, 2, 3))
@@ -932,11 +959,13 @@
     ada_bias_grad = jnp.sum(mod_rows, 0)
     got_up, got_down, tail, cond_sums, qkv_weight_grad, ada_weight_grad, fc2_weight_grad = (
         lax.optimization_barrier(
-            (got_up, got_down, tail, cond_sums, qkv_weight_grad, ada_weight_grad, fc2_weight_grad)
+            (got_up, got_down, tail, cond_sums, qkv_weight_grad, ada_weight_grad, fc2_mine)
         )
     )
     ring_total = blocks[0].astype(F32) + got_up.astype(F32) + got_down.astype(F32)
-    grad_normed_one, first_mine = ring_total[:local], ring_total[local:].astype(BF16)
+    grad_normed_one = ring_total[:local]
+    first_mine = [value[local:].astype(F32) for value in (blocks[0], got_up, got_down)]
+    first_mine = (first_mine[0] + first_mine[1] + first_mine[2]).astype(BF16)
     bias_sums = tail[: 3 * feats].reshape(3, heads, HD)
     qv_bias_grad = jnp.stack([bias_sums[0], bias_sums[2]], 1).reshape(-1)
     qk_scale_grad = tail[3 * feats : 3 * feats + heads]
@@ -951,7 +980,9 @@
     input_grad = (
         grad_resid + norm_back(unit_one, recip_one, grad_normed_one * (1.0 + scale_one))
     ).astype(BF16)
-    first_grad, order = share(first_mine)
+    first_hop = swap(first_mine, data_masks[-1])
+    cond_sums, first_hop = lax.optimization_barrier((cond_sums, first_hop))
+    first_grad, order = share(first_mine, first_hop)
     cond_sums = head_sum_near(cond_sums)
     _, silu_pull = jax.vjp(jax.nn.silu, cond_rows)
     grad_rows = silu_pull(cond_sums)[0]

time: 621 us -> 629 us (1.013); the launches traced: 621 us -> 622 us
  starting transfers between devices: 68.1 us -> 93.7 us
  waiting for transfers between devices: 203 us -> 181 us
    ppermute x15, waiting for transfers between devices: 113 us -> 55.8 us  [xor_head(): return lax.ppermute(value, 'head', [(i, i ^ mask) for i in range(count)])]
    ppermute x30, waiting for transfers between devices: 89.9 us -> 117 us  [rot(): return lax.ppermute(value, 'head', pairs)]
    ppermute x15 -> x14, starting transfers between devices: 15.3 us -> 37.5 us  [swap(): return lax.ppermute(value, 'dp', [(i, i ^ mask) for i in range(data_count)])]
    ppermute x15 -> x14, waiting for transfers between devices: 0.04 us -> 8.69 us  [swap(): return lax.ppermute(value, 'dp', [(i, i ^ mask) for i in range(data_count)])]
    pallas_call x1, Pallas kernels: 69 us -> 62 us  [attention_backward(): pl.pallas_call(functools.partial(backward_kernel, heads, rows_k), grid_sp...]
    unnamed x146 -> x161, local copies, waits for them, and re-layouts: 29.2 us -> 33.2 us
  transfers between devices with their start and end apart: 63 -> 62, of which waited for: 23 -> 22; matrix products, arithmetic and copies ran while one was open for 16% -> 16% of each run, Pallas kernels for 22% -> 22%
where the time goes in v4:
time: 629 us; the launch traced here: 622 us
  waiting for transfers between devices  181 us (29%)
  Pallas kernels  181 us (29%)
  starting transfers between devices  93.7 us (15%)
  other arithmetic  63 us (10%)
  local copies, waits for them, and re-layouts  60.5 us (10%)
  between operations  23.9 us (4%)
  matrix products  18 us (3%)
    ppermute x30, waiting for transfers between devices, rot(): return lax.ppermute(value, 'head', pairs)  117 us
    pallas_call x1, Pallas kernels, attention_backward(): pl.pallas_call(functools.partial(backward_kernel, heads, rows_k), grid_sp...  62 us
    ppermute x15, waiting for transfers between devices, xor_head(): return lax.ppermute(value, 'head', [(i, i ^ mask) for i in range(count)])  55.8 us
    pallas_call x1, Pallas kernels, mlp(): pl.pallas_call(functools.partial(mlp_kernel, rows), grid_spec=pltpu.Prefe...  41.2 us
    ppermute x30, starting transfers between devices, rot(): return lax.ppermute(value, 'head', pairs)  39.1 us
    ppermute x14, starting transfers between devices, swap(): return lax.ppermute(value, 'dp', [(i, i ^ mask) for i in range(data_count)])  37.5 us
    unnamed x161, local copies, waits for them, and re-layouts  33.2 us
    pallas_call x1, Pallas kernels, attention_forward(): pl.pallas_call(functools.partial(forward_kernel, heads, rows_k), grid_spe...  29.5 us
  transfers between devices with their start and end apart: 62, of which 22 were waited for; matrix products, arithmetic and copies ran while one was open for 16% of the time, Pallas kernels for 22%

profile of v4, /device:TPU:1, one launch (start us, length us, event | category | flops | bytes accessed | tf_op | source)
XLA Modules:
  0.0 621.8 jit_solution(270728220448951602)
XLA Ops:
  29.9 40.1 %collective-permute-done.5.piece_ref = bf16[512,1024]{1,0:T(8,128)(2,1)S(1)} collective-permute-done((bf16[512,1024]{1,0:T(8,128)(2,1)S(1)}, bf16[512,1024]{1,0:T(8,128)(2,1)S(1)}, u32[]{:S(2)}, u32[]{:S(2)}) %collective-permute-start.5) | collective-permute-done | bytes 1048608 | tf_op jit(solution)/shard_map/ppermute | solution.py:663
  73.4 48.2 %collective-permute-done.6.piece_ref = bf16[512,1024]{1,0:T(8,128)(2,1)} collective-permute-done((bf16[512,1024]{1,0:T(8,128)(2,1)S(1)}, bf16[512,1024]{1,0:T(8,128)(2,1)}, u32[]{:S(2)}, u32[]{:S(2)}) %collective-permute-start.6) | collective-permute-done | bytes 1048608 | tf_op jit(solution)/shard_map/ppermute | solution.py:663
  172.9 3.7 project.11
  183.8 3.6 project.14
  190.9 29.5 %attend.1 = (bf16[128,4096]{1,0:T(8,128)(2,1)S(1)}, f32[2,4096]{1,0:T(2,128)S(1)}) custom-call(s32[3]{0:T(128)S(1)} %bitcast.211, bf16[128,4096]{1,0:T(8,128)(2,1)S(1)} %get-tuple-element.198.query_ref, bf16[4096,128]{1,0:T(8,128)(2,1)S(1)} %get-tuple-element.199.key_ref, bf16[128,4096]{1,0:T(8,128)(2,1)S(1)} %get-tuple-element.200.valuet_ref), custom_call_target="tpu_custom_call" | custom-call | flops 33554432000 | bytes 4194304 | tf_op jit(solution)/shard_map/attend/pallas_call | solution.py:328
  232.4 5.3 collective-permute-done.17
  242.2 41.2 %mlp.1 = (bf16[2,8,128,1024]{3,2,1,0:T(8,128)(2,1)}, bf16[2,8,128,1024]{3,2,1,0:T(8,128)(2,1)}, bf16[2,8,128,1024]{3,2,1,0:T(8,128)(2,1)}, bf16[2,8,128,1024]{3,...) custom-call(s32[4]{0:T(128)S(1)} %broadcast_xor_fusion.part_ref, ...), custom_call_target="tpu_custom_call" | custom-call | flops 25769803776 | bytes 41943040 | tf_op jit(solution)/shard_map/mlp/pallas_call | solution.py:469
  283.5 10.9 %collective-permute-start.25 = (bf16[2,8,128,1024]{3,2,1,0:T(8,128)(2,1)}, bf16[2,8,128,1024]{3,2,1,0:T(8,128)(2,1)S(1)}, u32[]{:S(2)}, u32[]{:S(2)}) collective-permute-start(bf16[2,8,128,1024]{3,2,1,0:T(8,128)(2,1)} %get-tuple-element.216), channel_id=1, source_target_pairs={{0,8},{8,0},{16,24},{24,16},{1,9},{9,1},{17,25},{25,17},{2,10},{10... | collective-permute-start | bytes 12582920 | tf_op jit(solution)/shard_map/ppermute | solution.py:666
  299.3 4.0 fusion.22
  317.3 4.2 collective-permute-done.21
  324.9 4.2 collective-permute-start.28
  346.3 62.0 %attend_back.1 = (bf16[384,4096]{1,0:T(8,128)(2,1)}, f32[2,4096]{1,0:T(2,128)}) custom-call(s32[3]{0:T(128)} %bitcast.210, f32[2]{0:T(128)} %copy-done.26, f32[384,4096]{1,0:T(8,128)} %copy-done.3, bf16[128,4096]{1,0:T(8,128)(2,1)} %copy-done.6, bf16[4096,128]{1,0:T(8,128)(2,1)} %copy-done.9, bf16[128,4096]{1,0:T(8,128)(2,1)} %copy-done.12, ...), custom_call_target="tpu_custom_call" | custom-call | flops 67108864000 | bytes 14680064 | tf_op jit(solution)/shard_map/attend_back/pallas_call | solution.py:353
  415.6 12.3 %ring_blocks.3.blocks_ref = bf16[7,672,1024]{2,1,0:T(8,128)(2,1)} custom-call(s32[7]{0:T(128)} %stack.71.place_ref, bf16[384,4096]{1,0:T(8,128)(2,1)} %get-tuple-element.238.grad_ref, bf16[384,1024]{1,0:T(8,128)(2,1)} %bitcast.207, bf16[8,128,1024]{2,1,0:T(8,128)(2,1)} %get-tuple-element.225.one_ref, bf16[8,128,1024]{2,1,0:T(8,128)(2,1)} %collective-permute-done.29.two_ref, ...), custom_call_target="tpu_custom_call" | custom-call | flops 1 | bytes 1 | tf_op jit(solution)/shard_map/ring_blocks/pallas_call | solution.py:540
  430.9 7.6 %collective-permute-done.35.got_ref = bf16[336,1024]{1,0:T(8,128)(2,1)S(1)} collective-permute-done((bf16[336,1024]{1,0:T(8,128)(2,1)}, bf16[336,1024]{1,0:T(8,128)(2,1)S(1)}, u32[]{:S(2)}, u32[]{:S(2)}) %collective-permute-start.35) | collective-permute-done | bytes 688160 | tf_op jit(solution)/shard_map/ppermute | solution.py:663
  449.2 4.6 collective-permute-start.37
  454.1 8.0 %add_convert_fusion.8 = (bf16[384,1024]{1,0:T(8,128)(2,1)S(1)}, f32[1024]{0:T(1024)S(1)}) fusion(f32[1024]{0:T(1024)S(1)} %bitcast.253, f32[384]{0:T(512)S(1)} %convert_reduce_fusion.1, f32[1024]{0:T(1024)S(1)} %bitcast.240, bf16[3,2,64,1024]{3,2,1,0:T(8,128)(2,1)S(1)} %copy-done.5, bf16[384,4096]{1,0:T(8,128)(2,1)} %get-tuple-element.238.grad_ref, ...), kind=kOutput, calls=%fused_computation.67 | convolution fusion | flops 3223976960 | bytes 13121024 | tf_op jit(solution)/shard_map/dot_general | solution.py:42
  466.3 8.8 %collective-permute-done.38 = f32[1,2048]{1,0:T(1,128)S(1)} collective-permute-done((f32[1,2048]{1,0:T(1,128)S(1)}, f32[1,2048]{1,0:T(1,128)S(1)}, u32[]{:S(2)}, u32[]{:S(2)}) %collective-permute-start.38) | collective-permute-done | bytes 8224 | tf_op jit(solution)/shard_map/ppermute | solution.py:669
  481.6 5.5 fusion.2
  487.1 14.4 %collective-permute-start.46 = (bf16[2,128,1024]{2,1,0:T(8,128)(2,1)}, bf16[2,128,1024]{2,1,0:T(8,128)(2,1)}, u32[]{:S(2)}, u32[]{:S(2)}) collective-permute-start(bf16[2,128,1024]{2,1,0:T(8,128)(2,1)} %bitcast.226), channel_id=1, source_target_pairs={{0,16},{8,24},{16,0},{24,8},{1,17},{9,25},{17,1},{25,9},{2,18},{10... | collective-permute-start | bytes 1572872 | tf_op jit(solution)/shard_map/ppermute | solution.py:666
  504.8 8.7 %collective-permute-done.46 = bf16[2,128,1024]{2,1,0:T(8,128)(2,1)} collective-permute-done((bf16[2,128,1024]{2,1,0:T(8,128)(2,1)}, bf16[2,128,1024]{2,1,0:T(8,128)(2,1)}, u32[]{:S(2)}, u32[]{:S(2)}) %collective-permute-start.46) | collective-permute-done | bytes 524320 | tf_op jit(solution)/shard_map/ppermute | solution.py:666
  519.3 17.5 %collective-permute-done.43 = f32[1,16384]{1,0:T(1,128)S(1)} collective-permute-done((f32[1,16384]{1,0:T(1,128)S(1)}, f32[1,16384]{1,0:T(1,128)S(1)}, u32[]{:S(2)}, u32[]{:S(2)}) %collective-permute-start.43) | collective-permute-done | bytes 65568 | tf_op jit(solution)/shard_map/ppermute | solution.py:669
  542.8 5.5 fusion.1
  572.3 15.2 %collective-permute-done.53 = f32[4,1024]{1,0:T(4,128)S(1)} collective-permute-done((f32[4,1024]{1,0:T(4,128)S(1)}, f32[4,1024]{1,0:T(4,128)S(1)}, u32[]{:S(2)}, u32[]{:S(2)}) %collective-permute-start.53) | collective-permute-done | bytes 16416 | tf_op jit(solution)/shard_map/ppermute | solution.py:669
  610.3 4.5 finish_weights.1
  (448 shorter events, 228.5 us)
Async XLA Ops:
  7.2 141.9 %all-gather.6.cloned.1.call-start = ((), (), s32[]{:S(2)}) async-start(), calls=%async_computation.3 | async-start | bytes 10813440 | tf_op jit(solution)/shard_map/all_gather | solution.py:687
  10.2 231.9 %all-gather.4.cloned.1.call-start = ((), (), s32[]{:S(2)}) async-start(), calls=%async_computation.1 | async-start | bytes 8650752 | tf_op jit(solution)/shard_map/all_gather | solution.py:690
  12.0 475.1 %reduce-scatter.2.cloned.1.call-start = ((), (), s32[]{:S(2)}) async-start(), calls=%async_computation.2 | async-start | bytes 4718592 | tf_op jit(solution)/shard_map/reduce_scatter | solution.py:820
  27.4 42.6 %collective-permute-start.5 = (bf16[512,1024]{1,0:T(8,128)(2,1)S(1)}, bf16[512,1024]{1,0:T(8,128)(2,1)S(1)}, u32[]{:S(2)}, u32[]{:S(2)}) collective-permute-start(bf16[512,1024]{1,0:T(8,128)(2,1)S(1)} %fusion.14.piece_ref), channel_id=1, source_target_pairs={{2,0},{4,2},{6,4},{7,6},{5,7},{3,5},{1,3},{0,1},{10,8},{12,10},{14... | collective-permute-start | bytes 3145736 | tf_op jit(solution)/shard_map/ppermute | solution.py:663
  28.7 42.2 %collective-permute-start.4 = (bf16[512,1024]{1,0:T(8,128)(2,1)S(1)}, bf16[512,1024]{1,0:T(8,128)(2,1)S(1)}, u32[]{:S(2)}, u32[]{:S(2)}) collective-permute-start(bf16[512,1024]{1,0:T(8,128)(2,1)S(1)} %fusion.14.piece_ref), channel_id=1, source_target_pairs={{1,0},{0,2},{2,4},{4,6},{6,7},{7,5},{5,3},{3,1},{9,8},{8,10},{10,1... | collective-permute-start | bytes 3145736 | tf_op jit(solution)/shard_map/ppermute | solution.py:663
  69.9 51.6 %collective-permute-start.6 = (bf16[512,1024]{1,0:T(8,128)(2,1)S(1)}, bf16[512,1024]{1,0:T(8,128)(2,1)}, u32[]{:S(2)}, u32[]{:S(2)}) collective-permute-start(bf16[512,1024]{1,0:T(8,128)(2,1)S(1)} %collective-permute-done.5.piece_ref), channel_id=1, source_target_pairs={{2,0},{4,2},{6,4},{7,6},{5,7},{3,5},{1,3},{0,1},{10,8},{12,10},{14... | collective-permute-start | bytes 3145736 | tf_op jit(solution)/shard_map/ppermute | solution.py:663
  70.9 50.6 %collective-permute-start.8 = (bf16[512,1024]{1,0:T(8,128)(2,1)S(1)}, bf16[512,1024]{1,0:T(8,128)(2,1)}, u32[]{:S(2)}, u32[]{:S(2)}) collective-permute-start(bf16[512,1024]{1,0:T(8,128)(2,1)S(1)} %collective-permute-done.4.piece_ref), channel_id=1, source_target_pairs={{1,0},{0,2},{2,4},{4,6},{6,7},{7,5},{5,3},{3,1},{9,8},{8,10},{10,1... | collective-permute-start | bytes 3145736 | tf_op jit(solution)/shard_map/ppermute | solution.py:663
  146.9 40.6 %collective-permute-start.11 = (bf16[256,1024]{1,0:T(8,128)(2,1)}, bf16[256,1024]{1,0:T(8,128)(2,1)}, u32[]{:S(2)}, u32[]{:S(2)}) collective-permute-start(bf16[256,1024]{1,0:T(8,128)(2,1)} %slice.235), channel_id=1, source_target_pairs={{1,0},{0,2},{2,4},{4,6},{6,7},{7,5},{5,3},{3,1},{9,8},{8,10},{10,1... | collective-permute-start | bytes 1572872 | tf_op jit(solution)/shard_map/ppermute | solution.py:663
  154.3 33.2 %collective-permute-start.10 = (bf16[256,1024]{1,0:T(8,128)(2,1)}, bf16[256,1024]{1,0:T(8,128)(2,1)}, u32[]{:S(2)}, u32[]{:S(2)}) collective-permute-start(bf16[256,1024]{1,0:T(8,128)(2,1)} %slice.234), channel_id=1, source_target_pairs={{2,0},{4,2},{6,4},{7,6},{5,7},{3,5},{1,3},{0,1},{10,8},{12,10},{14... | collective-permute-start | bytes 1572872 | tf_op jit(solution)/shard_map/ppermute | solution.py:663
  283.5 47.1 %collective-permute-start.25 = (bf16[2,8,128,1024]{3,2,1,0:T(8,128)(2,1)}, bf16[2,8,128,1024]{3,2,1,0:T(8,128)(2,1)S(1)}, u32[]{:S(2)}, u32[]{:S(2)}) collective-permute-start(bf16[2,8,128,1024]{3,2,1,0:T(8,128)(2,1)} %get-tuple-element.216), channel_id=1, source_target_pairs={{0,8},{8,0},{16,24},{24,16},{1,9},{9,1},{17,25},{25,17},{2,10},{10... | collective-permute-start | bytes 12582920 | tf_op jit(solution)/shard_map/ppermute | solution.py:666
  296.6 36.1 %collective-permute-start.23 = (bf16[2,8,128,1024]{3,2,1,0:T(8,128)(2,1)}, bf16[2,8,128,1024]{3,2,1,0:T(8,128)(2,1)S(1)}, u32[]{:S(2)}, u32[]{:S(2)}) collective-permute-start(bf16[2,8,128,1024]{3,2,1,0:T(8,128)(2,1)} %get-tuple-element.214), channel_id=1, source_target_pairs={{0,8},{8,0},{16,24},{24,16},{1,9},{9,1},{17,25},{25,17},{2,10},{10... | collective-permute-start | bytes 12582920 | tf_op jit(solution)/shard_map/ppermute | solution.py:666
  339.0 69.3 %collective-permute-start.31 = (f32[1,14336]{1,0:T(1,128)S(1)}, f32[1,14336]{1,0:T(1,128)S(1)}, u32[]{:S(2)}, u32[]{:S(2)}) collective-permute-start(f32[1,14336]{1,0:T(1,128)S(1)} %bitcast.232), channel_id=1, source_target_pairs={{0,2},{1,3},{2,0},{3,1},{4,6},{5,7},{6,4},{7,5},{8,10},{9,11},{10,... | collective-permute-start | bytes 172040 | tf_op jit(solution)/shard_map/ppermute | solution.py:669
  339.9 68.4 %collective-permute-start.32 = (f32[1,14336]{1,0:T(1,128)S(1)}, f32[1,14336]{1,0:T(1,128)S(1)}, u32[]{:S(2)}, u32[]{:S(2)}) collective-permute-start(f32[1,14336]{1,0:T(1,128)S(1)} %bitcast.233), channel_id=1, source_target_pairs={{0,4},{1,5},{2,6},{3,7},{4,0},{5,1},{6,2},{7,3},{8,12},{9,13},{10,... | collective-permute-start | bytes 172040 | tf_op jit(solution)/shard_map/ppermute | solution.py:669
  342.6 65.7 %collective-permute-start.33 = (f32[1,14336]{1,0:T(1,128)S(1)}, f32[1,14336]{1,0:T(1,128)S(1)}, u32[]{:S(2)}, u32[]{:S(2)}) collective-permute-start(f32[1,14336]{1,0:T(1,128)S(1)} %bitcast.234), channel_id=1, source_target_pairs={{0,6},{1,7},{2,4},{3,5},{4,2},{5,3},{6,0},{7,1},{8,14},{9,15},{10,... | collective-permute-start | bytes 172040 | tf_op jit(solution)/shard_map/ppermute | solution.py:669
  342.6 65.8 %collective-permute-start.29 = (bf16[8,128,1024]{2,1,0:T(8,128)(2,1)}, bf16[8,128,1024]{2,1,0:T(8,128)(2,1)}, u32[]{:S(2)}, u32[]{:S(2)}) collective-permute-start(bf16[8,128,1024]{2,1,0:T(8,128)(2,1)} %get-tuple-element.221), channel_id=1, source_target_pairs={{0,16},{8,24},{16,0},{24,8},{1,17},{9,25},{17,1},{25,9},{2,18},{10... | collective-permute-start | bytes 6291464 | tf_op jit(solution)/shard_map/ppermute | solution.py:666
  346.3 62.2 %collective-permute-start.30 = (bf16[8,32,1024]{2,1,0:T(8,128)(2,1)}, bf16[8,32,1024]{2,1,0:T(8,128)(2,1)S(1)}, u32[]{:S(2)}, u32[]{:S(2)}) collective-permute-start(bf16[8,32,1024]{2,1,0:T(8,128)(2,1)} %get-tuple-element.222), channel_id=1, source_target_pairs={{0,16},{8,24},{16,0},{24,8},{1,17},{9,25},{17,1},{25,9},{2,18},{10... | collective-permute-start | bytes 1572872 | tf_op jit(solution)/shard_map/ppermute | solution.py:666
  447.6 34.0 %collective-permute-start.36 = (bf16[672,1024]{1,0:T(8,128)(2,1)}, bf16[672,1024]{1,0:T(8,128)(2,1)}, u32[]{:S(2)}, u32[]{:S(2)}) collective-permute-start(bf16[672,1024]{1,0:T(8,128)(2,1)} %add_half.2), channel_id=1, source_target_pairs={{1,0},{0,2},{2,4},{4,6},{6,7},{7,5},{5,3},{3,1},{9,8},{8,10},{10,1... | collective-permute-start | bytes 4128776 | tf_op jit(solution)/shard_map/ppermute | solution.py:663
  449.2 32.4 %collective-permute-start.37 = (bf16[672,1024]{1,0:T(8,128)(2,1)}, bf16[672,1024]{1,0:T(8,128)(2,1)}, u32[]{:S(2)}, u32[]{:S(2)}) collective-permute-start(bf16[672,1024]{1,0:T(8,128)(2,1)} %add_half.3), channel_id=1, source_target_pairs={{2,0},{4,2},{6,4},{7,6},{5,7},{3,5},{1,3},{0,1},{10,8},{12,10},{14... | collective-permute-start | bytes 4128776 | tf_op jit(solution)/shard_map/ppermute | solution.py:663
  503.3 39.5 %collective-permute-start.41 = (bf16[672,1024]{1,0:T(8,128)(2,1)}, bf16[672,1024]{1,0:T(8,128)(2,1)}, u32[]{:S(2)}, u32[]{:S(2)}) collective-permute-start(bf16[672,1024]{1,0:T(8,128)(2,1)} %get-tuple-element.246), channel_id=1, source_target_pairs={{1,0},{0,2},{2,4},{4,6},{6,7},{7,5},{5,3},{3,1},{9,8},{8,10},{10,1... | collective-permute-start | bytes 4128776 | tf_op jit(solution)/shard_map/ppermute | solution.py:663
  503.7 39.1 %collective-permute-start.42 = (bf16[672,1024]{1,0:T(8,128)(2,1)}, bf16[672,1024]{1,0:T(8,128)(2,1)}, u32[]{:S(2)}, u32[]{:S(2)}) collective-permute-start(bf16[672,1024]{1,0:T(8,128)(2,1)} %get-tuple-element.247), channel_id=1, source_target_pairs={{2,0},{4,2},{6,4},{7,6},{5,7},{3,5},{1,3},{0,1},{10,8},{12,10},{14... | collective-permute-start | bytes 4128776 | tf_op jit(solution)/shard_map/ppermute | solution.py:663
  554.9 34.2 %collective-permute-start.48 = (bf16[672,1024]{1,0:T(8,128)(2,1)}, bf16[672,1024]{1,0:T(8,128)(2,1)}, u32[]{:S(2)}, u32[]{:S(2)}) collective-permute-start(bf16[672,1024]{1,0:T(8,128)(2,1)} %get-tuple-element.256), channel_id=1, source_target_pairs={{1,0},{0,2},{2,4},{4,6},{6,7},{7,5},{5,3},{3,1},{9,8},{8,10},{10,1... | collective-permute-start | bytes 4128776 | tf_op jit(solution)/shard_map/ppermute | solution.py:663
  554.9 34.2 %collective-permute-start.49 = (bf16[672,1024]{1,0:T(8,128)(2,1)}, bf16[672,1024]{1,0:T(8,128)(2,1)}, u32[]{:S(2)}, u32[]{:S(2)}) collective-permute-start(bf16[672,1024]{1,0:T(8,128)(2,1)} %get-tuple-element.257), channel_id=1, source_target_pairs={{2,0},{4,2},{6,4},{7,6},{5,7},{3,5},{1,3},{0,1},{10,8},{12,10},{14... | collective-permute-start | bytes 4128776 | tf_op jit(solution)/shard_map/ppermute | solution.py:663
  559.0 28.4 %collective-permute-start.53 = (f32[4,1024]{1,0:T(4,128)S(1)}, f32[4,1024]{1,0:T(4,128)S(1)}, u32[]{:S(2)}, u32[]{:S(2)}) collective-permute-start(f32[4,1024]{1,0:T(4,128)S(1)} %fusion.44), channel_id=1, source_target_pairs={{0,2},{1,3},{2,0},{3,1},{4,6},{5,7},{6,4},{7,5},{8,10},{9,11},{10,... | collective-permute-start | bytes 49160 | tf_op jit(solution)/shard_map/ppermute | solution.py:669
  559.0 28.5 %collective-permute-start.54 = (f32[4,1024]{1,0:T(4,128)S(1)}, f32[4,1024]{1,0:T(4,128)S(1)}, u32[]{:S(2)}, u32[]{:S(2)}) collective-permute-start(f32[4,1024]{1,0:T(4,128)S(1)} %fusion.44), channel_id=1, source_target_pairs={{0,4},{1,5},{2,6},{3,7},{4,0},{5,1},{6,2},{7,3},{8,12},{9,13},{10,... | collective-permute-start | bytes 49160 | tf_op jit(solution)/shard_map/ppermute | solution.py:669
  (113 other events, 2010.3 us)
Sparse Core Ops, SparseCore 0:
  11.5 113.0 all-gather.5
  128.2 87.8 all-gather.3
  346.4 98.7 reduce-scatter.1
